TPU v7x, 32 devices: a whole 2x2x4 slice. The times are simulated.
32 devices in a mesh: gx: 2 (over x), gy: 4 (over z), gz: 4 (over y, core).
Axes of the slice: x: 2, y: 2, z: 4, core: 2. Of those that a mesh axis runs over, the one named last changes fastest.
Arguments:
- pressure_start: float32 [32, 256, 1024], P('gx', 'gy', 'gz'), may hold values from -6 to 6
- source: float32 [32, 256, 1024], P('gx', 'gy', 'gz'), may hold values from -16 to 16
- permeability: float32 [32, 256, 1024], P('gx', 'gy', 'gz'), may hold values from 0.1 to 10
Outputs:
- pressure: float32 [32, 256, 1024], P('gx', 'gy', 'gz')
All inputs are finite; a program needn't handle non-finite values.
Results may differ from a plain program's by a relative error of at most 0.0003.
Values sent between devices are 32-bit elements; how exact they have to be, the bound alone decides.
No kernel may reach another device: no remote copies, remote signals or barrier semaphores. Data moves between devices by JAX's collectives and lax.ppermute only.
A program may use at most 128 MiB of HBM per device.

v0:
```python
import jax
import jax.numpy as jnp
from jax import lax
from jax.sharding import PartitionSpec as P

RATIO = 8
SWEEPS = 4
COARSE_SWEEPS = 8


OMEGA = 0.8
OMEGA_COARSE = 0.8


def padded_2(block, sides, width):
    for axis, dim in sides:
        count = lax.axis_size(axis)
        forward = [(i, i + 1) for i in range(count - 1)]
        backward = [(target, source) for source, target in forward]
        low = lax.ppermute(
            lax.slice_in_dim(block, block.shape[dim] - width, None, axis=dim), axis, forward
        )
        high = lax.ppermute(lax.slice_in_dim(block, 0, width, axis=dim), axis, backward)
        block = jnp.concatenate([low, block, high], axis=dim)
    return block


def neighbours(padded):
    return (
        padded[:-2, 1:-1, 1:-1],
        padded[2:, 1:-1, 1:-1],
        padded[1:-1, :-2, 1:-1],
        padded[1:-1, 2:, 1:-1],
        padded[1:-1, 1:-1, :-2],
        padded[1:-1, 1:-1, 2:],
    )


def face_weights(padded):
    center = padded[1:-1, 1:-1, 1:-1]
    weights = tuple(
        (
            jnp.where(beside_cell > 0.0, 0.5 * (center + beside_cell), center)
            for beside_cell in neighbours(padded)
        )
    )
    diagonal_sum = weights[0] + weights[1] + weights[2] + weights[3] + weights[4] + weights[5]
    return (weights, diagonal_sum)


def apply_operator(padded, weights, diagonal_sum):
    beside = neighbours(padded)
    flux = weights[0] * beside[0] + weights[1] * beside[1] + weights[2] * beside[2]
    flux = flux + weights[3] * beside[3] + weights[4] * beside[4] + weights[5] * beside[5]
    return diagonal_sum * padded[1:-1, 1:-1, 1:-1] - flux


def block_sum(values):
    depth, rows, width = values.shape
    return values.reshape(depth // RATIO, RATIO, rows // RATIO, RATIO, width // RATIO, RATIO).sum(
        axis=(1, 3, 5)
    )


def coarse_faces(weights):
    depth, rows, width = weights[0].shape
    cells_z, cells_y, cells_x = (depth // RATIO, rows // RATIO, width // RATIO)
    low_z = weights[0][0::RATIO].reshape(cells_z, cells_y, RATIO, cells_x, RATIO).sum(axis=(2, 4))
    high_z = (
        weights[1][RATIO - 1 :: RATIO]
        .reshape(cells_z, cells_y, RATIO, cells_x, RATIO)
        .sum(axis=(2, 4))
    )
    low_y = (
        weights[2][:, 0::RATIO, :].reshape(cells_z, RATIO, cells_y, cells_x, RATIO).sum(axis=(1, 4))
    )
    high_y = (
        weights[3][:, RATIO - 1 :: RATIO, :]
        .reshape(cells_z, RATIO, cells_y, cells_x, RATIO)
        .sum(axis=(1, 4))
    )
    low_x = (
        weights[4][:, :, 0::RATIO].reshape(cells_z, RATIO, cells_y, RATIO, cells_x).sum(axis=(1, 3))
    )
    high_x = (
        weights[5][:, :, RATIO - 1 :: RATIO]
        .reshape(cells_z, RATIO, cells_y, RATIO, cells_x)
        .sum(axis=(1, 3))
    )
    return (low_z, high_z, low_y, high_y, low_x, high_x)


def fine_rims(values):
    return padded_2(values, (("gx", 0), ("gy", 1), ("gz", 2)), 1)


def zero_rims(values):
    return jnp.pad(values, 1)


def coarse_sweeps(coarse_rhs, faces, diagonal_sum, extend):
    correction = OMEGA_COARSE * coarse_rhs / diagonal_sum
    for sweep_index in range(COARSE_SWEEPS - 1):
        applied = apply_operator(extend(correction), faces, diagonal_sum)
        correction = correction + OMEGA_COARSE * (coarse_rhs - applied) / diagonal_sum
    applied = apply_operator(extend(correction), faces, diagonal_sum)
    return (correction, jnp.sum(coarse_rhs - applied), jnp.sum(diagonal_sum))


def shifted_down(values, axis_number):
    upper = lax.slice_in_dim(values, 1, values.shape[axis_number], 1, axis_number)
    empty = jnp.zeros_like(lax.slice_in_dim(values, 0, 1, 1, axis_number))
    return jnp.concatenate((upper, empty), axis=axis_number)


def shards(pressure_start, source, permeability):
    perm_padded = padded_2(permeability, (("gx", 0), ("gy", 1), ("gz", 2)), 1)
    own_weights, diagonal_sum = face_weights(perm_padded)
    applied = apply_operator(fine_rims(pressure_start), own_weights, diagonal_sum)
    start_residual = source - applied
    pressure_now = pressure_start + OMEGA * start_residual / diagonal_sum
    for sweep_index in range(SWEEPS - 1):
        applied = apply_operator(fine_rims(pressure_now), own_weights, diagonal_sum)
        pressure_now = pressure_now + OMEGA * (source - applied) / diagonal_sum
    coarse_rhs = block_sum(start_residual)
    faces = coarse_faces(own_weights)
    coarse_diagonal = faces[0] + faces[1] + faces[2] + faces[3] + faces[4] + faces[5]
    cells_z, cells_y, cells_x = coarse_rhs.shape
    packed = jnp.stack((coarse_rhs, coarse_diagonal, faces[0], faces[2], faces[4])).reshape(1, -1)
    everything = lax.all_gather(packed, ("gx", "gy", "gz"), axis=0, tiled=True)
    count_z, count_y, count_x = (lax.axis_size("gx"), lax.axis_size("gy"), lax.axis_size("gz"))
    coarse_grid = everything.reshape(count_z, count_y, count_x, 5, cells_z, cells_y, cells_x)
    coarse_grid = coarse_grid.transpose(3, 0, 4, 1, 5, 2, 6).reshape(
        5, count_z * cells_z, count_y * cells_y, count_x * cells_x
    )
    rhs_all, diagonal_all = (coarse_grid[0], coarse_grid[1])
    low_z, low_y, low_x = (coarse_grid[2], coarse_grid[3], coarse_grid[4])
    faces_all = (
        low_z,
        shifted_down(low_z, 0),
        low_y,
        shifted_down(low_y, 1),
        low_x,
        shifted_down(low_x, 2),
    )
    correction_all, leftover, diag_total = coarse_sweeps(
        rhs_all, faces_all, diagonal_all, zero_rims
    )
    start_z = lax.axis_index("gx") * cells_z
    start_y = lax.axis_index("gy") * cells_y
    start_x = lax.axis_index("gz") * cells_x
    correction = lax.dynamic_slice(
        correction_all, (start_z, start_y, start_x), (cells_z, cells_y, cells_x)
    )
    correction = correction + leftover / diag_total
    depth_all, rows_all, width_all = pressure_now.shape
    blocks = pressure_now.reshape(cells_z, RATIO, cells_y, RATIO, cells_x, RATIO)
    return (blocks + correction[:, None, :, None, :, None]).reshape(depth_all, rows_all, width_all)


def solution(mesh):
    return jax.shard_map(
        shards,
        mesh=mesh,
        in_specs=(P("gx", "gy", "gz"), P("gx", "gy", "gz"), P("gx", "gy", "gz")),
        out_specs=P("gx", "gy", "gz"),
        check_vma=False,
    )
```

profile of v0, /device:TPU:1, one launch (start us, length us, event | category | flops | bytes accessed | tf_op | source)
XLA Modules:
  0.0 299.8 jit_solution(3654660858962873308)
XLA Ops:
  0.9 3.9 %collective-permute-start.6 = (f32[1,64,256]{2,1,0:T(8,128)S(1)}, f32[1,64,256]{2,1,0:T(8,128)S(1)}, u32[]{:S(2)}, u32[]{:S(2)}) collective-permute-start(f32[1,64,256]{2,1,0:T(8,128)S(1)} %get-tuple-element.48), channel_id=1, source_target_pairs={{0,16},{1,17},{2,18},{3,19},{4,20},{5,21},{6,22},{7,23},{8,24},{9,... | collective-permute-start | bytes 196616 | tf_op jit(solution)/shard_map/ppermute | solution.py:20
  7.0 4.1 %collective-permute-start = (f32[1,64,256]{2,1,0:T(8,128)S(1)}, f32[1,64,256]{2,1,0:T(8,128)S(1)}, u32[]{:S(2)}, u32[]{:S(2)}) collective-permute-start(f32[1,64,256]{2,1,0:T(8,128)S(1)} %get-tuple-element.46), channel_id=1, source_target_pairs={{0,16},{1,17},{2,18},{3,19},{4,20},{5,21},{6,22},{7,23},{8,24},{9,... | collective-permute-start | bytes 196616 | tf_op jit(solution)/shard_map/ppermute | solution.py:20
  15.2 4.0 %collective-permute-start.8 = (f32[18,1,256]{2,1,0:T(1,128)S(1)}, f32[18,1,256]{2,1,0:T(1,128)S(1)}, u32[]{:S(2)}, u32[]{:S(2)}) collective-permute-start(f32[18,1,256]{2,1,0:T(1,128)S(1)} %get-tuple-element.37), channel_id=1, source_target_pairs={{0,4},{4,8},{8,12},{1,5},{5,9},{9,13},{2,6},{6,10},{10,14},{3,7},{... | collective-permute-start | bytes 55304 | tf_op jit(solution)/shard_map/ppermute | solution.py:20
  27.7 4.3 %collective-permute-start.11 = (f32[18,66,1]{1,2,0:T(1,128)S(1)}, f32[18,66,1]{1,2,0:T(1,128)S(1)}, u32[]{:S(2)}, u32[]{:S(2)}) collective-permute-start(f32[18,66,1]{1,2,0:T(1,128)S(1)} %copy.15), channel_id=1, source_target_pairs={{1,0},{2,1},{3,2},{5,4},{6,5},{7,6},{9,8},{10,9},{11,10},{13,12},{... | collective-permute-start | bytes 14264 | tf_op jit(solution)/shard_map/ppermute | solution.py:23
  47.0 13.2 %divide_add_fusion = (f32[16,64,256]{2,1,0:T(8,128)S(1)}, f32[16,64,256]{2,1,0:T(8,128)}, f32[16,64,256]{2,1,0:T(8,128)}, f32[16,64,256]{2,1,0:T(8,128)}, f32[16...) fusion(f32[16,64,256]{2,1,0:T(8,128)} %param.3, ...), kind=kLoop, calls=%fused_computation.149 | loop fusion | flops 17301504 | bytes 14248512 | tf_op jit(solution)/shard_map/add | solution.py:121
  60.3 12.2 %reshape.81 = f32[2,8,8,8,32,8]{5,4,3,2,1,0:T(8,128)} reshape(f32[16,64,256]{2,1,0:T(8,128)} %get-tuple-element.6) | data formatting | bytes 2097152 | tf_op jit(solution)/shard_map/reshape | solution.py:60
  72.5 7.2 %reduce_sum.93 = f32[2,8,32]{2,1,0:T(8,128)S(1)} reduce(f32[2,8,8,8,32,8]{5,4,3,2,1,0:T(8,128)} %reshape.81, f32[]{:T(128)} %constant.13.clone.1), dimensions={1,3,5}, to_apply=%region_0.1 | reduce | flops 261632 | bytes 1050628 | tf_op jit(solution)/shard_map/reduce_sum | solution.py:60
  79.7 5.4 %slice.474 = f32[16,64,32]{2,1,0:T(8,128)} slice(f32[16,64,256]{2,1,0:T(8,128)S(1)} %get-tuple-element.12), slice={[0:16:1], [0:64:1], [7:256:8]} | slice | bytes 262144 | tf_op jit(solution)/shard_map/slice | solution.py:86
  86.2 5.2 %slice.473 = f32[16,64,32]{2,1,0:T(8,128)} slice(f32[16,64,256]{2,1,0:T(8,128)S(1)} %get-tuple-element.11), slice={[0:16:1], [0:64:1], [0:256:8]} | slice | bytes 262144 | tf_op jit(solution)/shard_map/slice | solution.py:83
  114.4 44.0 %all-gather = f32[32,1,2560]{2,1,0:T(1,128)S(1)} all-gather(f32[1,1,2560]{2,1,0:T(1,128)S(1)} %reshape.90), channel_id=1, replica_groups=mesh['gx'=2,'gy'=4,'gz'=4] {'gx','gy','gz'}, dimensions={0}, use_global_device_ids=true | all-gather | bytes 337920 | tf_op jit(solution)/shard_map/all_gather | solution.py:130
  177.3 4.0 %collective-permute-start.12 = (f32[1,64,256]{2,1,0:T(8,128)S(1)}, f32[1,64,256]{2,1,0:T(8,128)S(1)}, u32[]{:S(2)}, u32[]{:S(2)}) collective-permute-start(f32[1,64,256]{2,1,0:T(8,128)S(1)} %get-tuple-element.43), channel_id=1, source_target_pairs={{0,16},{1,17},{2,18},{3,19},{4,20},{5,21},{6,22},{7,23},{8,24},{9,... | collective-permute-start | bytes 196616 | tf_op jit(solution)/shard_map/ppermute | solution.py:20
  184.0 4.0 %collective-permute-start.14 = (f32[18,1,256]{2,1,0:T(1,128)S(1)}, f32[18,1,256]{2,1,0:T(1,128)S(1)}, u32[]{:S(2)}, u32[]{:S(2)}) collective-permute-start(f32[18,1,256]{2,1,0:T(1,128)S(1)} %get-tuple-element.33), channel_id=1, source_target_pairs={{0,4},{4,8},{8,12},{1,5},{5,9},{9,13},{2,6},{6,10},{10,14},{3,7},{... | collective-permute-start | bytes 55304 | tf_op jit(solution)/shard_map/ppermute | solution.py:20
  191.5 4.4 %collective-permute-start.17 = (f32[18,66,1]{1,2,0:T(1,128)S(1)}, f32[18,66,1]{1,2,0:T(1,128)S(1)}, u32[]{:S(2)}, u32[]{:S(2)}) collective-permute-start(f32[18,66,1]{1,2,0:T(1,128)S(1)} %copy.19), channel_id=1, source_target_pairs={{1,0},{2,1},{3,2},{5,4},{6,5},{7,6},{9,8},{10,9},{11,10},{13,12},{... | collective-permute-start | bytes 14264 | tf_op jit(solution)/shard_map/ppermute | solution.py:23
  201.1 7.2 %fusion.39 = f32[16,64,256]{2,1,0:T(8,128)S(1)} fusion(f32[16,64,256]{2,1,0:T(8,128)} %copy-done.2, f32[16,64,256]{2,1,0:T(8,128)} %param.4, f32[16,64,256]{2,1,0:T(8,128)S(1)} %get-tuple-element.12, f32[18,66,1]{2,1,0:T(8,128)} %copy.20, f32[18,1,256]{2,1,0:T(1,128)} %copy-done.34, f32[18,1,256]{2,1,0:T(1,128)} %copy-done.36, f32[1,64,256]{2,1,0:T(8,128)} %copy-done.18, ...), kind=kLoop, calls=%fused_computation.81 | loop fusion | flops 10485760 | bytes 9614624 | tf_op jit(solution)/shard_map/add | solution.py:124
  209.7 4.0 %collective-permute-start.18 = (f32[1,64,256]{2,1,0:T(8,128)S(1)}, f32[1,64,256]{2,1,0:T(8,128)S(1)}, u32[]{:S(2)}, u32[]{:S(2)}) collective-permute-start(f32[1,64,256]{2,1,0:T(8,128)S(1)} %get-tuple-element.41), channel_id=1, source_target_pairs={{0,16},{1,17},{2,18},{3,19},{4,20},{5,21},{6,22},{7,23},{8,24},{9,... | collective-permute-start | bytes 196616 | tf_op jit(solution)/shard_map/ppermute | solution.py:20
  216.3 4.6 %collective-permute-start.20 = (f32[18,1,256]{2,1,0:T(1,128)S(1)}, f32[18,1,256]{2,1,0:T(1,128)S(1)}, u32[]{:S(2)}, u32[]{:S(2)}) collective-permute-start(f32[18,1,256]{2,1,0:T(1,128)S(1)} %get-tuple-element.31), channel_id=1, source_target_pairs={{0,4},{4,8},{8,12},{1,5},{5,9},{9,13},{2,6},{6,10},{10,14},{3,7},{... | collective-permute-start | bytes 55304 | tf_op jit(solution)/shard_map/ppermute | solution.py:20
  224.6 4.4 %collective-permute-start.23 = (f32[18,66,1]{1,2,0:T(1,128)S(1)}, f32[18,66,1]{1,2,0:T(1,128)}, u32[]{:S(2)}, u32[]{:S(2)}) collective-permute-start(f32[18,66,1]{1,2,0:T(1,128)S(1)} %copy.23), channel_id=1, source_target_pairs={{1,0},{2,1},{3,2},{5,4},{6,5},{7,6},{9,8},{10,9},{11,10},{13,12},{... | collective-permute-start | bytes 14264 | tf_op jit(solution)/shard_map/ppermute | solution.py:23
  239.3 4.8 %fusion.23 = f32[16,64,256]{2,1,0:T(8,128)S(1)} fusion(f32[16,64,256]{2,1,0:T(8,128)S(1)} %fusion.39, f32[16,64,256]{2,1,0:T(8,128)} %param.4, f32[16,64,256]{2,1,0:T(8,128)S(1)} %get-tuple-element.12, f32[18,66,1]{2,1,0:T(8,128)} %copy.24, f32[18,1,256]{2,1,0:T(1,128)} %copy-done.35, f32[18,1,256]{2,1,0:T(1,128)} %copy-done.37, ...), kind=kLoop, calls=%fused_computation.47 | loop fusion | flops 10485760 | bytes 9614624 | tf_op jit(solution)/shard_map/add | solution.py:124
  245.4 4.0 %collective-permute-start.24 = (f32[1,64,256]{2,1,0:T(8,128)S(1)}, f32[1,64,256]{2,1,0:T(8,128)S(1)}, u32[]{:S(2)}, u32[]{:S(2)}) collective-permute-start(f32[1,64,256]{2,1,0:T(8,128)S(1)} %get-tuple-element.39), channel_id=1, source_target_pairs={{0,16},{1,17},{2,18},{3,19},{4,20},{5,21},{6,22},{7,23},{8,24},{9,... | collective-permute-start | bytes 196616 | tf_op jit(solution)/shard_map/ppermute | solution.py:20
  252.1 4.6 %collective-permute-start.26 = (f32[18,1,256]{2,1,0:T(1,128)S(1)}, f32[18,1,256]{2,1,0:T(1,128)S(1)}, u32[]{:S(2)}, u32[]{:S(2)}) collective-permute-start(f32[18,1,256]{2,1,0:T(1,128)S(1)} %get-tuple-element.29), channel_id=1, source_target_pairs={{0,4},{4,8},{8,12},{1,5},{5,9},{9,13},{2,6},{6,10},{10,14},{3,7},{... | collective-permute-start | bytes 55304 | tf_op jit(solution)/shard_map/ppermute | solution.py:20
  261.8 3.8 %collective-permute-start.29 = (f32[18,66,1]{1,2,0:T(1,128)S(1)}, f32[18,66,1]{1,2,0:T(1,128)S(1)}, u32[]{:S(2)}, u32[]{:S(2)}) collective-permute-start(f32[18,66,1]{1,2,0:T(1,128)S(1)} %copy.27), channel_id=1, source_target_pairs={{1,0},{2,1},{3,2},{5,4},{6,5},{7,6},{9,8},{10,9},{11,10},{13,12},{... | collective-permute-start | bytes 14264 | tf_op jit(solution)/shard_map/ppermute | solution.py:23
  269.4 8.0 %add.436 = f32[2,8,8,8,32,8]{5,4,3,2,1,0:T(8,128)} broadcast(f32[2,8,32]{2,1,0:T(8,128)S(1)} %dynamic-slice_add_fusion), dimensions={0,2,4} | broadcast | bytes 1050624 | tf_op jit(solution)/shard_map/add | solution.py:158
  277.5 13.5 %add.437 = f32[16,64,256]{2,1,0:T(8,128)} reshape(f32[2,8,8,8,32,8]{5,4,3,2,1,0:T(8,128)} %add.436) | data formatting | bytes 2097152 | tf_op jit(solution)/shard_map/add | solution.py:158
  293.4 6.4 %fusion.7 = f32[16,64,256]{2,1,0:T(8,128)} fusion(f32[16,64,256]{2,1,0:T(8,128)} %add.437, f32[16,64,256]{2,1,0:T(8,128)S(1)} %copy-done.1, f32[16,64,256]{2,1,0:T(8,128)} %param.4, f32[16,64,256]{2,1,0:T(8,128)S(1)} %get-tuple-element.12, f32[18,66,1]{2,1,0:T(8,128)} %copy.28, f32[18,1,256]{2,1,0:T(1,128)S(1)} %copy-done.39, ...), kind=kLoop, calls=%fused_computation.13 | loop fusion | flops 10747904 | bytes 10663200 | tf_op jit(solution)/shard_map/add | solution.py:158
  (223 shorter events, 116.4 us)
Async XLA Ops:
  0.9 11.6 %collective-permute-start.6 = (f32[1,64,256]{2,1,0:T(8,128)S(1)}, f32[1,64,256]{2,1,0:T(8,128)S(1)}, u32[]{:S(2)}, u32[]{:S(2)}) collective-permute-start(f32[1,64,256]{2,1,0:T(8,128)S(1)} %get-tuple-element.48), channel_id=1, source_target_pairs={{0,16},{1,17},{2,18},{3,19},{4,20},{5,21},{6,22},{7,23},{8,24},{9,... | collective-permute-start | bytes 196616 | tf_op jit(solution)/shard_map/ppermute | solution.py:20
  4.8 9.0 %collective-permute-start.7 = (f32[1,64,256]{2,1,0:T(8,128)S(1)}, f32[1,64,256]{2,1,0:T(8,128)S(1)}, u32[]{:S(2)}, u32[]{:S(2)}) collective-permute-start(f32[1,64,256]{2,1,0:T(8,128)S(1)} %get-tuple-element.47), channel_id=1, source_target_pairs={{16,0},{17,1},{18,2},{19,3},{20,4},{21,5},{22,6},{23,7},{24,8},{25... | collective-permute-start | bytes 196616 | tf_op jit(solution)/shard_map/ppermute | solution.py:23
  7.0 12.2 %collective-permute-start = (f32[1,64,256]{2,1,0:T(8,128)S(1)}, f32[1,64,256]{2,1,0:T(8,128)S(1)}, u32[]{:S(2)}, u32[]{:S(2)}) collective-permute-start(f32[1,64,256]{2,1,0:T(8,128)S(1)} %get-tuple-element.46), channel_id=1, source_target_pairs={{0,16},{1,17},{2,18},{3,19},{4,20},{5,21},{6,22},{7,23},{8,24},{9,... | collective-permute-start | bytes 196616 | tf_op jit(solution)/shard_map/ppermute | solution.py:20
  11.2 8.2 %collective-permute-start.1 = (f32[1,64,256]{2,1,0:T(8,128)S(1)}, f32[1,64,256]{2,1,0:T(8,128)S(1)}, u32[]{:S(2)}, u32[]{:S(2)}) collective-permute-start(f32[1,64,256]{2,1,0:T(8,128)S(1)} %get-tuple-element.45), channel_id=1, source_target_pairs={{16,0},{17,1},{18,2},{19,3},{20,4},{21,5},{22,6},{23,7},{24,8},{25... | collective-permute-start | bytes 196616 | tf_op jit(solution)/shard_map/ppermute | solution.py:23
  13.9 10.0 %collective-permute-start.9 = (f32[18,1,256]{2,1,0:T(1,128)S(1)}, f32[18,1,256]{2,1,0:T(1,128)S(1)}, u32[]{:S(2)}, u32[]{:S(2)}) collective-permute-start(f32[18,1,256]{2,1,0:T(1,128)S(1)} %get-tuple-element.38), channel_id=1, source_target_pairs={{4,0},{8,4},{12,8},{5,1},{9,5},{13,9},{6,2},{10,6},{14,10},{7,3},{... | collective-permute-start | bytes 55304 | tf_op jit(solution)/shard_map/ppermute | solution.py:23
  15.2 8.7 %collective-permute-start.8 = (f32[18,1,256]{2,1,0:T(1,128)S(1)}, f32[18,1,256]{2,1,0:T(1,128)S(1)}, u32[]{:S(2)}, u32[]{:S(2)}) collective-permute-start(f32[18,1,256]{2,1,0:T(1,128)S(1)} %get-tuple-element.37), channel_id=1, source_target_pairs={{0,4},{4,8},{8,12},{1,5},{5,9},{9,13},{2,6},{6,10},{10,14},{3,7},{... | collective-permute-start | bytes 55304 | tf_op jit(solution)/shard_map/ppermute | solution.py:20
  19.4 16.5 %collective-permute-start.2 = (f32[18,1,256]{2,1,0:T(1,128)S(1)}, f32[18,1,256]{2,1,0:T(1,128)S(1)}, u32[]{:S(2)}, u32[]{:S(2)}) collective-permute-start(f32[18,1,256]{2,1,0:T(1,128)S(1)} %get-tuple-element.36), channel_id=1, source_target_pairs={{0,4},{4,8},{8,12},{1,5},{5,9},{9,13},{2,6},{6,10},{10,14},{3,7},{... | collective-permute-start | bytes 55304 | tf_op jit(solution)/shard_map/ppermute | solution.py:20
  22.6 13.3 %collective-permute-start.3 = (f32[18,1,256]{2,1,0:T(1,128)S(1)}, f32[18,1,256]{2,1,0:T(1,128)S(1)}, u32[]{:S(2)}, u32[]{:S(2)}) collective-permute-start(f32[18,1,256]{2,1,0:T(1,128)S(1)} %get-tuple-element.35), channel_id=1, source_target_pairs={{4,0},{8,4},{12,8},{5,1},{9,5},{13,9},{6,2},{10,6},{14,10},{7,3},{... | collective-permute-start | bytes 55304 | tf_op jit(solution)/shard_map/ppermute | solution.py:23
  27.7 14.0 %collective-permute-start.11 = (f32[18,66,1]{1,2,0:T(1,128)S(1)}, f32[18,66,1]{1,2,0:T(1,128)S(1)}, u32[]{:S(2)}, u32[]{:S(2)}) collective-permute-start(f32[18,66,1]{1,2,0:T(1,128)S(1)} %copy.15), channel_id=1, source_target_pairs={{1,0},{2,1},{3,2},{5,4},{6,5},{7,6},{9,8},{10,9},{11,10},{13,12},{... | collective-permute-start | bytes 14264 | tf_op jit(solution)/shard_map/ppermute | solution.py:23
  32.8 10.0 %collective-permute-start.10 = (f32[18,66,1]{1,2,0:T(1,128)}, f32[18,66,1]{1,2,0:T(1,128)}, u32[]{:S(2)}, u32[]{:S(2)}) collective-permute-start(f32[18,66,1]{1,2,0:T(1,128)} %copy.13), channel_id=1, source_target_pairs={{0,1},{1,2},{2,3},{4,5},{5,6},{6,7},{8,9},{9,10},{10,11},{12,13},{... | collective-permute-start | bytes 14264 | tf_op jit(solution)/shard_map/ppermute | solution.py:20
  36.8 7.9 %collective-permute-start.4 = (f32[18,66,1]{1,2,0:T(1,128)S(1)}, f32[18,66,1]{1,2,0:T(1,128)S(1)}, u32[]{:S(2)}, u32[]{:S(2)}) collective-permute-start(f32[18,66,1]{1,2,0:T(1,128)S(1)} %copy.9), channel_id=1, source_target_pairs={{0,1},{1,2},{2,3},{4,5},{5,6},{6,7},{8,9},{9,10},{10,11},{12,13},{... | collective-permute-start | bytes 14264 | tf_op jit(solution)/shard_map/ppermute | solution.py:20
  39.5 6.3 %collective-permute-start.5 = (f32[18,66,1]{1,2,0:T(1,128)S(1)}, f32[18,66,1]{1,2,0:T(1,128)S(1)}, u32[]{:S(2)}, u32[]{:S(2)}) collective-permute-start(f32[18,66,1]{1,2,0:T(1,128)S(1)} %copy.11), channel_id=1, source_target_pairs={{1,0},{2,1},{3,2},{5,4},{6,5},{7,6},{9,8},{10,9},{11,10},{13,12},{... | collective-permute-start | bytes 14264 | tf_op jit(solution)/shard_map/ppermute | solution.py:23
  176.0 6.2 %collective-permute-start.13 = (f32[1,64,256]{2,1,0:T(8,128)S(1)}, f32[1,64,256]{2,1,0:T(8,128)S(1)}, u32[]{:S(2)}, u32[]{:S(2)}) collective-permute-start(f32[1,64,256]{2,1,0:T(8,128)S(1)} %get-tuple-element.44), channel_id=1, source_target_pairs={{16,0},{17,1},{18,2},{19,3},{20,4},{21,5},{22,6},{23,7},{24,8},{25... | collective-permute-start | bytes 196616 | tf_op jit(solution)/shard_map/ppermute | solution.py:23
  182.7 6.1 %collective-permute-start.15 = (f32[18,1,256]{2,1,0:T(1,128)S(1)}, f32[18,1,256]{2,1,0:T(1,128)S(1)}, u32[]{:S(2)}, u32[]{:S(2)}) collective-permute-start(f32[18,1,256]{2,1,0:T(1,128)S(1)} %get-tuple-element.34), channel_id=1, source_target_pairs={{4,0},{8,4},{12,8},{5,1},{9,5},{13,9},{6,2},{10,6},{14,10},{7,3},{... | collective-permute-start | bytes 55304 | tf_op jit(solution)/shard_map/ppermute | solution.py:23
  191.5 7.3 %collective-permute-start.17 = (f32[18,66,1]{1,2,0:T(1,128)S(1)}, f32[18,66,1]{1,2,0:T(1,128)S(1)}, u32[]{:S(2)}, u32[]{:S(2)}) collective-permute-start(f32[18,66,1]{1,2,0:T(1,128)S(1)} %copy.19), channel_id=1, source_target_pairs={{1,0},{2,1},{3,2},{5,4},{6,5},{7,6},{9,8},{10,9},{11,10},{13,12},{... | collective-permute-start | bytes 14264 | tf_op jit(solution)/shard_map/ppermute | solution.py:23
  208.4 5.4 %collective-permute-start.19 = (f32[1,64,256]{2,1,0:T(8,128)S(1)}, f32[1,64,256]{2,1,0:T(8,128)S(1)}, u32[]{:S(2)}, u32[]{:S(2)}) collective-permute-start(f32[1,64,256]{2,1,0:T(8,128)S(1)} %get-tuple-element.42), channel_id=1, source_target_pairs={{16,0},{17,1},{18,2},{19,3},{20,4},{21,5},{22,6},{23,7},{24,8},{25... | collective-permute-start | bytes 196616 | tf_op jit(solution)/shard_map/ppermute | solution.py:23
  215.0 6.6 %collective-permute-start.21 = (f32[18,1,256]{2,1,0:T(1,128)S(1)}, f32[18,1,256]{2,1,0:T(1,128)S(1)}, u32[]{:S(2)}, u32[]{:S(2)}) collective-permute-start(f32[18,1,256]{2,1,0:T(1,128)S(1)} %get-tuple-element.32), channel_id=1, source_target_pairs={{4,0},{8,4},{12,8},{5,1},{9,5},{13,9},{6,2},{10,6},{14,10},{7,3},{... | collective-permute-start | bytes 55304 | tf_op jit(solution)/shard_map/ppermute | solution.py:23
  224.6 11.0 %collective-permute-start.23 = (f32[18,66,1]{1,2,0:T(1,128)S(1)}, f32[18,66,1]{1,2,0:T(1,128)}, u32[]{:S(2)}, u32[]{:S(2)}) collective-permute-start(f32[18,66,1]{1,2,0:T(1,128)S(1)} %copy.23), channel_id=1, source_target_pairs={{1,0},{2,1},{3,2},{5,4},{6,5},{7,6},{9,8},{10,9},{11,10},{13,12},{... | collective-permute-start | bytes 14264 | tf_op jit(solution)/shard_map/ppermute | solution.py:23
  230.9 6.5 %collective-permute-start.22 = (f32[18,66,1]{1,2,0:T(1,128)}, f32[18,66,1]{1,2,0:T(1,128)}, u32[]{:S(2)}, u32[]{:S(2)}) collective-permute-start(f32[18,66,1]{1,2,0:T(1,128)} %copy.21), channel_id=1, source_target_pairs={{0,1},{1,2},{2,3},{4,5},{5,6},{6,7},{8,9},{9,10},{10,11},{12,13},{... | collective-permute-start | bytes 14264 | tf_op jit(solution)/shard_map/ppermute | solution.py:20
  244.1 5.5 %collective-permute-start.25 = (f32[1,64,256]{2,1,0:T(8,128)S(1)}, f32[1,64,256]{2,1,0:T(8,128)S(1)}, u32[]{:S(2)}, u32[]{:S(2)}) collective-permute-start(f32[1,64,256]{2,1,0:T(8,128)S(1)} %get-tuple-element.40), channel_id=1, source_target_pairs={{16,0},{17,1},{18,2},{19,3},{20,4},{21,5},{22,6},{23,7},{24,8},{25... | collective-permute-start | bytes 196616 | tf_op jit(solution)/shard_map/ppermute | solution.py:23
  250.8 7.9 %collective-permute-start.27 = (f32[18,1,256]{2,1,0:T(1,128)S(1)}, f32[18,1,256]{2,1,0:T(1,128)S(1)}, u32[]{:S(2)}, u32[]{:S(2)}) collective-permute-start(f32[18,1,256]{2,1,0:T(1,128)S(1)} %get-tuple-element.30), channel_id=1, source_target_pairs={{4,0},{8,4},{12,8},{5,1},{9,5},{13,9},{6,2},{10,6},{14,10},{7,3},{... | collective-permute-start | bytes 55304 | tf_op jit(solution)/shard_map/ppermute | solution.py:23
  252.1 6.6 %collective-permute-start.26 = (f32[18,1,256]{2,1,0:T(1,128)S(1)}, f32[18,1,256]{2,1,0:T(1,128)S(1)}, u32[]{:S(2)}, u32[]{:S(2)}) collective-permute-start(f32[18,1,256]{2,1,0:T(1,128)S(1)} %get-tuple-element.29), channel_id=1, source_target_pairs={{0,4},{4,8},{8,12},{1,5},{5,9},{9,13},{2,6},{6,10},{10,14},{3,7},{... | collective-permute-start | bytes 55304 | tf_op jit(solution)/shard_map/ppermute | solution.py:20
  261.8 29.2 %collective-permute-start.29 = (f32[18,66,1]{1,2,0:T(1,128)S(1)}, f32[18,66,1]{1,2,0:T(1,128)S(1)}, u32[]{:S(2)}, u32[]{:S(2)}) collective-permute-start(f32[18,66,1]{1,2,0:T(1,128)S(1)} %copy.27), channel_id=1, source_target_pairs={{1,0},{2,1},{3,2},{5,4},{6,5},{7,6},{9,8},{10,9},{11,10},{13,12},{... | collective-permute-start | bytes 14264 | tf_op jit(solution)/shard_map/ppermute | solution.py:23
  265.8 26.4 %collective-permute-start.28 = (f32[18,66,1]{1,2,0:T(1,128)S(1)}, f32[18,66,1]{1,2,0:T(1,128)S(1)}, u32[]{:S(2)}, u32[]{:S(2)}) collective-permute-start(f32[18,66,1]{1,2,0:T(1,128)S(1)} %copy.25), channel_id=1, source_target_pairs={{0,1},{1,2},{2,3},{4,5},{5,6},{6,7},{8,9},{9,10},{10,11},{12,13},{... | collective-permute-start | bytes 14264 | tf_op jit(solution)/shard_map/ppermute | solution.py:20
  (48 other events, 426.1 us)
where the time goes:
time: 303 us; the launch traced here: 300 us
  local copies, waits for them, and re-layouts  104 us (34%)
  starting transfers between devices  84.9 us (28%)
  other arithmetic  61.9 us (20%)
  blocking collectives  44 us (15%)
    ppermute x15, starting transfers between devices, padded_2(): lax.ppermute(lax.slice_in_dim(block, block.shape[dim] - width, None, axis...  53.1 us
    all_gather x1, blocking collectives, shards(): everything = lax.all_gather(packed, ('gx', 'gy', 'gz'), axis=0, tiled=True)  44 us
    ppermute x15, starting transfers between devices, padded_2(): lax.ppermute(lax.slice_in_dim(block, 0, width, axis=dim), axis, backward)  31.8 us
    add x2, local copies, waits for them, and re-layouts, shards(): blocks + correction[:, None, :, None, :, None]  21.6 us
    add x1, other arithmetic, shards(): pressure_now = pressure_start + OMEGA * start_residual / diagonal_sum  13.2 us
    reshape x1, local copies, waits for them, and re-layouts, block_sum(): values.reshape(depth // RATIO, RATIO, rows // RATIO, RATIO, width // RATI...  12.2 us
    add x2, other arithmetic, shards(): pressure_now = pressure_now + OMEGA * (source - applied) / diagonal_sum  12 us
    slice x13, local copies, waits for them, and re-layouts, padded_2(): lax.slice_in_dim(block, block.shape[dim] - width, None, axis=dim)  7.29 us
  transfers between devices with their start and end apart: 30, of which 5 were waited for; matrix products, arithmetic and copies ran while one was open for 15% of the time, Pallas kernels for 0%

commit v1 on v0

v1 whole, which is shorter than its diff:
```python
import functools

import jax
import jax.numpy as jnp
from jax import lax
from jax.experimental import pallas as pl
from jax.experimental.pallas import tpu as pltpu
from jax.sharding import PartitionSpec as P

RATIO = 8
SWEEPS = 4
COARSE_SWEEPS = 8
OMEGA = 0.8
OMEGA_COARSE = 0.8

LANES = 128
ROWS = 8
DEPTH = SWEEPS
SLOTS = LANES // DEPTH
F32 = jnp.float32
VMEM_LIMIT = 12 * 1024 * 1024


def pairs(count, odd):
    start = 1 if odd else 0
    out = []
    for low in range(start, count + start - 1, 2):
        high = (low + 1) % count
        out += [(low, high), (high, low)]
    return out


def flips(count, bit):
    return [(i, i ^ bit) for i in range(count)]


def on_chip(value):
    return pltpu.with_memory_space_constraint(value, pltpu.VMEM)


def run(kernel, outs, args, scratch=(), flops=1000, name=None, out_spaces=None):
    whole = pl.BlockSpec(memory_space=pltpu.VMEM)
    shapes = [pltpu.VMEM(shape, F32) for shape in outs] if out_spaces is None else out_spaces
    result = pl.pallas_call(
        kernel,
        out_shape=shapes,
        in_specs=[whole] * len(args),
        out_specs=[whole] * len(outs),
        scratch_shapes=list(scratch),
        compiler_params=pltpu.CompilerParams(vmem_limit_bytes=VMEM_LIMIT),
        cost_estimate=pl.CostEstimate(flops=flops, bytes_accessed=0, transcendentals=0),
        name=name,
    )(*[on_chip(a) for a in args])
    return result


def lane_of(shape):
    return lax.broadcasted_iota(jnp.int32, shape, len(shape) - 1)


def row_of(shape):
    return lax.broadcasted_iota(jnp.int32, shape, len(shape) - 2)


def roll(values, shift, axis):
    size = values.shape[axis]
    if isinstance(shift, int):
        shift = shift % size
        if shift == 0:
            return values
    return pltpu.roll(values, shift, axis)


def face(one, other):
    half = jnp.where(jnp.minimum(one, other) > 0.0, 0.5, 1.0)
    return half * (one + other)


def group_rows(values):
    rows, width = values.shape
    return values.reshape(rows // RATIO, RATIO, width).sum(axis=1)


def split3(values):
    a = values.astype(jnp.bfloat16)
    rest = values - a.astype(F32)
    b = rest.astype(jnp.bfloat16)
    c = (rest - b.astype(F32)).astype(jnp.bfloat16)
    return jnp.concatenate([a, b, c], axis=0)


def exact_dot(values, onehot):
    rows = values.shape[0]
    out = jnp.dot(split3(values), onehot, preferred_element_type=F32)
    return out[:rows] + out[rows : 2 * rows] + out[2 * rows :]


class Grid:
    def __init__(self, shape):
        self.Z, self.Y, self.X = shape
        self.nz, self.ny, self.nx = (lax.axis_size("gx"), lax.axis_size("gy"), lax.axis_size("gz"))
        self.cz, self.cy, self.cx = (n // RATIO for n in shape)
        self.blocks = -(-3 * self.Z // SLOTS)
        self.XE = self.X + LANES
        self.YE = self.Y + ROWS
        self.ZE = self.Z + 2 * DEPTH
        self.zsides = 1 if self.nz == 2 else 2
        self.ysides = 1 if self.ny == 2 else 2
        self.xsides = 1 if self.nx == 2 else 2
        assert 2 * DEPTH == ROWS and 2 * self.Z <= SLOTS and self.Z % 2 == 0
        assert self.blocks * LANES <= self.X and self.cy == ROWS
        assert self.cx * self.nx == LANES

    def where(self):
        return lax.axis_index("gx"), lax.axis_index("gy"), lax.axis_index("gz")

    def slot(self, q, z):
        index = q * self.Z + z
        return index // SLOTS, (index % SLOTS) * DEPTH


def pack_kernel(g, *refs):
    src = refs[:3]
    z_out = refs[3 : 3 + g.zsides]
    x_out = refs[3 + g.zsides :]
    zi, yi, xi = g.where()
    for side, out in enumerate(z_out):
        high = (zi % 2) == side
        at = jnp.where(high, g.Z - DEPTH, 0)
        out[0:DEPTH] = src[0][pl.ds(at, DEPTH)]
        out[DEPTH : 2 * DEPTH] = src[1][pl.ds(at, DEPTH)]
        at = jnp.where(high, g.Z - DEPTH + 1, 0)
        out[2 * DEPTH :] = src[2][pl.ds(at, DEPTH - 1)]
    lane = lane_of((g.Y, LANES))
    packs = []
    for high in (True, False):
        acc = [jnp.zeros((g.Y, LANES), F32) for _ in range(g.blocks)]
        for q in range(3):
            for z in range(g.Z):
                block, at = g.slot(q, z)
                if high:
                    moved = roll(src[q][z, :, g.X - LANES :], at + DEPTH, 1)
                else:
                    moved = roll(src[q][z, :, :LANES], at, 1)
                acc[block] = jnp.where((lane >= at) & (lane < at + DEPTH), moved, acc[block])
        packs.append(acc)
    even = (xi % 2) == 0
    for block in range(g.blocks):
        hi, lo = packs[0][block], packs[1][block]
        for side, out in enumerate(x_out):
            out[block] = jnp.where(even == (side == 0), hi, lo)


def pick(first, second, even, inside):
    if second is None:
        return jnp.where(even & inside, first, 0.0)
    return jnp.where(inside, jnp.where(even, first, second), 0.0)


def from_high(index, count, bufs, view):
    even = (index % 2) == 0
    second = view(bufs[1]) if len(bufs) > 1 else None
    return pick(view(bufs[0]), second, even, index < count - 1)


def from_low(index, count, bufs, view):
    odd = (index % 2) == 1
    second = view(bufs[1]) if len(bufs) > 1 else None
    return pick(view(bufs[0]), second, odd, index > 0)


def pack_rows_kernel(g, *refs):
    src = refs[:3]
    x_in = refs[3 : 3 + g.xsides]
    y_out = refs[3 + g.xsides :]
    zi, yi, xi = g.where()
    half = g.Z // 2
    last = g.Y - ROWS
    for side, out in enumerate(y_out):
        high = (yi % 2) == side

        def fill(top, out=out):
            for q in range(3):
                for pair in range(half):
                    a, b = src[q][2 * pair], src[q][2 * pair + 1]
                    if top:
                        part = jnp.concatenate([a[g.Y - DEPTH :], b[g.Y - DEPTH :]], axis=0)
                    else:
                        part = jnp.concatenate([a[:DEPTH], b[:DEPTH]], axis=0)
                    out[q * half + pair] = part
            rows = slice(g.Y - DEPTH, g.Y) if top else slice(0, DEPTH)
            for block in range(g.blocks):
                hi = from_high(xi, g.nx, x_in, lambda r: r[block, rows, :])
                lo = from_low(xi, g.nx, x_in, lambda r: r[block, rows, :])
                out[3 * half, :, block * LANES : (block + 1) * LANES] = jnp.concatenate(
                    [hi, lo], axis=0
                )

        pl.when(high)(functools.partial(fill, True))
        pl.when(jnp.logical_not(high))(functools.partial(fill, False))


def gather_rows(g, yi, y_in, hy, ly):
    hy[...] = from_high(yi, g.ny, y_in, lambda r: r[...])
    ly[...] = from_low(yi, g.ny, y_in, lambda r: r[...])


def gather_strips(g, xi, x_in, hy, ly, xh, xl):
    half = g.Z // 2
    for block in range(g.blocks):
        lanes = slice(block * LANES, (block + 1) * LANES)
        xh[block, : g.Y] = from_high(xi, g.nx, x_in, lambda r: r[block])
        xl[block, : g.Y] = from_low(xi, g.nx, x_in, lambda r: r[block])
        top, low = hy[3 * half, :, lanes], ly[3 * half, :, lanes]
        xh[block, g.Y :] = jnp.concatenate([top[:DEPTH], low[:DEPTH]], axis=0)
        xl[block, g.Y :] = jnp.concatenate([top[DEPTH:], low[DEPTH:]], axis=0)


def row_halo(g, hy, ly, q, z):
    half = g.Z // 2
    at = (z % 2) * DEPTH
    block = q * half + z // 2
    return jnp.concatenate([hy[block, at : at + DEPTH], ly[block, at : at + DEPTH]], axis=0)


def restrict_kernel(g, *refs):
    n = 3
    src = refs[:n]
    z_in = refs[n : n + g.zsides]
    n += g.zsides
    y_in = refs[n : n + g.ysides]
    n += g.ysides
    x_in = refs[n : n + g.xsides]
    n += g.xsides
    x_own = refs[n : n + g.xsides]
    n += g.xsides
    outs = refs[n : n + g.zsides]
    n += g.zsides
    hy, ly, xh, xl = refs[n:]
    p, k, s = src
    zi, yi, xi = g.where()
    gather_rows(g, yi, y_in, hy, ly)
    gather_strips(g, xi, x_in, hy, ly, xh, xl)
    Z, Y, X = g.Z, g.Y, g.X
    half = Z // 2

    zero = jnp.zeros((Y, X), F32)
    flux_z, weight_z = [], []
    for layer in range(0, Z + 1, RATIO):
        if layer == 0:
            p0 = from_low(zi, g.nz, z_in, lambda r: r[DEPTH - 1])
            k0 = from_low(zi, g.nz, z_in, lambda r: r[2 * DEPTH - 1])
        else:
            p0, k0 = p[layer - 1], k[layer - 1]
        if layer == Z:
            p1 = from_high(zi, g.nz, z_in, lambda r: r[0])
            k1 = from_high(zi, g.nz, z_in, lambda r: r[DEPTH])
        else:
            p1, k1 = p[layer], k[layer]
        w = face(k0, k1)
        weight_z.append(group_rows(w))
        flux_z.append(group_rows(w * (p1 - p0)))

    lane = lane_of((Y, LANES))
    even = (xi % 2) == 0
    if g.xsides == 1:
        own_hi = own_lo = x_own[0][0]
    else:
        own_hi = jnp.where(even, x_own[0][0], x_own[1][0])
        own_lo = jnp.where(even, x_own[1][0], x_own[0][0])

    def side_sums(own, other, lane_in, flip):
        wk = face(roll(own, -Z * DEPTH, 1), roll(other, -Z * DEPTH, 1))
        diff = (other - own) if flip else (own - other)
        keep = (lane % DEPTH == lane_in) & (lane < Z * DEPTH)
        w = jnp.where(keep, wk, 0.0)
        result = []
        for value in (w, w * diff):
            total = group_rows(value)
            step = DEPTH
            while step < RATIO * DEPTH:
                total = total + roll(total, -step, 1)
                step *= 2
            result.append(total)
        return result

    low_w, low_f = side_sums(own_lo, roll(xl[0, :Y], -(DEPTH - 1), 1), 0, False)
    high_w, high_f = side_sums(own_hi, roll(xh[0, :Y], DEPTH - 1, 1), DEPTH - 1, True)
    lane8 = lane_of((ROWS, X))
    row8 = row_of((ROWS, X))
    row = row_of((Y, X))
    inner = (lane8 % RATIO == 0) & (lane8 > 0)

    def widen(value, at, cell):
        moved = roll(value, (at % LANES) - cell, 1)
        wide = jnp.concatenate([moved] * (X // LANES), axis=1)
        return jnp.where(lane8 == at, wide, 0.0)

    rows = []
    for cz in range(g.cz):
        acc_s = zero
        acc_w = zero
        acc_f = zero
        acc_wy = zero
        acc_fy = zero
        low_wy = low_fy = top_w = top_f = jnp.zeros((1, X), F32)
        for z in range(cz * RATIO, (cz + 1) * RATIO):
            pz, kz = p[z], k[z]
            acc_s = acc_s + s[z]
            w = 0.5 * (kz + roll(kz, 1, 1))
            acc_w = acc_w + w
            acc_f = acc_f + w * (pz - roll(pz, 1, 1))
            w = 0.5 * (kz + roll(kz, 1, 0))
            acc_wy = acc_wy + w
            acc_fy = acc_fy + w * (pz - roll(pz, 1, 0))
            at = (z % 2) * DEPTH
            below = [ly[q * half + z // 2, at + DEPTH - 1 : at + DEPTH, :] for q in range(2)]
            above = [hy[q * half + z // 2, at : at + 1, :] for q in range(2)]
            w = face(kz[:1], below[1])
            low_wy = low_wy + w
            low_fy = low_fy + w * (pz[:1] - below[0])
            w = face(kz[Y - 1 :], above[1])
            top_w = top_w + w
            top_f = top_f + w * (above[0] - pz[Y - 1 :])

        def lower(acc, low):
            kept = group_rows(jnp.where(row % RATIO == 0, acc, 0.0))
            return jnp.where(row8 == 0, jnp.broadcast_to(low, (ROWS, X)), kept)

        weight_y = lower(acc_wy, low_wy)
        flux_y = lower(acc_fy, low_fy)

        def upper(values, top):
            return jnp.where(
                row8 == g.cy - 1, jnp.broadcast_to(top, (ROWS, X)), roll(values, -1, 0)
            )

        weight_x = jnp.where(inner, group_rows(acc_w), 0.0)
        flux_x = jnp.where(inner, group_rows(acc_f), 0.0)
        cell = cz * RATIO * DEPTH
        x_low = widen(low_w, 0, cell)
        x_high = widen(high_w, X - 1, cell + DEPTH - 1)
        f_low = widen(low_f, 0, cell)
        f_high = widen(high_f, X - 1, cell + DEPTH - 1)
        rhs = (
            group_rows(acc_s)
            - (flux_z[cz] - flux_z[cz + 1])
            - (flux_y - upper(flux_y, top_f))
            - (flux_x - roll(flux_x, -1, 1))
            - (f_low - f_high)
        )
        diagonal = (
            weight_z[cz]
            + weight_z[cz + 1]
            + weight_y
            + upper(weight_y, top_w)
            + weight_x
            + roll(weight_x, -1, 1)
            + x_low
            + x_high
        )
        rows.append([rhs, diagonal, weight_z[cz], weight_y, weight_x + x_low])

    items = [rows[cz][q] for q in range(5) for cz in range(g.cz)]
    onehot = (
        lax.broadcasted_iota(jnp.int32, (X, LANES), 0) // RATIO
        == lax.broadcasted_iota(jnp.int32, (X, LANES), 1)
    ).astype(jnp.bfloat16)
    summed = exact_dot(jnp.concatenate(items, axis=0), onehot)
    per = LANES // g.cx
    cells = [jnp.zeros((ROWS, LANES), F32) for _ in range(coarse_blocks(g))]
    for m in range(len(items)):
        place = lax.rem(m % per + xi, per) * g.cx
        cells[m // per] = cells[m // per] + pltpu.roll(
            summed[m * ROWS : (m + 1) * ROWS], place, 1
        )
    for block, value in enumerate(cells):
        outs[0][block] = value

    for side, out in enumerate(outs):
        base = coarse_blocks(g) if side == 0 else 0
        high = (zi % 2) == side

        def fill(top, out=out, base=base):
            first = Z - DEPTH if top else 0
            for q in range(3):
                for d in range(DEPTH):
                    part = row_halo(g, hy, ly, q, first + d)
                    for half_lane in range(X // LANES):
                        out[base + (q * DEPTH + d) * (X // LANES) + half_lane] = part[
                            :, half_lane * LANES : (half_lane + 1) * LANES
                        ]
            at_block = base + 3 * DEPTH * (X // LANES)
            wide = lane_of((g.YE, LANES))
            acc = jnp.zeros((g.YE, LANES), F32)
            span = DEPTH * DEPTH
            for piece, (ref, q) in enumerate((r, q) for r in (xh, xl) for q in range(3)):
                block, lane_at = g.slot(q, first)
                moved = roll(ref[block], piece * span - lane_at, 1)
                acc = jnp.where((wide >= piece * span) & (wide < (piece + 1) * span), moved, acc)
            out[at_block:] = acc.reshape(g.YE // ROWS, ROWS, LANES)

        pl.when(high)(functools.partial(fill, True))
        pl.when(jnp.logical_not(high))(functools.partial(fill, False))


def coarse_blocks(g):
    per = LANES // g.cx
    return -(-5 * g.cz // per)


def relay_blocks(g):
    return 3 * DEPTH * (g.X // LANES) + g.YE // ROWS


def extend_kernel(g, *refs):
    n = 3
    src = refs[:n]
    y_in = refs[n : n + g.ysides]
    n += g.ysides
    x_in = refs[n : n + g.xsides]
    n += g.xsides
    outs = refs[n : n + 3]
    hy, ly, xh, xl = refs[n + 3 :]
    zi, yi, xi = g.where()
    gather_rows(g, yi, y_in, hy, ly)
    gather_strips(g, xi, x_in, hy, ly, xh, xl)
    lane = lane_of((g.YE, LANES))
    for q in range(3):
        for z in range(g.Z):
            outs[q][z, : g.Y, : g.X] = src[q][z]
            outs[q][z, g.Y :, : g.X] = row_halo(g, hy, ly, q, z)
            block, at = g.slot(q, z)
            hi = roll(xh[block], -at, 1)
            lo = roll(xl[block], -at - DEPTH, 1)
            outs[q][z, :, g.X :] = jnp.where(
                lane < DEPTH, hi, jnp.where(lane >= LANES - DEPTH, lo, 0.0)
            )


def sweep_range(g, zi, sweep):
    reach = SWEEPS - sweep
    low = jnp.where(zi > 0, DEPTH - reach, DEPTH)
    high = jnp.where(zi < g.nz - 1, DEPTH + g.Z + reach, DEPTH + g.Z)
    return low, high


def weights_kernel(g, *refs):
    own = refs[:3]
    n = 3
    z_in = refs[n : n + g.zsides]
    n += g.zsides
    relay = refs[n : n + g.zsides]
    n += g.zsides
    pe, se, fz, fy, fx, dinv = refs[n : n + 6]
    ke = refs[n + 6]
    zi, yi, xi = g.where()
    Z, Y, X = g.Z, g.Y, g.X
    ext = (pe, ke, se)
    for q in range(3):
        ext[q][DEPTH : DEPTH + Z] = own[q][...]
    zero = jnp.zeros((g.YE, g.XE), F32)
    lane = lane_of((g.YE, LANES))
    for side in range(g.zsides):
        base = coarse_blocks(g) if side == 0 else 0
        above = (zi % 2) == side

        def fill(top, side=side, base=base):
            first = DEPTH + Z if top else 0
            for q in range(3):
                for d in range(DEPTH):
                    if q < 2:
                        at = q * DEPTH + d
                    else:
                        at = 2 * DEPTH + (d if top else d - 1)
                        if (top and d == DEPTH - 1) or (not top and d == 0):
                            ext[q][first + d] = zero
                            continue
                    ext[q][first + d, :Y, :X] = z_in[side][at]
                    for part in range(X // LANES):
                        ext[q][first + d, Y:, part * LANES : (part + 1) * LANES] = relay[side][
                            base + (q * DEPTH + d) * (X // LANES) + part
                        ]
                    strip = relay[side][base + 3 * DEPTH * (X // LANES) :].reshape(g.YE, LANES)
                    at_hi = (q * DEPTH + d) * DEPTH
                    at_lo = ((3 + q) * DEPTH + d) * DEPTH
                    hi = roll(strip, -at_hi, 1)
                    lo = roll(strip, -at_lo - DEPTH, 1)
                    ext[q][first + d, :, X:] = jnp.where(
                        lane < DEPTH, hi, jnp.where(lane >= LANES - DEPTH, lo, 0.0)
                    )

        pl.when(above & (zi < g.nz - 1))(functools.partial(fill, True))
        pl.when(jnp.logical_not(above) & (zi > 0))(functools.partial(fill, False))

    @pl.when(zi == 0)
    def _():
        pe[DEPTH - 1] = zero
        ke[DEPTH - 1] = zero

    @pl.when(zi == g.nz - 1)
    def _():
        pe[DEPTH + Z] = zero
        ke[DEPTH + Z] = zero

    low, high = sweep_range(g, zi, 1)
    fz[low] = face(ke[low], ke[low - 1])

    def body(z, carry):
        kz = ke[z]
        above = face(ke[z + 1], kz)
        fz[z + 1] = above
        wy = face(kz, roll(kz, 1, 0))
        wx = face(kz, roll(kz, 1, 1))
        fy[z] = wy
        fx[z] = wx
        total = fz[z] + above + wy + roll(wy, -1, 0) + wx + roll(wx, -1, 1)
        dinv[z] = jnp.where(kz > 0.0, OMEGA / total, 0.0)
        return carry

    lax.fori_loop(low, high, body, 0)


def sweep_kernel(g, sweep, *refs):
    v, s, fz, fy, fx, dinv, out = refs
    zi, yi, xi = g.where()
    final = sweep == SWEEPS
    low, high = sweep_range(g, zi, sweep)

    def body(z, carry):
        vz = v[z]
        wy, wx = fy[z], fx[z]
        total = s[z] + fz[z] * v[z - 1] + fz[z + 1] * v[z + 1]
        total = total + wy * roll(vz, 1, 0) + roll(wy * vz, -1, 0)
        total = total + wx * roll(vz, 1, 1) + roll(wx * vz, -1, 1)
        new = (1.0 - OMEGA) * vz + dinv[z] * total
        if final:
            out[z - DEPTH] = new[: g.Y, : g.X]
        else:
            out[z] = new
        return carry

    lax.fori_loop(low, high, body, 0)
    if not final:
        zero = jnp.zeros((g.YE, g.XE), F32)

        @pl.when(zi == 0)
        def _():
            out[DEPTH - 1] = zero

        @pl.when(zi == g.nz - 1)
        def _():
            out[DEPTH + g.Z] = zero


def solve_kernel(g, gathered, fine, out):
    zi, yi, xi = g.where()
    per = LANES // g.cx
    group = lane_of((ROWS, LANES)) // g.cx

    def relative(a, b, c):
        d = jnp.bitwise_xor(a, zi) + g.nz * jnp.bitwise_xor(b, yi)
        e = jnp.bitwise_xor(c, xi)
        rev = 0
        bits = g.nx.bit_length() - 1
        for bit in range(bits):
            rev = rev + ((e >> bit) & 1) * (1 << (bits - 1 - bit))
        return d + g.nz * g.ny * rev

    layers = g.nz * g.cz
    height = g.ny * g.cy
    fields = []
    for q in range(5):
        planes = []
        for layer in range(layers):
            a, cz = divmod(layer, g.cz)
            m = q * g.cz + cz
            tiles = []
            for b in range(g.ny):
                value = gathered[relative(a, b, 0), m // per]
                for c in range(1, g.nx):
                    value = jnp.where(
                        group == (m % per + c) % per, gathered[relative(a, b, c), m // per], value
                    )
                tiles.append(roll(value, -(m % per) * g.cx, 1))
            planes.append(jnp.concatenate(tiles, axis=0))
        fields.append(planes)
    rhs, diagonal, wz, wy, wx = fields
    shape = (height, LANES)
    zero = jnp.zeros(shape, F32)
    wz = [zero] + wz[1:]
    wy = [jnp.where(row_of(shape) == 0, 0.0, w) for w in wy]
    wx = [jnp.where(lane_of(shape) == 0, 0.0, w) for w in wx]
    scale = [OMEGA_COARSE / d for d in diagonal]

    def flux(e):
        result = []
        for i in range(layers):
            total = wy[i] * roll(e[i], 1, 0) + roll(wy[i] * e[i], -1, 0)
            total = total + wx[i] * roll(e[i], 1, 1) + roll(wx[i] * e[i], -1, 1)
            if i > 0:
                total = total + wz[i] * e[i - 1]
            if i < layers - 1:
                total = total + wz[i + 1] * e[i + 1]
            result.append(total)
        return result

    e = [sc * r for sc, r in zip(scale, rhs)]
    for _ in range(COARSE_SWEEPS - 1):
        f = flux(e)
        e = [(1.0 - OMEGA_COARSE) * e[i] + scale[i] * (rhs[i] + f[i]) for i in range(layers)]
    f = flux(e)
    left = zero
    total = zero
    for i in range(layers):
        left = left + (rhs[i] - diagonal[i] * e[i] + f[i])
        total = total + diagonal[i]
    shift = jnp.sum(left) / jnp.sum(total)

    own = []
    for cz in range(g.cz):
        mine = jnp.zeros((ROWS, LANES), F32)
        for a in range(g.nz):
            for b in range(g.ny):
                here = (zi == a) & (yi == b)
                mine = jnp.where(here, e[a * g.cz + cz][b * ROWS : (b + 1) * ROWS], mine)
        own.append(mine)
    onehot = (
        lax.broadcasted_iota(jnp.int32, (LANES, g.X), 0)
        == xi * g.cx + lax.broadcasted_iota(jnp.int32, (LANES, g.X), 1) // RATIO
    ).astype(jnp.bfloat16)
    wide = exact_dot(jnp.concatenate(own, axis=0), onehot) + shift
    for cz in range(g.cz):
        block = wide[cz * ROWS : (cz + 1) * ROWS]
        spread = jnp.broadcast_to(block[:, None, :], (g.cy, RATIO, g.X)).reshape(g.Y, g.X)
        for z in range(cz * RATIO, (cz + 1) * RATIO):
            out[z] = fine[z] + spread


def exchange(bufs, axis, count):
    return [lax.ppermute(b, axis, pairs(count, odd)) for odd, b in enumerate(bufs)]


def shards(pressure_start, source, permeability):
    g = Grid(pressure_start.shape)
    Z, Y, X = g.Z, g.Y, g.X
    fields = [on_chip(a) for a in (pressure_start, permeability, source)]
    z_shape = (3 * DEPTH - 1, Y, X)
    x_shape = (g.blocks, Y, LANES)
    y_shape = (3 * Z // 2 + 1, ROWS, X)
    sent = run(
        functools.partial(pack_kernel, g),
        [z_shape] * g.zsides + [x_shape] * g.xsides,
        fields,
        name="pack_faces",
    )
    z_sent, x_sent = sent[: g.zsides], sent[g.zsides :]
    z_got = exchange(z_sent, "gx", g.nz)
    x_got = exchange(x_sent, "gz", g.nx)
    y_sent = run(
        functools.partial(pack_rows_kernel, g), [y_shape] * g.ysides, fields + x_got, name="pack_rows"
    )
    y_got = exchange(y_sent, "gy", g.ny)

    halo_scratch = [
        pltpu.VMEM(y_shape, F32),
        pltpu.VMEM(y_shape, F32),
        pltpu.VMEM((g.blocks, g.YE, LANES), F32),
        pltpu.VMEM((g.blocks, g.YE, LANES), F32),
    ]
    nc, nr = coarse_blocks(g), relay_blocks(g)
    packed = run(
        functools.partial(restrict_kernel, g),
        [(nc + nr, ROWS, LANES)] + [(nr, ROWS, LANES)] * (g.zsides - 1),
        fields + z_got + y_got + x_got + list(x_sent),
        scratch=halo_scratch,
        name="restrict",
    )
    relay = exchange(packed, "gx", g.nz)
    cells = jnp.stack([packed[0][:nc], relay[0][:nc]])
    bit = 2
    while bit < g.nz:
        cells = jnp.concatenate([cells, lax.ppermute(cells, "gx", flips(g.nz, bit))])
        bit *= 2
    bit = 1
    while bit < g.ny:
        cells = jnp.concatenate([cells, lax.ppermute(cells, "gy", flips(g.ny, bit))])
        bit *= 2
    bit = g.nx // 2
    while bit >= 1:
        cells = jnp.concatenate([cells, lax.ppermute(cells, "gz", flips(g.nx, bit))])
        bit //= 2

    own = (Z, g.YE, g.XE)
    ext = (g.ZE, g.YE, g.XE)
    extended = run(
        functools.partial(extend_kernel, g),
        [own] * 3,
        fields + y_got + x_got,
        scratch=halo_scratch,
        name="extend",
    )
    pe, se, fz, fy, fx, dinv = run(
        functools.partial(weights_kernel, g),
        [ext] * 6,
        list(extended) + z_got + relay,
        scratch=[pltpu.VMEM(ext, F32)],
        name="weights",
    )
    v = pe
    for sweep in range(1, SWEEPS + 1):
        shape = (Z, Y, X) if sweep == SWEEPS else ext
        (v,) = run(
            functools.partial(sweep_kernel, g, sweep),
            [shape],
            [v, se, fz, fy, fx, dinv],
            name=f"sweep_{sweep}",
        )
    (out,) = run(
        functools.partial(solve_kernel, g),
        [(Z, Y, X)],
        [cells, v],
        name="solve",
        out_spaces=[jax.ShapeDtypeStruct((Z, Y, X), F32)],
    )
    return out


def solution(mesh):
    return jax.shard_map(
        shards,
        mesh=mesh,
        in_specs=(P("gx", "gy", "gz"), P("gx", "gy", "gz"), P("gx", "gy", "gz")),
        out_specs=P("gx", "gy", "gz"),
        check_vma=False,
    )
```

time: 303 us -> 64.6 us (0.21)
  local copies, waits for them, and re-layouts: 104 us -> 3.73 us
  starting transfers between devices: 84.9 us -> 15.5 us
  other arithmetic: 61.9 us -> 0.02 us
  blocking collectives: 44 us -> 0 us
  waiting for transfers between devices: 2.91 us -> 24.9 us
  Pallas kernels: 0 us -> 20 us
    ppermute x30 -> x10, starting transfers between devices: 84.9 us -> 15.5 us  [the longest x6 8.12 us: exchange(): lax.ppermute(b, axis, pairs(count, odd))]
    all_gather x1 -> x0, blocking collectives: 44 us -> none  [shards(): everything = lax.all_gather(packed, ('gx', 'gy', 'gz'), axis=0, tiled=True)]
    add x12 -> x0, other arithmetic: 37.9 us -> none  [the longest x1 13.2 us: shards(): pressure_now = pressure_start + OMEGA * start_residual / diagonal_sum]
    slice x36 -> x0, local copies, waits for them, and re-layouts: 36 us -> none  [the longest x13 7.29 us: padded_2(): lax.slice_in_dim(block, block.shape[dim] - width, None, axis=dim)]
    reshape x6 -> x0, local copies, waits for them, and re-layouts: 24.7 us -> none  [the longest x1 12.2 us: block_sum(): values.reshape(depth // RATIO, RATIO, rows // RATIO, RATIO, width // RATI...]
    ppermute x30 -> x10, waiting for transfers between devices: 2.91 us -> 24.9 us  [the longest x6 17.1 us: exchange(): lax.ppermute(b, axis, pairs(count, odd))]
    add x2 -> x0, local copies, waits for them, and re-layouts: 21.6 us -> none  [shards(): blocks + correction[:, None, :, None, :, None]]
    reduce_sum x9 -> x0, other arithmetic: 20.4 us -> none  [the longest x1 7.22 us: block_sum(): values.reshape(depth // RATIO, RATIO, rows // RATIO, RATIO, width // RATI...]
  transfers between devices with their start and end apart: 30 -> 10, of which waited for: 5 -> 7; matrix products, arithmetic and copies ran while one was open for 15% -> 0% of each run, Pallas kernels for 0% -> 24%
where the time goes in v1:
time: 64.6 us; the launch traced here: 64.3 us
  waiting for transfers between devices  24.9 us (39%)
  Pallas kernels  20 us (31%)
  starting transfers between devices  15.5 us (24%)
  local copies, waits for them, and re-layouts  3.73 us (6%)
    pallas_call x10, Pallas kernels, run(): pl.pallas_call(kernel, out_shape=shapes, in_specs=[whole] * len(args), ou...  20 us
    ppermute x6, waiting for transfers between devices, exchange(): lax.ppermute(b, axis, pairs(count, odd))  17.1 us
    ppermute x6, starting transfers between devices, exchange(): lax.ppermute(b, axis, pairs(count, odd))  8.12 us
    ppermute x2, starting transfers between devices, shards(): lax.ppermute(cells, 'gz', flips(g.nx, bit))  6.19 us
    ppermute x2, waiting for transfers between devices, shards(): lax.ppermute(cells, 'gy', flips(g.ny, bit))  5.57 us
    unnamed x10, local copies, waits for them, and re-layouts  3.69 us
    ppermute x2, waiting for transfers between devices, shards(): lax.ppermute(cells, 'gz', flips(g.nx, bit))  2.22 us
  transfers between devices with their start and end apart: 10, of which 7 were waited for; matrix products, arithmetic and copies ran while one was open for 0% of the time, Pallas kernels for 24%

profile of v1, /device:TPU:1, one launch (start us, length us, event | category | flops | bytes accessed | tf_op | source)
XLA Modules:
  0.0 64.3 jit_solution(16790908095213272523)
XLA Ops:
  0.0 1.2 %copy-done = f32[16,64,256]{2,1,0:T(8,128)S(1)} copy-done((f32[16,64,256]{2,1,0:T(8,128)S(1)}, f32[16,64,256]{2,1,0:T(8,128)}, u32[]{:S(2)}) %copy-start) | copy-done | bytes 1048600
  1.2 1.2 %copy-done.1 = f32[16,64,256]{2,1,0:T(8,128)S(1)} copy-done((f32[16,64,256]{2,1,0:T(8,128)S(1)}, f32[16,64,256]{2,1,0:T(8,128)}, u32[]{:S(2)}) %copy-start.1) | copy-done | bytes 1048600
  2.5 1.2 %copy-done.2 = f32[16,64,256]{2,1,0:T(8,128)S(1)} copy-done((f32[16,64,256]{2,1,0:T(8,128)S(1)}, f32[16,64,256]{2,1,0:T(8,128)}, u32[]{:S(2)}) %copy-start.2) | copy-done | bytes 1048600
  4.6 2.1 %collective-permute-start = (f32[11,64,256]{2,1,0:T(8,128)S(1)}, f32[11,64,256]{2,1,0:T(8,128)S(1)}, u32[]{:S(2)}, u32[]{:S(2)}) collective-permute-start(f32[11,64,256]{2,1,0:T(8,128)S(1)} %get-tuple-element.19), channel_id=1, source_target_pairs={{0,16},{16,0},{1,17},{17,1},{2,18},{18,2},{3,19},{19,3},{4,20},{20... | collective-permute-start | bytes 2162696 | tf_op jit(solution)/shard_map/ppermute | solution.py:641
  8.8 2.9 %collective-permute-done.2.refs_4_.refs_7_.refs_6_ = f32[2,64,128]{2,1,0:T(8,128)S(1)} collective-permute-done((f32[2,64,128]{2,1,0:T(8,128)S(1)}, f32[2,64,128]{2,1,0:T(8,128)S(1)}, u32[]{:S(2)}, u32[]{:S(2)}) %collective-permute-start.2) | collective-permute-done | bytes 65568 | tf_op jit(solution)/shard_map/ppermute | solution.py:641
  11.7 1.4 %collective-permute-start.3 = (f32[25,8,256]{2,1,0:T(8,128)S(1)}, f32[25,8,256]{2,1,0:T(8,128)S(1)}, u32[]{:S(2)}, u32[]{:S(2)}) collective-permute-start(f32[25,8,256]{2,1,0:T(8,128)S(1)} %get-tuple-element.22), channel_id=1, source_target_pairs={{0,4},{4,0},{8,12},{12,8},{1,5},{5,1},{9,13},{13,9},{2,6},{6,2},{1... | collective-permute-start | bytes 614408 | tf_op jit(solution)/shard_map/ppermute | solution.py:641
  13.1 2.2 %collective-permute-start.4 = (f32[25,8,256]{2,1,0:T(8,128)S(1)}, f32[25,8,256]{2,1,0:T(8,128)S(1)}, u32[]{:S(2)}, u32[]{:S(2)}) collective-permute-start(f32[25,8,256]{2,1,0:T(8,128)S(1)} %get-tuple-element.23), channel_id=1, source_target_pairs={{4,8},{8,4},{12,0},{0,12},{5,9},{9,5},{13,1},{1,13},{6,10},{10,6},... | collective-permute-start | bytes 614408 | tf_op jit(solution)/shard_map/ppermute | solution.py:641
  15.3 3.4 %collective-permute-done.3.refs_4_.refs_3_ = f32[25,8,256]{2,1,0:T(8,128)S(1)} collective-permute-done((f32[25,8,256]{2,1,0:T(8,128)S(1)}, f32[25,8,256]{2,1,0:T(8,128)S(1)}, u32[]{:S(2)}, u32[]{:S(2)}) %collective-permute-start.3) | collective-permute-done | bytes 204832 | tf_op jit(solution)/shard_map/ppermute | solution.py:641
  18.7 6.5 %collective-permute-done.4.refs_5_.refs_4_ = f32[25,8,256]{2,1,0:T(8,128)S(1)} collective-permute-done((f32[25,8,256]{2,1,0:T(8,128)S(1)}, f32[25,8,256]{2,1,0:T(8,128)S(1)}, u32[]{:S(2)}, u32[]{:S(2)}) %collective-permute-start.4) | collective-permute-done | bytes 204832 | tf_op jit(solution)/shard_map/ppermute | solution.py:641
  25.1 1.7 %restrict.1 = f32[36,8,128]{2,1,0:T(8,128)S(1)} custom-call(f32[16,64,256]{2,1,0:T(8,128)S(1)} %copy-done, f32[16,64,256]{2,1,0:T(8,128)S(1)} %copy-done.1, f32[16,64,256]{2,1,0:T(8,128)S(1)} %copy-done.2, f32[11,64,256]{2,1,0:T(8,128)S(1)} %collective-permute-done.refs_3_, f32[25,8,256]{2,1,0:T(8,128)S(1)} %collective-permute-done.3.refs_4_.refs_3_, ...), custom_call_target="tpu_custom_call" | custom-call | flops 1000 | tf_op jit(solution)/shard_map/restrict/pallas_call | solution.py:44
  27.2 4.4 %collective-permute-done.5.refs_4_ = f32[36,8,128]{2,1,0:T(8,128)S(1)} collective-permute-done((f32[36,8,128]{2,1,0:T(8,128)S(1)}, f32[36,8,128]{2,1,0:T(8,128)S(1)}, u32[]{:S(2)}, u32[]{:S(2)}) %collective-permute-start.5) | collective-permute-done | bytes 147488 | tf_op jit(solution)/shard_map/ppermute | solution.py:641
  31.6 2.7 %collective-permute-done.6 = f32[2,3,8,128]{3,2,1,0:T(8,128)S(1)} collective-permute-done((f32[2,3,8,128]{3,2,1,0:T(8,128)S(1)}, f32[2,3,8,128]{3,2,1,0:T(8,128)S(1)}, u32[]{:S(2)}, u32[]{:S(2)}) %collective-permute-start.6) | collective-permute-done | bytes 24608 | tf_op jit(solution)/shard_map/ppermute | solution.py:687
  34.3 1.2 %collective-permute-start.7 = (f32[4,3,8,128]{3,2,1,0:T(8,128)S(1)}, f32[4,3,8,128]{3,2,1,0:T(8,128)S(1)}, u32[]{:S(2)}, u32[]{:S(2)}) collective-permute-start(f32[4,3,8,128]{3,2,1,0:T(8,128)S(1)} %pad_maximum_fusion.1), channel_id=1, source_target_pairs={{0,8},{4,12},{8,0},{12,4},{1,9},{5,13},{9,1},{13,5},{2,10},{6,14},... | collective-permute-start | bytes 147464 | tf_op jit(solution)/shard_map/ppermute | solution.py:687
  35.5 2.9 %collective-permute-done.7 = f32[4,3,8,128]{3,2,1,0:T(8,128)S(1)} collective-permute-done((f32[4,3,8,128]{3,2,1,0:T(8,128)S(1)}, f32[4,3,8,128]{3,2,1,0:T(8,128)S(1)}, u32[]{:S(2)}, u32[]{:S(2)}) %collective-permute-start.7) | collective-permute-done | bytes 49184 | tf_op jit(solution)/shard_map/ppermute | solution.py:687
  38.4 1.3 %collective-permute-start.8 = (f32[8,3,8,128]{3,2,1,0:T(8,128)S(1)}, f32[8,3,8,128]{3,2,1,0:T(8,128)S(1)}, u32[]{:S(2)}, u32[]{:S(2)}) collective-permute-start(f32[8,3,8,128]{3,2,1,0:T(8,128)S(1)} %pad_maximum_fusion), channel_id=1, source_target_pairs={{0,2},{1,3},{2,0},{3,1},{4,6},{5,7},{6,4},{7,5},{8,10},{9,11},{10,... | collective-permute-start | bytes 294920 | tf_op jit(solution)/shard_map/ppermute | solution.py:691
  39.7 2.2 %collective-permute-done.8 = f32[8,3,8,128]{3,2,1,0:T(8,128)S(1)} collective-permute-done((f32[8,3,8,128]{3,2,1,0:T(8,128)S(1)}, f32[8,3,8,128]{3,2,1,0:T(8,128)S(1)}, u32[]{:S(2)}, u32[]{:S(2)}) %collective-permute-start.8) | collective-permute-done | bytes 98336 | tf_op jit(solution)/shard_map/ppermute | solution.py:691
  42.0 4.9 %collective-permute-start.9 = (f32[16,3,8,128]{3,2,1,0:T(8,128)S(1)}, f32[16,3,8,128]{3,2,1,0:T(8,128)S(1)}, u32[]{:S(2)}, u32[]{:S(2)}) collective-permute-start(f32[16,3,8,128]{3,2,1,0:T(8,128)S(1)} %get-tuple-element.37), channel_id=1, source_target_pairs={{0,1},{1,0},{2,3},{3,2},{4,5},{5,4},{6,7},{7,6},{8,9},{9,8},{10,11... | collective-permute-start | bytes 589832 | tf_op jit(solution)/shard_map/ppermute | solution.py:691
  46.8 1.2 %extend.1 = (f32[16,72,384]{2,1,0:T(8,128)S(1)}, f32[16,72,384]{2,1,0:T(8,128)S(1)}, f32[16,72,384]{2,1,0:T(8,128)S(1)}) custom-call(f32[16,64,256]{2,1,0:T(8,128)S(1)} %copy-done, f32[16,64,256]{2,1,0:T(8,128)S(1)} %copy-done.1, f32[16,64,256]{2,1,0:T(8,128)S(1)} %copy-done.2, f32[25,8,256]{2,1,0:T(8,128)S(1)} %collective-permute-done.3.refs_4_.refs_3_, ...), custom_call_target="tpu_custom_call" | custom-call | flops 1000 | tf_op jit(solution)/shard_map/extend/pallas_call | solution.py:44
  48.0 4.5 %weights.1 = (f32[24,72,384]{2,1,0:T(8,128)S(1)}, f32[24,72,384]{2,1,0:T(8,128)S(1)}, f32[24,72,384]{2,1,0:T(8,128)S(1)}, f32[24,72,384]{2,1,0:T(8,128)S(1)}, f3...) custom-call(f32[16,72,384]{2,1,0:T(8,128)S(1)} %get-tuple-element.24.refs_0_, ...), custom_call_target="tpu_custom_call" | custom-call | flops 1000 | tf_op jit(solution)/shard_map/weights/pallas_call | solution.py:44
  52.6 2.7 %sweep_1.1.refs_0_ = f32[24,72,384]{2,1,0:T(8,128)S(1)} custom-call(f32[24,72,384]{2,1,0:T(8,128)S(1)} %get-tuple-element.27.refs_0_, f32[24,72,384]{2,1,0:T(8,128)S(1)} %get-tuple-element.28.refs_1_, f32[24,72,384]{2,1,0:T(8,128)S(1)} %get-tuple-element.29.refs_2_, f32[24,72,384]{2,1,0:T(8,128)S(1)} %get-tuple-element.30.refs_3_, ...), custom_call_target="tpu_custom_call" | custom-call | flops 1000 | tf_op jit(solution)/shard_map/sweep_1/pallas_call | solution.py:44
  55.2 2.5 %sweep_2.1.refs_0_ = f32[24,72,384]{2,1,0:T(8,128)S(1)} custom-call(f32[24,72,384]{2,1,0:T(8,128)S(1)} %sweep_1.1.refs_0_, f32[24,72,384]{2,1,0:T(8,128)S(1)} %get-tuple-element.28.refs_1_, f32[24,72,384]{2,1,0:T(8,128)S(1)} %get-tuple-element.29.refs_2_, f32[24,72,384]{2,1,0:T(8,128)S(1)} %get-tuple-element.30.refs_3_, ...), custom_call_target="tpu_custom_call" | custom-call | flops 1000 | tf_op jit(solution)/shard_map/sweep_2/pallas_call | solution.py:44
  57.8 2.4 %sweep_3.1.refs_0_ = f32[24,72,384]{2,1,0:T(8,128)S(1)} custom-call(f32[24,72,384]{2,1,0:T(8,128)S(1)} %sweep_2.1.refs_0_, f32[24,72,384]{2,1,0:T(8,128)S(1)} %get-tuple-element.28.refs_1_, f32[24,72,384]{2,1,0:T(8,128)S(1)} %get-tuple-element.29.refs_2_, f32[24,72,384]{2,1,0:T(8,128)S(1)} %get-tuple-element.30.refs_3_, ...), custom_call_target="tpu_custom_call" | custom-call | flops 1000 | tf_op jit(solution)/shard_map/sweep_3/pallas_call | solution.py:44
  60.2 2.0 %sweep_4.1.fine = f32[16,64,256]{2,1,0:T(8,128)S(1)} custom-call(f32[24,72,384]{2,1,0:T(8,128)S(1)} %sweep_3.1.refs_0_, f32[24,72,384]{2,1,0:T(8,128)S(1)} %get-tuple-element.28.refs_1_, f32[24,72,384]{2,1,0:T(8,128)S(1)} %get-tuple-element.29.refs_2_, f32[24,72,384]{2,1,0:T(8,128)S(1)} %get-tuple-element.30.refs_3_, ...), custom_call_target="tpu_custom_call" | custom-call | flops 1000 | tf_op jit(solution)/shard_map/sweep_4/pallas_call | solution.py:44
  62.2 2.1 %solve.1 = f32[16,64,256]{2,1,0:T(8,128)} custom-call(f32[32,3,8,128]{3,2,1,0:T(8,128)S(1)} %constant_dynamic-update-slice_fusion.5.gathered, f32[16,64,256]{2,1,0:T(8,128)S(1)} %sweep_4.1.fine), custom_call_target="tpu_custom_call" | custom-call | flops 1000 | tf_op jit(solution)/shard_map/solve/pallas_call | solution.py:44
  (23 shorter events, 3.5 us)
Async XLA Ops:
  0.0 1.2 %copy-start = (f32[16,64,256]{2,1,0:T(8,128)S(1)}, f32[16,64,256]{2,1,0:T(8,128)}, u32[]{:S(2)}) copy-start(f32[16,64,256]{2,1,0:T(8,128)} %refs_0_.7) | copy-start | bytes 3145732
  1.2 1.2 %copy-start.1 = (f32[16,64,256]{2,1,0:T(8,128)S(1)}, f32[16,64,256]{2,1,0:T(8,128)}, u32[]{:S(2)}) copy-start(f32[16,64,256]{2,1,0:T(8,128)} %refs_1_.7) | copy-start | bytes 3145732
  2.5 1.2 %copy-start.2 = (f32[16,64,256]{2,1,0:T(8,128)S(1)}, f32[16,64,256]{2,1,0:T(8,128)}, u32[]{:S(2)}) copy-start(f32[16,64,256]{2,1,0:T(8,128)} %refs_2_.7) | copy-start | bytes 3145732
  4.6 20.6 %collective-permute-start = (f32[11,64,256]{2,1,0:T(8,128)S(1)}, f32[11,64,256]{2,1,0:T(8,128)S(1)}, u32[]{:S(2)}, u32[]{:S(2)}) collective-permute-start(f32[11,64,256]{2,1,0:T(8,128)S(1)} %get-tuple-element.19), channel_id=1, source_target_pairs={{0,16},{16,0},{1,17},{17,1},{2,18},{18,2},{3,19},{19,3},{4,20},{20... | collective-permute-start | bytes 2162696 | tf_op jit(solution)/shard_map/ppermute | solution.py:641
  6.7 2.1 %collective-permute-start.1 = (f32[2,64,128]{2,1,0:T(8,128)S(1)}, f32[2,64,128]{2,1,0:T(8,128)S(1)}, u32[]{:S(2)}, u32[]{:S(2)}) collective-permute-start(f32[2,64,128]{2,1,0:T(8,128)S(1)} %get-tuple-element.20.refs_8_), channel_id=1, source_target_pairs={{0,1},{1,0},{2,3},{3,2},{4,5},{5,4},{6,7},{7,6},{8,9},{9,8},{10,11... | collective-permute-start | bytes 196616 | tf_op jit(solution)/shard_map/ppermute | solution.py:641
  7.7 4.0 %collective-permute-start.2 = (f32[2,64,128]{2,1,0:T(8,128)S(1)}, f32[2,64,128]{2,1,0:T(8,128)S(1)}, u32[]{:S(2)}, u32[]{:S(2)}) collective-permute-start(f32[2,64,128]{2,1,0:T(8,128)S(1)} %get-tuple-element.21.refs_9_), channel_id=1, source_target_pairs={{1,2},{2,1},{3,0},{0,3},{5,6},{6,5},{7,4},{4,7},{9,10},{10,9},{11,... | collective-permute-start | bytes 196616 | tf_op jit(solution)/shard_map/ppermute | solution.py:641
  11.7 7.0 %collective-permute-start.3 = (f32[25,8,256]{2,1,0:T(8,128)S(1)}, f32[25,8,256]{2,1,0:T(8,128)S(1)}, u32[]{:S(2)}, u32[]{:S(2)}) collective-permute-start(f32[25,8,256]{2,1,0:T(8,128)S(1)} %get-tuple-element.22), channel_id=1, source_target_pairs={{0,4},{4,0},{8,12},{12,8},{1,5},{5,1},{9,13},{13,9},{2,6},{6,2},{1... | collective-permute-start | bytes 614408 | tf_op jit(solution)/shard_map/ppermute | solution.py:641
  13.1 12.1 %collective-permute-start.4 = (f32[25,8,256]{2,1,0:T(8,128)S(1)}, f32[25,8,256]{2,1,0:T(8,128)S(1)}, u32[]{:S(2)}, u32[]{:S(2)}) collective-permute-start(f32[25,8,256]{2,1,0:T(8,128)S(1)} %get-tuple-element.23), channel_id=1, source_target_pairs={{4,8},{8,4},{12,0},{0,12},{5,9},{9,5},{13,1},{1,13},{6,10},{10,6},... | collective-permute-start | bytes 614408 | tf_op jit(solution)/shard_map/ppermute | solution.py:641
  26.8 4.8 %collective-permute-start.5 = (f32[36,8,128]{2,1,0:T(8,128)S(1)}, f32[36,8,128]{2,1,0:T(8,128)S(1)}, u32[]{:S(2)}, u32[]{:S(2)}) collective-permute-start(f32[36,8,128]{2,1,0:T(8,128)S(1)} %restrict.1), channel_id=1, source_target_pairs={{0,16},{16,0},{1,17},{17,1},{2,18},{18,2},{3,19},{19,3},{4,20},{20... | collective-permute-start | bytes 442376 | tf_op jit(solution)/shard_map/ppermute | solution.py:641
  31.6 2.7 %collective-permute-start.6 = (f32[2,3,8,128]{3,2,1,0:T(8,128)S(1)}, f32[2,3,8,128]{3,2,1,0:T(8,128)S(1)}, u32[]{:S(2)}, u32[]{:S(2)}) collective-permute-start(f32[2,3,8,128]{3,2,1,0:T(8,128)S(1)} %pad_maximum_fusion.2), channel_id=1, source_target_pairs={{0,4},{4,0},{8,12},{12,8},{1,5},{5,1},{9,13},{13,9},{2,6},{6,2},{1... | collective-permute-start | bytes 73736 | tf_op jit(solution)/shard_map/ppermute | solution.py:687
  34.3 4.1 %collective-permute-start.7 = (f32[4,3,8,128]{3,2,1,0:T(8,128)S(1)}, f32[4,3,8,128]{3,2,1,0:T(8,128)S(1)}, u32[]{:S(2)}, u32[]{:S(2)}) collective-permute-start(f32[4,3,8,128]{3,2,1,0:T(8,128)S(1)} %pad_maximum_fusion.1), channel_id=1, source_target_pairs={{0,8},{4,12},{8,0},{12,4},{1,9},{5,13},{9,1},{13,5},{2,10},{6,14},... | collective-permute-start | bytes 147464 | tf_op jit(solution)/shard_map/ppermute | solution.py:687
  38.4 3.5 %collective-permute-start.8 = (f32[8,3,8,128]{3,2,1,0:T(8,128)S(1)}, f32[8,3,8,128]{3,2,1,0:T(8,128)S(1)}, u32[]{:S(2)}, u32[]{:S(2)}) collective-permute-start(f32[8,3,8,128]{3,2,1,0:T(8,128)S(1)} %pad_maximum_fusion), channel_id=1, source_target_pairs={{0,2},{1,3},{2,0},{3,1},{4,6},{5,7},{6,4},{7,5},{8,10},{9,11},{10,... | collective-permute-start | bytes 294920 | tf_op jit(solution)/shard_map/ppermute | solution.py:691
  42.0 20.2 %collective-permute-start.9 = (f32[16,3,8,128]{3,2,1,0:T(8,128)S(1)}, f32[16,3,8,128]{3,2,1,0:T(8,128)S(1)}, u32[]{:S(2)}, u32[]{:S(2)}) collective-permute-start(f32[16,3,8,128]{3,2,1,0:T(8,128)S(1)} %get-tuple-element.37), channel_id=1, source_target_pairs={{0,1},{1,0},{2,3},{3,2},{4,5},{5,4},{6,7},{7,6},{8,9},{9,8},{10,11... | collective-permute-start | bytes 589832 | tf_op jit(solution)/shard_map/ppermute | solution.py:691

commit v2 on v1

--- a/solution.py
+++ b/solution.py
@@ -30,6 +30,18 @@
     return out
 
 
+def spread_pairs(outer, inner):
+    out = []
+    for i in range(outer):
+        for j in range(inner):
+            if i in (0, outer - 1):
+                target = i * inner + (j ^ 1)
+            else:
+                target = (i + 1 if i % 2 else i - 1) * inner + j
+            out.append((i * inner + j, target))
+    return out
+
+
 def flips(count, bit):
     return [(i, i ^ bit) for i in range(count)]
 
@@ -38,20 +50,22 @@
     return pltpu.with_memory_space_constraint(value, pltpu.VMEM)
 
 
-def run(kernel, outs, args, scratch=(), flops=1000, name=None, out_spaces=None):
+def run(kernel, outs, args, scratch=(), us=1.0, name=None, spaces=None, far=False, aliases=None):
     whole = pl.BlockSpec(memory_space=pltpu.VMEM)
-    shapes = [pltpu.VMEM(shape, F32) for shape in outs] if out_spaces is None else out_spaces
-    result = pl.pallas_call(
+    shapes = [pltpu.VMEM(shape, F32) for shape in outs] if spaces is None else spaces
+    return pl.pallas_call(
         kernel,
         out_shape=shapes,
-        in_specs=[whole] * len(args),
+        in_specs=[pl.BlockSpec(memory_space=pltpu.HBM) if far else whole] * len(args),
         out_specs=[whole] * len(outs),
         scratch_shapes=list(scratch),
+        input_output_aliases=aliases or {},
         compiler_params=pltpu.CompilerParams(vmem_limit_bytes=VMEM_LIMIT),
-        cost_estimate=pl.CostEstimate(flops=flops, bytes_accessed=0, transcendentals=0),
+        cost_estimate=pl.CostEstimate(
+            flops=1000, bytes_accessed=int(us * 3_500_000), transcendentals=0
+        ),
         name=name,
-    )(*[on_chip(a) for a in args])
-    return result
+    )(*[pltpu.with_memory_space_constraint(a, pltpu.HBM) if far else on_chip(a) for a in args])
 
 
 def lane_of(shape):
@@ -114,6 +128,12 @@
     def where(self):
         return lax.axis_index("gx"), lax.axis_index("gy"), lax.axis_index("gz")
 
+    def steps(self):
+        bits = [("gx", 1 << i) for i in range(1, self.nz.bit_length() - 1)]
+        bits += [("gy", 1 << i) for i in reversed(range(1, self.ny.bit_length() - 1))]
+        bits += [("gz", 1 << i) for i in reversed(range(1, self.nx.bit_length() - 1))]
+        return bits + [("gy", 1), ("gz", 1)]
+
     def slot(self, q, z):
         index = q * self.Z + z
         return index // SLOTS, (index % SLOTS) * DEPTH
@@ -121,34 +141,51 @@
 
 def pack_kernel(g, *refs):
     src = refs[:3]
-    z_out = refs[3 : 3 + g.zsides]
-    x_out = refs[3 + g.zsides :]
+    fields = refs[3:6]
+    n = 6
+    near = refs[n : n + g.zsides]
+    n += g.zsides
+    deep = refs[n : n + g.zsides]
+    n += g.zsides
+    x_out = refs[n : n + g.xsides]
+    sems = refs[n + g.xsides]
     zi, yi, xi = g.where()
-    for side, out in enumerate(z_out):
+    copies = []
+
+    def send(q, at, size, out, place):
+        source = src[q].at[pl.ds(at, size)]
+        target = out.at[pl.ds(place, size)]
+        copies.append(pltpu.make_async_copy(source, target, sems.at[3 + len(copies)]))
+
+    rest = DEPTH - 1
+    for side in range(g.zsides):
         high = (zi % 2) == side
-        at = jnp.where(high, g.Z - DEPTH, 0)
-        out[0:DEPTH] = src[0][pl.ds(at, DEPTH)]
-        out[DEPTH : 2 * DEPTH] = src[1][pl.ds(at, DEPTH)]
-        at = jnp.where(high, g.Z - DEPTH + 1, 0)
-        out[2 * DEPTH :] = src[2][pl.ds(at, DEPTH - 1)]
+        for q in range(2):
+            send(q, jnp.where(high, g.Z - 1, 0), 1, near[side], q)
+        for q in range(3):
+            first = jnp.where(high, g.Z - rest if q == 2 else g.Z - DEPTH, 0 if q == 2 else 1)
+            send(q, first, rest, deep[side], q * rest)
+    loads = [pltpu.make_async_copy(src[q], fields[q], sems.at[q]) for q in range(3)]
+    for copy in loads + copies:
+        copy.start()
     lane = lane_of((g.Y, LANES))
-    packs = []
-    for high in (True, False):
-        acc = [jnp.zeros((g.Y, LANES), F32) for _ in range(g.blocks)]
-        for q in range(3):
-            for z in range(g.Z):
-                block, at = g.slot(q, z)
-                if high:
-                    moved = roll(src[q][z, :, g.X - LANES :], at + DEPTH, 1)
-                else:
-                    moved = roll(src[q][z, :, :LANES], at, 1)
-                acc[block] = jnp.where((lane >= at) & (lane < at + DEPTH), moved, acc[block])
-        packs.append(acc)
+    hi_pack = [jnp.zeros((g.Y, LANES), F32) for _ in range(g.blocks)]
+    lo_pack = list(hi_pack)
+    for q in range(3):
+        loads[q].wait()
+        for z in range(g.Z):
+            block, at = g.slot(q, z)
+            keep = (lane >= at) & (lane < at + DEPTH)
+            moved = roll(fields[q][z, :, g.X - LANES :], at + DEPTH, 1)
+            hi_pack[block] = jnp.where(keep, moved, hi_pack[block])
+            moved = roll(fields[q][z, :, :LANES], at, 1)
+            lo_pack[block] = jnp.where(keep, moved, lo_pack[block])
     even = (xi % 2) == 0
     for block in range(g.blocks):
-        hi, lo = packs[0][block], packs[1][block]
         for side, out in enumerate(x_out):
-            out[block] = jnp.where(even == (side == 0), hi, lo)
+            out[block] = jnp.where(even == (side == 0), hi_pack[block], lo_pack[block])
+    for copy in copies:
+        copy.wait()
 
 
 def pick(first, second, even, inside):
@@ -172,7 +209,7 @@
 def pack_rows_kernel(g, *refs):
     src = refs[:3]
     x_in = refs[3 : 3 + g.xsides]
-    y_out = refs[3 + g.xsides :]
+    y_out = refs[3 + g.xsides + g.zsides :]
     zi, yi, xi = g.where()
     half = g.Z // 2
     last = g.Y - ROWS
@@ -248,13 +285,13 @@
     flux_z, weight_z = [], []
     for layer in range(0, Z + 1, RATIO):
         if layer == 0:
-            p0 = from_low(zi, g.nz, z_in, lambda r: r[DEPTH - 1])
-            k0 = from_low(zi, g.nz, z_in, lambda r: r[2 * DEPTH - 1])
+            p0 = from_low(zi, g.nz, z_in, lambda r: r[0])
+            k0 = from_low(zi, g.nz, z_in, lambda r: r[1])
         else:
             p0, k0 = p[layer - 1], k[layer - 1]
         if layer == Z:
             p1 = from_high(zi, g.nz, z_in, lambda r: r[0])
-            k1 = from_high(zi, g.nz, z_in, lambda r: r[DEPTH])
+            k1 = from_high(zi, g.nz, z_in, lambda r: r[1])
         else:
             p1, k1 = p[layer], k[layer]
         w = face(k0, k1)
@@ -413,6 +450,21 @@
     return 3 * DEPTH * (g.X // LANES) + g.YE // ROWS
 
 
+def strip_tile(g, hi, lo):
+    lane = lane_of((g.YE, LANES))
+    return jnp.where(lane < DEPTH, hi, jnp.where(lane >= LANES - DEPTH, lo, 0.0))
+
+
+def side_faces(kz):
+    wy = face(kz, roll(kz, 1, 0))
+    wx = face(kz, roll(kz, 1, 1))
+    return wy, wx, wy + roll(wy, -1, 0) + wx + roll(wx, -1, 1)
+
+
+def scale_of(kz, total):
+    return jnp.where(kz > 0.0, OMEGA / total, 0.0)
+
+
 def extend_kernel(g, *refs):
     n = 3
     src = refs[:n]
@@ -420,137 +472,194 @@
     n += g.ysides
     x_in = refs[n : n + g.xsides]
     n += g.xsides
-    outs = refs[n : n + 3]
-    hy, ly, xh, xl = refs[n + 3 :]
+    pe, ke, se, fz, fy, fx, dinv, token = refs[n : n + 8]
+    hy, ly, xh, xl = refs[n + 8 :]
+    token[...] = jnp.zeros((ROWS, LANES), F32)
     zi, yi, xi = g.where()
     gather_rows(g, yi, y_in, hy, ly)
     gather_strips(g, xi, x_in, hy, ly, xh, xl)
-    lane = lane_of((g.YE, LANES))
-    for q in range(3):
+    for q, out in enumerate((pe, ke, se)):
         for z in range(g.Z):
-            outs[q][z, : g.Y, : g.X] = src[q][z]
-            outs[q][z, g.Y :, : g.X] = row_halo(g, hy, ly, q, z)
+            out[z, : g.Y, : g.X] = src[q][z]
+            out[z, g.Y :, : g.X] = row_halo(g, hy, ly, q, z)
             block, at = g.slot(q, z)
             hi = roll(xh[block], -at, 1)
             lo = roll(xl[block], -at - DEPTH, 1)
-            outs[q][z, :, g.X :] = jnp.where(
-                lane < DEPTH, hi, jnp.where(lane >= LANES - DEPTH, lo, 0.0)
-            )
-
-
-def sweep_range(g, zi, sweep):
-    reach = SWEEPS - sweep
-    low = jnp.where(zi > 0, DEPTH - reach, DEPTH)
-    high = jnp.where(zi < g.nz - 1, DEPTH + g.Z + reach, DEPTH + g.Z)
-    return low, high
-
-
-def weights_kernel(g, *refs):
-    own = refs[:3]
-    n = 3
-    z_in = refs[n : n + g.zsides]
-    n += g.zsides
-    relay = refs[n : n + g.zsides]
-    n += g.zsides
-    pe, se, fz, fy, fx, dinv = refs[n : n + 6]
-    ke = refs[n + 6]
-    zi, yi, xi = g.where()
-    Z, Y, X = g.Z, g.Y, g.X
-    ext = (pe, ke, se)
-    for q in range(3):
-        ext[q][DEPTH : DEPTH + Z] = own[q][...]
-    zero = jnp.zeros((g.YE, g.XE), F32)
-    lane = lane_of((g.YE, LANES))
-    for side in range(g.zsides):
-        base = coarse_blocks(g) if side == 0 else 0
-        above = (zi % 2) == side
-
-        def fill(top, side=side, base=base):
-            first = DEPTH + Z if top else 0
-            for q in range(3):
-                for d in range(DEPTH):
-                    if q < 2:
-                        at = q * DEPTH + d
-                    else:
-                        at = 2 * DEPTH + (d if top else d - 1)
-                        if (top and d == DEPTH - 1) or (not top and d == 0):
-                            ext[q][first + d] = zero
-                            continue
-                    ext[q][first + d, :Y, :X] = z_in[side][at]
-                    for part in range(X // LANES):
-                        ext[q][first + d, Y:, part * LANES : (part + 1) * LANES] = relay[side][
-                            base + (q * DEPTH + d) * (X // LANES) + part
-                        ]
-                    strip = relay[side][base + 3 * DEPTH * (X // LANES) :].reshape(g.YE, LANES)
-                    at_hi = (q * DEPTH + d) * DEPTH
-                    at_lo = ((3 + q) * DEPTH + d) * DEPTH
-                    hi = roll(strip, -at_hi, 1)
-                    lo = roll(strip, -at_lo - DEPTH, 1)
-                    ext[q][first + d, :, X:] = jnp.where(
-                        lane < DEPTH, hi, jnp.where(lane >= LANES - DEPTH, lo, 0.0)
-                    )
-
-        pl.when(above & (zi < g.nz - 1))(functools.partial(fill, True))
-        pl.when(jnp.logical_not(above) & (zi > 0))(functools.partial(fill, False))
-
-    @pl.when(zi == 0)
-    def _():
-        pe[DEPTH - 1] = zero
-        ke[DEPTH - 1] = zero
-
-    @pl.when(zi == g.nz - 1)
-    def _():
-        pe[DEPTH + Z] = zero
-        ke[DEPTH + Z] = zero
-
-    low, high = sweep_range(g, zi, 1)
-    fz[low] = face(ke[low], ke[low - 1])
+            out[z, :, g.X :] = strip_tile(g, hi, lo)
+    fy[0], fx[0], _ = side_faces(ke[0])
+    fz[1] = face(ke[1], ke[0])
 
     def body(z, carry):
         kz = ke[z]
         above = face(ke[z + 1], kz)
         fz[z + 1] = above
-        wy = face(kz, roll(kz, 1, 0))
-        wx = face(kz, roll(kz, 1, 1))
+        wy, wx, total = side_faces(kz)
         fy[z] = wy
         fx[z] = wx
-        total = fz[z] + above + wy + roll(wy, -1, 0) + wx + roll(wx, -1, 1)
-        dinv[z] = jnp.where(kz > 0.0, OMEGA / total, 0.0)
+        dinv[z] = scale_of(kz, total + fz[z] + above)
         return carry
 
-    lax.fori_loop(low, high, body, 0)
+    lax.fori_loop(1, g.Z - 1, body, 0)
+    fy[g.Z - 1], fx[g.Z - 1], _ = side_faces(ke[g.Z - 1])
+
+
+def halo_kernel(g, *refs):
+    ke, fy, fx, fz = refs[:4]
+    n = 4
+    near = refs[n : n + g.zsides]
+    n += g.zsides
+    deep = refs[n : n + g.zsides]
+    n += g.zsides
+    relay = refs[n : n + g.zsides]
+    n += g.zsides
+    ph, sh, hz, hy, hx, hd = refs[n : n + 6]
+    kh = refs[n + 6]
+    zi, yi, xi = g.where()
+    Z, Y, X = g.Z, g.Y, g.X
+    parts = X // LANES
+    zero = jnp.zeros((g.YE, g.XE), F32)
+
+    def k_at(z):
+        return ke[z] if 0 <= z < Z else kh[z + DEPTH if z < 0 else z - Z + DEPTH]
+
+    def own_faces(z):
+        wy, wx = fy[z], fx[z]
+        return wy + roll(wy, -1, 0) + wx + roll(wx, -1, 1)
+
+    def fill(top, side):
+        base = coarse_blocks(g) if side == 0 else 0
+        first = DEPTH if top else 0
+        strip = relay[side][base + 3 * DEPTH * parts :].reshape(g.YE, LANES)
+        for q, out in enumerate((ph, kh, sh)):
+            for d in range(DEPTH):
+                rest = DEPTH - 1
+                if q < 2 and d == (0 if top else rest):
+                    plane = near[side][q]
+                elif q < 2:
+                    plane = deep[side][q * rest + (d - 1 if top else d)]
+                elif d == (rest if top else 0):
+                    continue
+                else:
+                    plane = deep[side][q * rest + (d if top else d - 1)]
+                out[first + d, :Y, :X] = plane
+                for part in range(parts):
+                    lanes = slice(part * LANES, (part + 1) * LANES)
+                    out[first + d, Y:, lanes] = relay[side][base + (q * DEPTH + d) * parts + part]
+                hi = roll(strip, -(q * DEPTH + d) * DEPTH, 1)
+                lo = roll(strip, -((3 + q) * DEPTH + d) * DEPTH - DEPTH, 1)
+                out[first + d, :, X:] = strip_tile(g, hi, lo)
+        if top:
+            layers = range(Z, Z + DEPTH - 1)
+            kz = k_at(Z - 1)
+            below = face(k_at(Z), kz)
+            hz[DEPTH] = below
+            hd[DEPTH] = scale_of(kz, own_faces(Z - 1) + fz[Z - 1] + below)
+            for z in layers:
+                kz = k_at(z)
+                above = face(k_at(z + 1), kz)
+                hz[z + 1 - Z + DEPTH] = above
+                wy, wx, total = side_faces(kz)
+                hy[z - Z + DEPTH] = wy
+                hx[z - Z + DEPTH] = wx
+                hd[z + 1 - Z + DEPTH] = scale_of(kz, total + below + above)
+                below = above
+        else:
+            kz = k_at(0)
+            above = face(kz, k_at(-1))
+            hz[DEPTH - 1] = above
+            hd[DEPTH - 1] = scale_of(kz, own_faces(0) + fz[1] + above)
+            for z in range(-1, -DEPTH, -1):
+                kz = k_at(z)
+                below = face(kz, k_at(z - 1))
+                hz[z + DEPTH - 1] = below
+                wy, wx, total = side_faces(kz)
+                hy[z + DEPTH] = wy
+                hx[z + DEPTH] = wx
+                hd[z + DEPTH - 1] = scale_of(kz, total + below + above)
+                above = below
+
+    for side in range(g.zsides):
+        above = (zi % 2) == side
+        pl.when(above & (zi < g.nz - 1))(functools.partial(fill, True, side))
+        pl.when(jnp.logical_not(above) & (zi > 0))(functools.partial(fill, False, side))
+
+    @pl.when(zi == 0)
+    def _():
+        ph[DEPTH - 1] = zero
+        kz = ke[0]
+        hz[DEPTH - 1] = kz
+        hd[DEPTH - 1] = scale_of(kz, own_faces(0) + fz[1] + kz)
+
+    @pl.when(zi == g.nz - 1)
+    def _():
+        ph[DEPTH] = zero
+        kz = ke[Z - 1]
+        hz[DEPTH] = kz
+        hd[DEPTH] = scale_of(kz, own_faces(Z - 1) + fz[Z - 1] + kz)
 
 
 def sweep_kernel(g, sweep, *refs):
-    v, s, fz, fy, fx, dinv, out = refs
+    v, vh, s, fz, fy, fx, dinv, sh, hz, hy, hx, hd = refs[:12]
+    out = refs[12]
+    refs[-1][...] = jnp.zeros((ROWS, LANES), F32)
+    out_halo = refs[13]
     zi, yi, xi = g.where()
+    Z = g.Z
     final = sweep == SWEEPS
-    low, high = sweep_range(g, zi, sweep)
-
-    def body(z, carry):
-        vz = v[z]
-        wy, wx = fy[z], fx[z]
-        total = s[z] + fz[z] * v[z - 1] + fz[z + 1] * v[z + 1]
+    reach = SWEEPS - sweep
+
+    def update(vz, low, high, source, z_low, z_high, wy, wx, scale):
+        total = source + z_low * low + z_high * high
         total = total + wy * roll(vz, 1, 0) + roll(wy * vz, -1, 0)
         total = total + wx * roll(vz, 1, 1) + roll(wx * vz, -1, 1)
-        new = (1.0 - OMEGA) * vz + dinv[z] * total
-        if final:
-            out[z - DEPTH] = new[: g.Y, : g.X]
-        else:
-            out[z] = new
+        return (1.0 - OMEGA) * vz + scale * total
+
+    def store(z, new):
+        out[z] = new[: g.Y, : g.X] if final else new
+
+    def pick_layer(own, halo, z):
+        return own[z] if 0 <= z < Z else halo[z + DEPTH if z < 0 else z - Z + DEPTH]
+
+    def z_face(z):
+        return fz[z] if 1 <= z < Z else hz[z + DEPTH - 1 if z < 1 else z - Z + DEPTH]
+
+    def edge(z):
+        scale = dinv[z] if 0 < z < Z - 1 else hd[z + DEPTH - 1 if z < 1 else z - Z + 1 + DEPTH]
+        return update(
+            pick_layer(v, vh, z),
+            pick_layer(v, vh, z - 1),
+            pick_layer(v, vh, z + 1),
+            pick_layer(s, sh, z),
+            z_face(z),
+            z_face(z + 1),
+            pick_layer(fy, hy, z),
+            pick_layer(fx, hx, z),
+            scale,
+        )
+
+    store(0, edge(0))
+
+    def body(z, carry):
+        store(z, update(v[z], v[z - 1], v[z + 1], s[z], fz[z], fz[z + 1], fy[z], fx[z], dinv[z]))
         return carry
 
-    lax.fori_loop(low, high, body, 0)
-    if not final:
-        zero = jnp.zeros((g.YE, g.XE), F32)
-
-        @pl.when(zi == 0)
-        def _():
-            out[DEPTH - 1] = zero
-
-        @pl.when(zi == g.nz - 1)
-        def _():
-            out[DEPTH + g.Z] = zero
+    lax.fori_loop(1, Z - 1, body, 0)
+    store(Z - 1, edge(Z - 1))
+    if final:
+        return
+    zero = jnp.zeros((g.YE, g.XE), F32)
+
+    def halo(layers):
+        for z in layers:
+            out_halo[z + DEPTH if z < 0 else z - Z + DEPTH] = edge(z)
+
+    def outside(at):
+        out_halo[at] = zero
+
+    pl.when(zi > 0)(functools.partial(halo, range(-reach, 0)))
+    pl.when(zi < g.nz - 1)(functools.partial(halo, range(Z, Z + reach)))
+    pl.when(zi == 0)(functools.partial(outside, DEPTH - 1))
+    pl.when(zi == g.nz - 1)(functools.partial(outside, DEPTH))
 
 
 def solve_kernel(g, gathered, fine, out):
@@ -558,14 +667,18 @@
     per = LANES // g.cx
     group = lane_of((ROWS, LANES)) // g.cx
 
+    order = [("gx", 1)] + g.steps()
+
     def relative(a, b, c):
-        d = jnp.bitwise_xor(a, zi) + g.nz * jnp.bitwise_xor(b, yi)
-        e = jnp.bitwise_xor(c, xi)
-        rev = 0
-        bits = g.nx.bit_length() - 1
-        for bit in range(bits):
-            rev = rev + ((e >> bit) & 1) * (1 << (bits - 1 - bit))
-        return d + g.nz * g.ny * rev
+        apart = {
+            "gx": jnp.bitwise_xor(a, zi),
+            "gy": jnp.bitwise_xor(b, yi),
+            "gz": jnp.bitwise_xor(c, xi),
+        }
+        at = 0
+        for number, (axis, bit) in enumerate(order):
+            at = at + (1 << number) * ((apart[axis] & bit) // bit)
+        return at
 
     layers = g.nz * g.cz
     height = g.ny * g.cy
@@ -637,30 +750,56 @@
             out[z] = fine[z] + spread
 
 
-def exchange(bufs, axis, count):
-    return [lax.ppermute(b, axis, pairs(count, odd)) for odd, b in enumerate(bufs)]
+def merge_kernel(cells, got, token, out):
+    count = cells.shape[0]
+    out[:count] = cells[...]
+    out[count:] = got[...]
+
+
+def merge(cells, got, token):
+    shape = (2 * cells.shape[0],) + cells.shape[1:]
+    (out,) = run(merge_kernel, [shape], [cells, got, token], us=0.05, name="merge")
+    return out
+
+
+def exchange(bufs, axis, count, beside=None):
+    got = [lax.ppermute(bufs[0], axis, pairs(count, 0))]
+    if len(bufs) > 1:
+        if beside is None:
+            got.append(lax.ppermute(bufs[1], axis, pairs(count, 1)))
+        else:
+            perm = spread_pairs(count, lax.axis_size(beside))
+            got.append(lax.ppermute(bufs[1], (axis, beside), perm))
+    return got
 
 
 def shards(pressure_start, source, permeability):
     g = Grid(pressure_start.shape)
     Z, Y, X = g.Z, g.Y, g.X
-    fields = [on_chip(a) for a in (pressure_start, permeability, source)]
-    z_shape = (3 * DEPTH - 1, Y, X)
+    fields = [pressure_start, permeability, source]
     x_shape = (g.blocks, Y, LANES)
     y_shape = (3 * Z // 2 + 1, ROWS, X)
     sent = run(
         functools.partial(pack_kernel, g),
-        [z_shape] * g.zsides + [x_shape] * g.xsides,
+        [(Z, Y, X)] * 3
+        + [(2, Y, X)] * g.zsides
+        + [(3 * (DEPTH - 1), Y, X)] * g.zsides
+        + [x_shape] * g.xsides,
         fields,
+        scratch=[pltpu.SemaphoreType.DMA((3 + 5 * g.zsides,))],
         name="pack_faces",
+        far=True,
     )
-    z_sent, x_sent = sent[: g.zsides], sent[g.zsides :]
-    z_got = exchange(z_sent, "gx", g.nz)
+    sent = list(sent)
+    fields, near, deep = sent[:3], sent[3 : 3 + g.zsides], sent[3 + g.zsides : 3 + 2 * g.zsides]
+    x_sent = sent[3 + 2 * g.zsides :]
+    near_got = exchange(near, "gx", g.nz, "gz")
     x_got = exchange(x_sent, "gz", g.nx)
+    deep_got = exchange(deep, "gx", g.nz, "gz")
     y_sent = run(
-        functools.partial(pack_rows_kernel, g), [y_shape] * g.ysides, fields + x_got, name="pack_rows"
+        functools.partial(pack_rows_kernel, g), [y_shape] * g.ysides, fields + x_got + near_got, name="pack_rows"
     )
-    y_got = exchange(y_sent, "gy", g.ny)
+    y_got = exchange(y_sent, "gy", g.ny, "gz")
 
     halo_scratch = [
         pltpu.VMEM(y_shape, F32),
@@ -672,56 +811,56 @@
     packed = run(
         functools.partial(restrict_kernel, g),
         [(nc + nr, ROWS, LANES)] + [(nr, ROWS, LANES)] * (g.zsides - 1),
-        fields + z_got + y_got + x_got + list(x_sent),
+        fields + near_got + y_got + x_got + x_sent,
         scratch=halo_scratch,
         name="restrict",
     )
-    relay = exchange(packed, "gx", g.nz)
-    cells = jnp.stack([packed[0][:nc], relay[0][:nc]])
-    bit = 2
-    while bit < g.nz:
-        cells = jnp.concatenate([cells, lax.ppermute(cells, "gx", flips(g.nz, bit))])
-        bit *= 2
-    bit = 1
-    while bit < g.ny:
-        cells = jnp.concatenate([cells, lax.ppermute(cells, "gy", flips(g.ny, bit))])
-        bit *= 2
-    bit = g.nx // 2
-    while bit >= 1:
-        cells = jnp.concatenate([cells, lax.ppermute(cells, "gz", flips(g.nx, bit))])
-        bit //= 2
-
+    relay = exchange(packed, "gx", g.nz, "gz")
+    tile = (ROWS, LANES)
     own = (Z, g.YE, g.XE)
-    ext = (g.ZE, g.YE, g.XE)
-    extended = run(
+    far = (2 * DEPTH, g.YE, g.XE)
+    pe, ke, se, fz, fy, fx, dinv, token = run(
         functools.partial(extend_kernel, g),
-        [own] * 3,
+        [own] * 7 + [tile],
         fields + y_got + x_got,
         scratch=halo_scratch,
+        us=0.5,
         name="extend",
     )
-    pe, se, fz, fy, fx, dinv = run(
-        functools.partial(weights_kernel, g),
-        [ext] * 6,
-        list(extended) + z_got + relay,
-        scratch=[pltpu.VMEM(ext, F32)],
-        name="weights",
+    ph, sh, hz, hy, hx, hd = run(
+        functools.partial(halo_kernel, g),
+        [far] * 6,
+        [ke, fy, fx, fz] + near_got + deep_got + relay,
+        scratch=[pltpu.VMEM(far, F32)],
+        us=0.1,
+        name="halo",
     )
-    v = pe
-    for sweep in range(1, SWEEPS + 1):
-        shape = (Z, Y, X) if sweep == SWEEPS else ext
-        (v,) = run(
-            functools.partial(sweep_kernel, g, sweep),
-            [shape],
-            [v, se, fz, fy, fx, dinv],
-            name=f"sweep_{sweep}",
-        )
+    cells = merge(packed[0][None, :nc], relay[0][None, :nc], token)
+    v, vh = pe, ph
+    steps = g.steps()
+    for number in range(max(len(steps), SWEEPS)):
+        if number < len(steps):
+            axis, bit = steps[number]
+            got = lax.ppermute(cells, axis, flips(lax.axis_size(axis), bit))
+        if number < SWEEPS:
+            final = number == SWEEPS - 1
+            result = run(
+                functools.partial(sweep_kernel, g, number + 1),
+                ([(Z, Y, X)] if final else [own, far]) + [tile],
+                [v, vh, se, fz, fy, fx, dinv, sh, hz, hy, hx, hd],
+                us=0.5,
+                name=f"sweep_{number + 1}",
+            )
+            v, vh, token = result[0], result[1], result[-1]
+        if number < len(steps):
+            cells = merge(cells, got, token)
     (out,) = run(
         functools.partial(solve_kernel, g),
         [(Z, Y, X)],
         [cells, v],
+        us=2.0,
         name="solve",
-        out_spaces=[jax.ShapeDtypeStruct((Z, Y, X), F32)],
+        spaces=[jax.ShapeDtypeStruct((Z, Y, X), F32)],
     )
     return out
 

time: 64.6 us -> 48.8 us (0.76)
  waiting for transfers between devices: 24.9 us -> 13.6 us
  local copies, waits for them, and re-layouts: 3.73 us -> 0.01 us
  starting transfers between devices: 15.5 us -> 14 us
  Pallas kernels: 20 us -> 21 us
    ppermute x10 -> x11, waiting for transfers between devices: 24.9 us -> 13.6 us  [the longest x5 10.6 us: exchange(): got = [lax.ppermute(bufs[0], axis, pairs(count, 0))]]
    unnamed x10 -> x0, local copies, waits for them, and re-layouts: 3.69 us -> none
    ppermute x10 -> x11, starting transfers between devices: 15.5 us -> 14 us  [the longest x4 6.81 us: shards(): got = lax.ppermute(cells, axis, flips(lax.axis_size(axis), bit))]
    pallas_call x10 -> x15, Pallas kernels: 20 us -> 21 us  [run(): pl.pallas_call(kernel, out_shape=shapes, in_specs=[pl.BlockSpec(memory_sp...]
  transfers between devices with their start and end apart: 10 -> 11, of which waited for: 7 -> 4; matrix products, arithmetic and copies ran while one was open for 0% -> 0% of each run, Pallas kernels for 24% -> 34%
where the time goes in v2:
time: 48.8 us; the launch traced here: 48.7 us
  Pallas kernels  21 us (43%)
  starting transfers between devices  14 us (29%)
  waiting for transfers between devices  13.6 us (28%)
    pallas_call x15, Pallas kernels, run(): pl.pallas_call(kernel, out_shape=shapes, in_specs=[pl.BlockSpec(memory_sp...  21 us
    ppermute x5, waiting for transfers between devices, exchange(): got = [lax.ppermute(bufs[0], axis, pairs(count, 0))]  10.6 us
    ppermute x4, starting transfers between devices, shards(): got = lax.ppermute(cells, axis, flips(lax.axis_size(axis), bit))  6.81 us
    ppermute x5, starting transfers between devices, exchange(): got = [lax.ppermute(bufs[0], axis, pairs(count, 0))]  5.73 us
    ppermute x1, waiting for transfers between devices, exchange(): got.append(lax.ppermute(bufs[1], axis, pairs(count, 1)))  2.58 us
    ppermute x1, starting transfers between devices, exchange(): got.append(lax.ppermute(bufs[1], axis, pairs(count, 1)))  1.13 us
  transfers between devices with their start and end apart: 11, of which 4 were waited for; matrix products, arithmetic and copies ran while one was open for 0% of the time, Pallas kernels for 34%

profile of v2, /device:TPU:1, one launch (start us, length us, event | category | flops | bytes accessed | tf_op | source)
XLA Modules:
  0.0 48.7 jit_solution(17249208616220824806)
XLA Ops:
  0.0 2.3 %pack_faces.1 = (f32[16,64,256]{2,1,0:T(8,128)S(1)}, f32[16,64,256]{2,1,0:T(8,128)S(1)}, f32[16,64,256]{2,1,0:T(8,128)S(1)}, f32[2,64,256]{2,1,0:T(8,128)S(1)}, ...) custom-call(f32[16,64,256]{2,1,0:T(8,128)} %refs_0_.1, f32[16,64,256]{2,1,0:T(8,128)} %refs_1_.1, ...), custom_call_target="tpu_custom_call" | custom-call | flops 1000 | bytes 3500000 | tf_op jit(solution)/shard_map/pack_faces/pallas_call | solution.py:56
  2.3 2.1 %collective-permute-start = (f32[2,64,256]{2,1,0:T(8,128)S(1)}, f32[2,64,256]{2,1,0:T(8,128)S(1)}, u32[]{:S(2)}, u32[]{:S(2)}) collective-permute-start(f32[2,64,256]{2,1,0:T(8,128)S(1)} %get-tuple-element.42), channel_id=1, source_target_pairs={{0,16},{16,0},{1,17},{17,1},{2,18},{18,2},{3,19},{19,3},{4,20},{20... | collective-permute-start | bytes 393224 | tf_op jit(solution)/shard_map/ppermute | solution.py:766
  4.4 1.0 %collective-permute-start.1 = (f32[2,64,128]{2,1,0:T(8,128)S(1)}, f32[2,64,128]{2,1,0:T(8,128)S(1)}, u32[]{:S(2)}, u32[]{:S(2)}) collective-permute-start(f32[2,64,128]{2,1,0:T(8,128)S(1)} %get-tuple-element.43.refs_8_), channel_id=1, source_target_pairs={{0,1},{1,0},{2,3},{3,2},{4,5},{5,4},{6,7},{7,6},{8,9},{9,8},{10,11... | collective-permute-start | bytes 196616 | tf_op jit(solution)/shard_map/ppermute | solution.py:766
  5.4 1.1 %collective-permute-start.2 = (f32[2,64,128]{2,1,0:T(8,128)S(1)}, f32[2,64,128]{2,1,0:T(8,128)S(1)}, u32[]{:S(2)}, u32[]{:S(2)}) collective-permute-start(f32[2,64,128]{2,1,0:T(8,128)S(1)} %get-tuple-element.44.refs_9_), channel_id=1, source_target_pairs={{1,2},{2,1},{3,0},{0,3},{5,6},{6,5},{7,4},{4,7},{9,10},{10,9},{11,... | collective-permute-start | bytes 196616 | tf_op jit(solution)/shard_map/ppermute | solution.py:769
  6.5 2.6 %collective-permute-done.2.refs_4_.refs_7_.refs_6_ = f32[2,64,128]{2,1,0:T(8,128)S(1)} collective-permute-done((f32[2,64,128]{2,1,0:T(8,128)S(1)}, f32[2,64,128]{2,1,0:T(8,128)S(1)}, u32[]{:S(2)}, u32[]{:S(2)}) %collective-permute-start.2) | collective-permute-done | bytes 65568 | tf_op jit(solution)/shard_map/ppermute | solution.py:769
  9.2 1.4 %collective-permute-start.3 = (f32[25,8,256]{2,1,0:T(8,128)S(1)}, f32[25,8,256]{2,1,0:T(8,128)S(1)}, u32[]{:S(2)}, u32[]{:S(2)}) collective-permute-start(f32[25,8,256]{2,1,0:T(8,128)S(1)} %get-tuple-element.45), channel_id=1, source_target_pairs={{0,4},{4,0},{8,12},{12,8},{1,5},{5,1},{9,13},{13,9},{2,6},{6,2},{1... | collective-permute-start | bytes 614408 | tf_op jit(solution)/shard_map/ppermute | solution.py:766
  10.5 0.3 collective-permute-start.4
  10.9 1.2 %collective-permute-start.7 = (f32[9,64,256]{2,1,0:T(8,128)S(1)}, f32[9,64,256]{2,1,0:T(8,128)S(1)}, u32[]{:S(2)}, u32[]{:S(2)}) collective-permute-start(f32[9,64,256]{2,1,0:T(8,128)S(1)} %get-tuple-element.53), channel_id=1, source_target_pairs={{0,16},{16,0},{1,17},{17,1},{2,18},{18,2},{3,19},{19,3},{4,20},{20... | collective-permute-start | bytes 1769480 | tf_op jit(solution)/shard_map/ppermute | solution.py:766
  12.1 3.8 %collective-permute-done.3.refs_4_.refs_3_ = f32[25,8,256]{2,1,0:T(8,128)S(1)} collective-permute-done((f32[25,8,256]{2,1,0:T(8,128)S(1)}, f32[25,8,256]{2,1,0:T(8,128)S(1)}, u32[]{:S(2)}, u32[]{:S(2)}) %collective-permute-start.3) | collective-permute-done | bytes 204832 | tf_op jit(solution)/shard_map/ppermute | solution.py:766
  15.9 1.7 %restrict.1 = f32[36,8,128]{2,1,0:T(8,128)S(1)} custom-call(f32[16,64,256]{2,1,0:T(8,128)S(1)} %get-tuple-element.39.refs_0_, f32[16,64,256]{2,1,0:T(8,128)S(1)} %get-tuple-element.40.refs_1_, f32[16,64,256]{2,1,0:T(8,128)S(1)} %get-tuple-element.41.refs_2_, f32[2,64,256]{2,1,0:T(8,128)S(1)} %collective-permute-done.refs_5_.refs_3_.refs_4_, ...), custom_call_target="tpu_custom_call" | custom-call | flops 1000 | bytes 3500000 | tf_op jit(solution)/shard_map/restrict/pallas_call | solution.py:56
  17.7 0.1 collective-permute-start.5
  17.7 4.3 %extend.1 = (f32[16,72,384]{2,1,0:T(8,128)S(1)}, f32[16,72,384]{2,1,0:T(8,128)S(1)}, f32[16,72,384]{2,1,0:T(8,128)S(1)}, f32[16,72,384]{2,1,0:T(8,128)S(1)}, f32...) custom-call(f32[16,64,256]{2,1,0:T(8,128)S(1)} %get-tuple-element.39.re, ...), custom_call_target="tpu_custom_call" | custom-call | flops 1000 | bytes 1750000 | tf_op jit(solution)/shard_map/extend/pallas_call | solution.py:56
  22.1 6.7 %collective-permute-done.5.refs_6_ = f32[36,8,128]{2,1,0:T(8,128)S(1)} collective-permute-done((f32[36,8,128]{2,1,0:T(8,128)S(1)}, f32[36,8,128]{2,1,0:T(8,128)S(1)}, u32[]{:S(2)}, u32[]{:S(2)}) %collective-permute-start.5) | collective-permute-done | bytes 147488 | tf_op jit(solution)/shard_map/ppermute | solution.py:766
  28.8 1.8 %collective-permute-start.6 = (f32[2,3,8,128]{3,2,1,0:T(8,128)S(1)}, f32[2,3,8,128]{3,2,1,0:T(8,128)S(1)}, u32[]{:S(2)}, u32[]{:S(2)}) collective-permute-start(f32[2,3,8,128]{3,2,1,0:T(8,128)S(1)} %merge.5.cells), channel_id=1, source_target_pairs={{0,8},{4,12},{8,0},{12,4},{1,9},{5,13},{9,1},{13,5},{2,10},{6,14},... | collective-permute-start | bytes 73736 | tf_op jit(solution)/shard_map/ppermute | solution.py:844
  30.6 0.8 %halo.1 = (f32[8,72,384]{2,1,0:T(8,128)S(1)}, f32[8,72,384]{2,1,0:T(8,128)S(1)}, f32[8,72,384]{2,1,0:T(8,128)S(1)}, f32[8,72,384]{2,1,0:T(8,128)S(1)}, f32[8,72,...) custom-call(f32[16,72,384]{2,1,0:T(8,128)S(1)} %get-tuple-element.49.refs_0_, ...), custom_call_target="tpu_custom_call" | custom-call | flops 1000 | bytes 350000 | tf_op jit(solution)/shard_map/halo/pallas_call | solution.py:56
  31.4 2.6 %sweep_1.1 = (f32[16,72,384]{2,1,0:T(8,128)S(1)}, f32[8,72,384]{2,1,0:T(8,128)S(1)}, f32[8,128]{1,0:T(8,128)S(1)}) custom-call(f32[16,72,384]{2,1,0:T(8,128)S(1)} %get-tuple-element.48.refs_0_, f32[8,72,384]{2,1,0:T(8,128)S(1)} %get-tuple-element.54.refs_1_, f32[16,72,384]{2,1,0:T(8,128)S(1)} %get-tuple-element.55.refs_2_, ...), custom_call_target="tpu_custom_call" | custom-call | flops 1000 | bytes 1750000 | tf_op jit(solution)/shard_map/sweep_1/pallas_call | solution.py:56
  34.1 1.3 %collective-permute-start.8 = (f32[4,3,8,128]{3,2,1,0:T(8,128)S(1)}, f32[4,3,8,128]{3,2,1,0:T(8,128)S(1)}, u32[]{:S(2)}, u32[]{:S(2)}) collective-permute-start(f32[4,3,8,128]{3,2,1,0:T(8,128)S(1)} %merge.6.cells), channel_id=1, source_target_pairs={{0,2},{1,3},{2,0},{3,1},{4,6},{5,7},{6,4},{7,5},{8,10},{9,11},{10,... | collective-permute-start | bytes 147464 | tf_op jit(solution)/shard_map/ppermute | solution.py:844
  35.4 2.5 %sweep_2.1 = (f32[16,72,384]{2,1,0:T(8,128)S(1)}, f32[8,72,384]{2,1,0:T(8,128)S(1)}, f32[8,128]{1,0:T(8,128)S(1)}) custom-call(f32[16,72,384]{2,1,0:T(8,128)S(1)} %get-tuple-element.63.refs_0_, f32[8,72,384]{2,1,0:T(8,128)S(1)} %get-tuple-element.64.refs_1_, f32[16,72,384]{2,1,0:T(8,128)S(1)} %get-tuple-element.55.refs_2_, ...), custom_call_target="tpu_custom_call" | custom-call | flops 1000 | bytes 1750000 | tf_op jit(solution)/shard_map/sweep_2/pallas_call | solution.py:56
  37.9 0.7 %collective-permute-start.9 = (f32[8,3,8,128]{3,2,1,0:T(8,128)S(1)}, f32[8,3,8,128]{3,2,1,0:T(8,128)S(1)}, u32[]{:S(2)}, u32[]{:S(2)}) collective-permute-start(f32[8,3,8,128]{3,2,1,0:T(8,128)S(1)} %merge.7.cells), channel_id=1, source_target_pairs={{0,4},{4,0},{8,12},{12,8},{1,5},{5,1},{9,13},{13,9},{2,6},{6,2},{1... | collective-permute-start | bytes 294920 | tf_op jit(solution)/shard_map/ppermute | solution.py:844
  38.6 2.4 %sweep_3.1 = (f32[16,72,384]{2,1,0:T(8,128)S(1)}, f32[8,72,384]{2,1,0:T(8,128)S(1)}, f32[8,128]{1,0:T(8,128)S(1)}) custom-call(f32[16,72,384]{2,1,0:T(8,128)S(1)} %get-tuple-element.66.refs_0_, f32[8,72,384]{2,1,0:T(8,128)S(1)} %get-tuple-element.67.refs_1_, f32[16,72,384]{2,1,0:T(8,128)S(1)} %get-tuple-element.55.refs_2_, ...), custom_call_target="tpu_custom_call" | custom-call | flops 1000 | bytes 1750000 | tf_op jit(solution)/shard_map/sweep_3/pallas_call | solution.py:56
  41.0 0.4 collective-permute-done.9.got
  41.5 3.0 %collective-permute-start.10 = (f32[16,3,8,128]{3,2,1,0:T(8,128)S(1)}, f32[16,3,8,128]{3,2,1,0:T(8,128)S(1)}, u32[]{:S(2)}, u32[]{:S(2)}) collective-permute-start(f32[16,3,8,128]{3,2,1,0:T(8,128)S(1)} %merge.8.cells), channel_id=1, source_target_pairs={{0,1},{1,0},{2,3},{3,2},{4,5},{5,4},{6,7},{7,6},{8,9},{9,8},{10,11... | collective-permute-start | bytes 589832 | tf_op jit(solution)/shard_map/ppermute | solution.py:844
  44.4 2.0 %sweep_4.1 = (f32[16,64,256]{2,1,0:T(8,128)S(1)}, f32[8,128]{1,0:T(8,128)S(1)}) custom-call(f32[16,72,384]{2,1,0:T(8,128)S(1)} %get-tuple-element.69.refs_0_, f32[8,72,384]{2,1,0:T(8,128)S(1)} %get-tuple-element.70.refs_1_, f32[16,72,384]{2,1,0:T(8,128)S(1)} %get-tuple-element.55.refs_2_, f32[16,72,384]{2,1,0:T(8,128)S(1)} %get-tuple-element.52.refs_3_, ...), custom_call_target="tpu_custom_call" | custom-call | flops 1000 | bytes 1750000 | tf_op jit(solution)/shard_map/sweep_4/pallas_call | solution.py:56
  46.5 2.2 %solve.1 = f32[16,64,256]{2,1,0:T(8,128)} custom-call(f32[32,3,8,128]{3,2,1,0:T(8,128)S(1)} %merge.9.gathered, f32[16,64,256]{2,1,0:T(8,128)S(1)} %get-tuple-element.72.fine), custom_call_target="tpu_custom_call" | custom-call | flops 1000 | bytes 7000000 | tf_op jit(solution)/shard_map/solve/pallas_call | solution.py:56
  (15 shorter events, 0.2 us)
Async XLA Ops:
  2.3 6.8 %collective-permute-start = (f32[2,64,256]{2,1,0:T(8,128)S(1)}, f32[2,64,256]{2,1,0:T(8,128)S(1)}, u32[]{:S(2)}, u32[]{:S(2)}) collective-permute-start(f32[2,64,256]{2,1,0:T(8,128)S(1)} %get-tuple-element.42), channel_id=1, source_target_pairs={{0,16},{16,0},{1,17},{17,1},{2,18},{18,2},{3,19},{19,3},{4,20},{20... | collective-permute-start | bytes 393224 | tf_op jit(solution)/shard_map/ppermute | solution.py:766
  4.4 2.1 %collective-permute-start.1 = (f32[2,64,128]{2,1,0:T(8,128)S(1)}, f32[2,64,128]{2,1,0:T(8,128)S(1)}, u32[]{:S(2)}, u32[]{:S(2)}) collective-permute-start(f32[2,64,128]{2,1,0:T(8,128)S(1)} %get-tuple-element.43.refs_8_), channel_id=1, source_target_pairs={{0,1},{1,0},{2,3},{3,2},{4,5},{5,4},{6,7},{7,6},{8,9},{9,8},{10,11... | collective-permute-start | bytes 196616 | tf_op jit(solution)/shard_map/ppermute | solution.py:766
  5.4 3.7 %collective-permute-start.2 = (f32[2,64,128]{2,1,0:T(8,128)S(1)}, f32[2,64,128]{2,1,0:T(8,128)S(1)}, u32[]{:S(2)}, u32[]{:S(2)}) collective-permute-start(f32[2,64,128]{2,1,0:T(8,128)S(1)} %get-tuple-element.44.refs_9_), channel_id=1, source_target_pairs={{1,2},{2,1},{3,0},{0,3},{5,6},{6,5},{7,4},{4,7},{9,10},{10,9},{11,... | collective-permute-start | bytes 196616 | tf_op jit(solution)/shard_map/ppermute | solution.py:769
  9.2 6.7 %collective-permute-start.3 = (f32[25,8,256]{2,1,0:T(8,128)S(1)}, f32[25,8,256]{2,1,0:T(8,128)S(1)}, u32[]{:S(2)}, u32[]{:S(2)}) collective-permute-start(f32[25,8,256]{2,1,0:T(8,128)S(1)} %get-tuple-element.45), channel_id=1, source_target_pairs={{0,4},{4,0},{8,12},{12,8},{1,5},{5,1},{9,13},{13,9},{2,6},{6,2},{1... | collective-permute-start | bytes 614408 | tf_op jit(solution)/shard_map/ppermute | solution.py:766
  10.5 5.4 %collective-permute-start.4 = (f32[25,8,256]{2,1,0:T(8,128)S(1)}, f32[25,8,256]{2,1,0:T(8,128)S(1)}, u32[]{:S(2)}, u32[]{:S(2)}) collective-permute-start(f32[25,8,256]{2,1,0:T(8,128)S(1)} %get-tuple-element.46), channel_id=1, source_target_pairs={{0,1},{1,0},{2,3},{3,2},{4,8},{5,9},{6,10},{7,11},{8,4},{9,5},{10,... | collective-permute-start | bytes 614408 | tf_op jit(solution)/shard_map/ppermute | solution.py:772
  10.9 19.8 %collective-permute-start.7 = (f32[9,64,256]{2,1,0:T(8,128)S(1)}, f32[9,64,256]{2,1,0:T(8,128)S(1)}, u32[]{:S(2)}, u32[]{:S(2)}) collective-permute-start(f32[9,64,256]{2,1,0:T(8,128)S(1)} %get-tuple-element.53), channel_id=1, source_target_pairs={{0,16},{16,0},{1,17},{17,1},{2,18},{18,2},{3,19},{19,3},{4,20},{20... | collective-permute-start | bytes 1769480 | tf_op jit(solution)/shard_map/ppermute | solution.py:766
  17.7 11.1 %collective-permute-start.5 = (f32[36,8,128]{2,1,0:T(8,128)S(1)}, f32[36,8,128]{2,1,0:T(8,128)S(1)}, u32[]{:S(2)}, u32[]{:S(2)}) collective-permute-start(f32[36,8,128]{2,1,0:T(8,128)S(1)} %restrict.1), channel_id=1, source_target_pairs={{0,16},{16,0},{1,17},{17,1},{2,18},{18,2},{3,19},{19,3},{4,20},{20... | collective-permute-start | bytes 442376 | tf_op jit(solution)/shard_map/ppermute | solution.py:766
  28.8 5.2 %collective-permute-start.6 = (f32[2,3,8,128]{3,2,1,0:T(8,128)S(1)}, f32[2,3,8,128]{3,2,1,0:T(8,128)S(1)}, u32[]{:S(2)}, u32[]{:S(2)}) collective-permute-start(f32[2,3,8,128]{3,2,1,0:T(8,128)S(1)} %merge.5.cells), channel_id=1, source_target_pairs={{0,8},{4,12},{8,0},{12,4},{1,9},{5,13},{9,1},{13,5},{2,10},{6,14},... | collective-permute-start | bytes 73736 | tf_op jit(solution)/shard_map/ppermute | solution.py:844
  34.1 3.8 %collective-permute-start.8 = (f32[4,3,8,128]{3,2,1,0:T(8,128)S(1)}, f32[4,3,8,128]{3,2,1,0:T(8,128)S(1)}, u32[]{:S(2)}, u32[]{:S(2)}) collective-permute-start(f32[4,3,8,128]{3,2,1,0:T(8,128)S(1)} %merge.6.cells), channel_id=1, source_target_pairs={{0,2},{1,3},{2,0},{3,1},{4,6},{5,7},{6,4},{7,5},{8,10},{9,11},{10,... | collective-permute-start | bytes 147464 | tf_op jit(solution)/shard_map/ppermute | solution.py:844
  37.9 3.5 %collective-permute-start.9 = (f32[8,3,8,128]{3,2,1,0:T(8,128)S(1)}, f32[8,3,8,128]{3,2,1,0:T(8,128)S(1)}, u32[]{:S(2)}, u32[]{:S(2)}) collective-permute-start(f32[8,3,8,128]{3,2,1,0:T(8,128)S(1)} %merge.7.cells), channel_id=1, source_target_pairs={{0,4},{4,0},{8,12},{12,8},{1,5},{5,1},{9,13},{13,9},{2,6},{6,2},{1... | collective-permute-start | bytes 294920 | tf_op jit(solution)/shard_map/ppermute | solution.py:844
  41.5 5.0 %collective-permute-start.10 = (f32[16,3,8,128]{3,2,1,0:T(8,128)S(1)}, f32[16,3,8,128]{3,2,1,0:T(8,128)S(1)}, u32[]{:S(2)}, u32[]{:S(2)}) collective-permute-start(f32[16,3,8,128]{3,2,1,0:T(8,128)S(1)} %merge.8.cells), channel_id=1, source_target_pairs={{0,1},{1,0},{2,3},{3,2},{4,5},{5,4},{6,7},{7,6},{8,9},{9,8},{10,11... | collective-permute-start | bytes 589832 | tf_op jit(solution)/shard_map/ppermute | solution.py:844

commit v3 on v2

--- a/solution.py
+++ b/solution.py
@@ -19,6 +19,7 @@
 SLOTS = LANES // DEPTH
 F32 = jnp.float32
 VMEM_LIMIT = 12 * 1024 * 1024
+US = dict(local=1.2, rows=0.1, side=0.8, weights=3.2, restrict=0.6, extend=1.0, halo=1.4, outer=0.8, sweep=2.2, solve=2.2)
 
 
 def pairs(count, odd):
@@ -129,10 +130,10 @@
         return lax.axis_index("gx"), lax.axis_index("gy"), lax.axis_index("gz")
 
     def steps(self):
-        bits = [("gx", 1 << i) for i in range(1, self.nz.bit_length() - 1)]
+        bits = [("gx", 1 << i) for i in reversed(range(1, self.nz.bit_length() - 1))]
         bits += [("gy", 1 << i) for i in reversed(range(1, self.ny.bit_length() - 1))]
         bits += [("gz", 1 << i) for i in reversed(range(1, self.nx.bit_length() - 1))]
-        return bits + [("gy", 1), ("gz", 1)]
+        return bits + [("gy", 1), ("gx", 1), ("gz", 1)]
 
     def slot(self, q, z):
         index = q * self.Z + z
@@ -145,8 +146,6 @@
     n = 6
     near = refs[n : n + g.zsides]
     n += g.zsides
-    deep = refs[n : n + g.zsides]
-    n += g.zsides
     x_out = refs[n : n + g.xsides]
     sems = refs[n + g.xsides]
     zi, yi, xi = g.where()
@@ -157,14 +156,10 @@
         target = out.at[pl.ds(place, size)]
         copies.append(pltpu.make_async_copy(source, target, sems.at[3 + len(copies)]))
 
-    rest = DEPTH - 1
     for side in range(g.zsides):
         high = (zi % 2) == side
         for q in range(2):
             send(q, jnp.where(high, g.Z - 1, 0), 1, near[side], q)
-        for q in range(3):
-            first = jnp.where(high, g.Z - rest if q == 2 else g.Z - DEPTH, 0 if q == 2 else 1)
-            send(q, first, rest, deep[side], q * rest)
     loads = [pltpu.make_async_copy(src[q], fields[q], sems.at[q]) for q in range(3)]
     for copy in loads + copies:
         copy.start()
@@ -209,7 +204,7 @@
 def pack_rows_kernel(g, *refs):
     src = refs[:3]
     x_in = refs[3 : 3 + g.xsides]
-    y_out = refs[3 + g.xsides + g.zsides :]
+    y_out = refs[len(refs) - g.ysides :]
     zi, yi, xi = g.where()
     half = g.Z // 2
     last = g.Y - ROWS
@@ -260,43 +255,83 @@
     return jnp.concatenate([hy[block, at : at + DEPTH], ly[block, at : at + DEPTH]], axis=0)
 
 
-def restrict_kernel(g, *refs):
-    n = 3
-    src = refs[:n]
-    z_in = refs[n : n + g.zsides]
-    n += g.zsides
-    y_in = refs[n : n + g.ysides]
-    n += g.ysides
+def deep_kernel(g, p, k, s, after, *deep):
+    rest = DEPTH - 1
+    zi = g.where()[0]
+    for side in range(g.zsides):
+        high = (zi % 2) == side
+        for q, src in enumerate((p, k, s)):
+            first = jnp.where(high, g.Z - rest if q == 2 else g.Z - DEPTH, 0 if q == 2 else 1)
+            deep[side][q * rest : (q + 1) * rest] = src[pl.ds(first, rest)]
+
+
+def local_kernel(g, p, k, s, out, token):
+    token[...] = jnp.zeros((ROWS, LANES), F32)
+    Z, Y, X = g.Z, g.Y, g.X
+    zero = jnp.zeros((Y, X), F32)
+    none = jnp.zeros((ROWS, X), F32)
+    flux_z, weight_z = [none], [none]
+    for layer in range(RATIO, Z, RATIO):
+        w = 0.5 * (k[layer] + k[layer - 1])
+        weight_z.append(group_rows(w))
+        flux_z.append(group_rows(w * (p[layer] - p[layer - 1])))
+    weight_z.append(none)
+    flux_z.append(none)
+    inner_x = (lane_of((ROWS, X)) % RATIO == 0) & (lane_of((ROWS, X)) > 0)
+    first_y = row_of((Y, X)) % RATIO == 0
+    row8 = row_of((ROWS, X))
+    for cz in range(g.cz):
+        acc_s = acc_wx = acc_fx = acc_wy = acc_fy = zero
+        for z in range(cz * RATIO, (cz + 1) * RATIO):
+            pz, kz = p[z], k[z]
+            acc_s = acc_s + s[z]
+            w = kz + roll(kz, 1, 1)
+            acc_wx = acc_wx + w
+            acc_fx = acc_fx + w * (pz - roll(pz, 1, 1))
+            w = kz + roll(kz, 1, 0)
+            acc_wy = acc_wy + w
+            acc_fy = acc_fy + w * (pz - roll(pz, 1, 0))
+        weight_x = jnp.where(inner_x, 0.5 * group_rows(acc_wx), 0.0)
+        flux_x = jnp.where(inner_x, 0.5 * group_rows(acc_fx), 0.0)
+        weight_y, flux_y = (
+            jnp.where(row8 > 0, 0.5 * group_rows(jnp.where(first_y, acc, 0.0)), 0.0)
+            for acc in (acc_wy, acc_fy)
+        )
+        out[0, cz] = (
+            group_rows(acc_s)
+            - (flux_z[cz] - flux_z[cz + 1])
+            - (flux_y - roll(flux_y, -1, 0))
+            - (flux_x - roll(flux_x, -1, 1))
+        )
+        out[1, cz] = (
+            weight_z[cz]
+            + weight_z[cz + 1]
+            + weight_y
+            + roll(weight_y, -1, 0)
+            + weight_x
+            + roll(weight_x, -1, 1)
+        )
+        out[2, cz] = weight_z[cz]
+        out[3, cz] = weight_y
+        out[4, cz] = weight_x
+
+
+def side_kernel(g, *refs):
+    p, k, s, sums = refs[:4]
+    n = 4
     x_in = refs[n : n + g.xsides]
     n += g.xsides
     x_own = refs[n : n + g.xsides]
     n += g.xsides
-    outs = refs[n : n + g.zsides]
-    n += g.zsides
-    hy, ly, xh, xl = refs[n:]
-    p, k, s = src
+    n += g.ysides
+    out, xp, xk, xs, token = refs[n : n + 5]
+    xh, xl = refs[n + 5 :]
     zi, yi, xi = g.where()
-    gather_rows(g, yi, y_in, hy, ly)
-    gather_strips(g, xi, x_in, hy, ly, xh, xl)
     Z, Y, X = g.Z, g.Y, g.X
-    half = Z // 2
-
-    zero = jnp.zeros((Y, X), F32)
-    flux_z, weight_z = [], []
-    for layer in range(0, Z + 1, RATIO):
-        if layer == 0:
-            p0 = from_low(zi, g.nz, z_in, lambda r: r[0])
-            k0 = from_low(zi, g.nz, z_in, lambda r: r[1])
-        else:
-            p0, k0 = p[layer - 1], k[layer - 1]
-        if layer == Z:
-            p1 = from_high(zi, g.nz, z_in, lambda r: r[0])
-            k1 = from_high(zi, g.nz, z_in, lambda r: r[1])
-        else:
-            p1, k1 = p[layer], k[layer]
-        w = face(k0, k1)
-        weight_z.append(group_rows(w))
-        flux_z.append(group_rows(w * (p1 - p0)))
+    token[...] = jnp.zeros((ROWS, LANES), F32)
+    for block in range(g.blocks):
+        xh[block] = from_high(xi, g.nx, x_in, lambda r: r[block])
+        xl[block] = from_low(xi, g.nx, x_in, lambda r: r[block])
 
     lane = lane_of((Y, LANES))
     even = (xi % 2) == 0
@@ -321,84 +356,113 @@
             result.append(total)
         return result
 
-    low_w, low_f = side_sums(own_lo, roll(xl[0, :Y], -(DEPTH - 1), 1), 0, False)
-    high_w, high_f = side_sums(own_hi, roll(xh[0, :Y], DEPTH - 1, 1), DEPTH - 1, True)
+    low_w, low_f = side_sums(own_lo, roll(xl[0], -(DEPTH - 1), 1), 0, False)
+    high_w, high_f = side_sums(own_hi, roll(xh[0], DEPTH - 1, 1), DEPTH - 1, True)
     lane8 = lane_of((ROWS, X))
-    row8 = row_of((ROWS, X))
-    row = row_of((Y, X))
-    inner = (lane8 % RATIO == 0) & (lane8 > 0)
 
     def widen(value, at, cell):
         moved = roll(value, (at % LANES) - cell, 1)
         wide = jnp.concatenate([moved] * (X // LANES), axis=1)
         return jnp.where(lane8 == at, wide, 0.0)
 
-    rows = []
     for cz in range(g.cz):
-        acc_s = zero
-        acc_w = zero
-        acc_f = zero
-        acc_wy = zero
-        acc_fy = zero
-        low_wy = low_fy = top_w = top_f = jnp.zeros((1, X), F32)
-        for z in range(cz * RATIO, (cz + 1) * RATIO):
-            pz, kz = p[z], k[z]
-            acc_s = acc_s + s[z]
-            w = 0.5 * (kz + roll(kz, 1, 1))
-            acc_w = acc_w + w
-            acc_f = acc_f + w * (pz - roll(pz, 1, 1))
-            w = 0.5 * (kz + roll(kz, 1, 0))
-            acc_wy = acc_wy + w
-            acc_fy = acc_fy + w * (pz - roll(pz, 1, 0))
-            at = (z % 2) * DEPTH
-            below = [ly[q * half + z // 2, at + DEPTH - 1 : at + DEPTH, :] for q in range(2)]
-            above = [hy[q * half + z // 2, at : at + 1, :] for q in range(2)]
-            w = face(kz[:1], below[1])
-            low_wy = low_wy + w
-            low_fy = low_fy + w * (pz[:1] - below[0])
-            w = face(kz[Y - 1 :], above[1])
-            top_w = top_w + w
-            top_f = top_f + w * (above[0] - pz[Y - 1 :])
-
-        def lower(acc, low):
-            kept = group_rows(jnp.where(row % RATIO == 0, acc, 0.0))
-            return jnp.where(row8 == 0, jnp.broadcast_to(low, (ROWS, X)), kept)
-
-        weight_y = lower(acc_wy, low_wy)
-        flux_y = lower(acc_fy, low_fy)
-
-        def upper(values, top):
-            return jnp.where(
-                row8 == g.cy - 1, jnp.broadcast_to(top, (ROWS, X)), roll(values, -1, 0)
-            )
-
-        weight_x = jnp.where(inner, group_rows(acc_w), 0.0)
-        flux_x = jnp.where(inner, group_rows(acc_f), 0.0)
         cell = cz * RATIO * DEPTH
         x_low = widen(low_w, 0, cell)
         x_high = widen(high_w, X - 1, cell + DEPTH - 1)
         f_low = widen(low_f, 0, cell)
         f_high = widen(high_f, X - 1, cell + DEPTH - 1)
-        rhs = (
-            group_rows(acc_s)
-            - (flux_z[cz] - flux_z[cz + 1])
-            - (flux_y - upper(flux_y, top_f))
-            - (flux_x - roll(flux_x, -1, 1))
-            - (f_low - f_high)
-        )
-        diagonal = (
-            weight_z[cz]
-            + weight_z[cz + 1]
-            + weight_y
-            + upper(weight_y, top_w)
-            + weight_x
-            + roll(weight_x, -1, 1)
-            + x_low
-            + x_high
-        )
-        rows.append([rhs, diagonal, weight_z[cz], weight_y, weight_x + x_low])
-
-    items = [rows[cz][q] for q in range(5) for cz in range(g.cz)]
+        out[0, cz] = sums[0, cz] - (f_low - f_high)
+        out[1, cz] = sums[1, cz] + x_low + x_high
+        out[2, cz] = sums[2, cz]
+        out[3, cz] = sums[3, cz]
+        out[4, cz] = sums[4, cz] + x_low
+
+    for q, dst in enumerate((xp, xk, xs)):
+        for z in range(Z):
+            block, at = g.slot(q, z)
+            hi = roll(xh[block], -at, 1)
+            lo = roll(xl[block], -at - DEPTH, 1)
+            dst[z] = strip_tile(hi, lo)
+
+
+def weights_kernel(g, k, xk, after, fz, fy, fx, dinv, token):
+    token[...] = jnp.zeros((ROWS, LANES), F32)
+    Z = g.Z
+
+    def k_at(z):
+        return jnp.concatenate([k[z], xk[z]], axis=1)
+
+    fy[0], fx[0], _ = side_faces(k_at(0))
+    fz[1] = face(k_at(1), k_at(0))
+
+    def body(z, carry):
+        kz = k_at(z)
+        above = face(k_at(z + 1), kz)
+        fz[z + 1] = above
+        wy, wx, total = side_faces(kz)
+        fy[z] = wy
+        fx[z] = wx
+        dinv[z] = scale_of(kz, total + fz[z] + above)
+        return carry
+
+    lax.fori_loop(1, Z - 1, body, 0)
+    fy[Z - 1], fx[Z - 1], _ = side_faces(k_at(Z - 1))
+
+
+def restrict_kernel(g, *refs):
+    p, k, sums = refs[:3]
+    n = 3
+    near = refs[n : n + g.zsides]
+    n += g.zsides
+    y_in = refs[n : n + g.ysides]
+    n += g.ysides
+    out = refs[n + 1]
+    zi, yi, xi = g.where()
+    Z, Y, X = g.Z, g.Y, g.X
+    half = Z // 2
+    row8 = row_of((ROWS, X))
+    p0, k0 = (from_low(zi, g.nz, near, lambda r, q=q: r[q]) for q in range(2))
+    w = face(k0, k[0])
+    low_wz, low_fz = group_rows(w), group_rows(w * (p[0] - p0))
+    p1, k1 = (from_high(zi, g.nz, near, lambda r, q=q: r[q]) for q in range(2))
+    w = face(k[Z - 1], k1)
+    top_wz, top_fz = group_rows(w), group_rows(w * (p1 - p[Z - 1]))
+    items = []
+    for cz in range(g.cz):
+        low_w = low_f = top_w = top_f = jnp.zeros((1, X), F32)
+        for z in range(cz * RATIO, (cz + 1) * RATIO):
+            at = (z % 2) * DEPTH
+            below, above = [], []
+            for q in range(2):
+                block = q * half + z // 2
+                row = at + DEPTH - 1
+                below.append(from_low(yi, g.ny, y_in, lambda r: r[block, row : row + 1, :]))
+                above.append(from_high(yi, g.ny, y_in, lambda r: r[block, at : at + 1, :]))
+            kz, pz = k[z, 0:1, :], p[z, 0:1, :]
+            w = face(kz, below[1])
+            low_w = low_w + w
+            low_f = low_f + w * (pz - below[0])
+            kz, pz = k[z, Y - 1 :, :], p[z, Y - 1 :, :]
+            w = face(kz, above[1])
+            top_w = top_w + w
+            top_f = top_f + w * (above[0] - pz)
+
+        def at_row(row, value):
+            return jnp.where(row8 == row, jnp.broadcast_to(value, (ROWS, X)), 0.0)
+
+        low_wy = at_row(0, low_w)
+        rhs = sums[0, cz] - at_row(0, low_f) + at_row(g.cy - 1, top_f)
+        diagonal = sums[1, cz] + low_wy + at_row(g.cy - 1, top_w)
+        wz = sums[2, cz]
+        if cz == 0:
+            rhs = rhs - low_fz
+            diagonal = diagonal + low_wz
+            wz = wz + low_wz
+        if cz == g.cz - 1:
+            rhs = rhs + top_fz
+            diagonal = diagonal + top_wz
+        items.append([rhs, diagonal, wz, sums[3, cz] + low_wy, sums[4, cz]])
+    items = [items[cz][q] for q in range(5) for cz in range(g.cz)]
     onehot = (
         lax.broadcasted_iota(jnp.int32, (X, LANES), 0) // RATIO
         == lax.broadcasted_iota(jnp.int32, (X, LANES), 1)
@@ -412,22 +476,24 @@
             summed[m * ROWS : (m + 1) * ROWS], place, 1
         )
     for block, value in enumerate(cells):
-        outs[0][block] = value
-
+        out[0, block] = value
+
+
+def fill_relay(g, hy, ly, xh, xl, outs, zi):
+    Z, X = g.Z, g.X
     for side, out in enumerate(outs):
-        base = coarse_blocks(g) if side == 0 else 0
         high = (zi % 2) == side
 
-        def fill(top, out=out, base=base):
+        def fill(top, out=out):
             first = Z - DEPTH if top else 0
             for q in range(3):
                 for d in range(DEPTH):
                     part = row_halo(g, hy, ly, q, first + d)
                     for half_lane in range(X // LANES):
-                        out[base + (q * DEPTH + d) * (X // LANES) + half_lane] = part[
+                        out[(q * DEPTH + d) * (X // LANES) + half_lane] = part[
                             :, half_lane * LANES : (half_lane + 1) * LANES
                         ]
-            at_block = base + 3 * DEPTH * (X // LANES)
+            at_block = 3 * DEPTH * (X // LANES)
             wide = lane_of((g.YE, LANES))
             acc = jnp.zeros((g.YE, LANES), F32)
             span = DEPTH * DEPTH
@@ -450,8 +516,8 @@
     return 3 * DEPTH * (g.X // LANES) + g.YE // ROWS
 
 
-def strip_tile(g, hi, lo):
-    lane = lane_of((g.YE, LANES))
+def strip_tile(hi, lo):
+    lane = lane_of(hi.shape)
     return jnp.where(lane < DEPTH, hi, jnp.where(lane >= LANES - DEPTH, lo, 0.0))
 
 
@@ -465,74 +531,137 @@
     return jnp.where(kz > 0.0, OMEGA / total, 0.0)
 
 
+class Fields:
+    def __init__(self, main, side, rows):
+        self.parts = main, side, rows
+
+    def __getitem__(self, z):
+        main, side, rows = self.parts
+        wide = jnp.concatenate([main[z], side[z]], axis=1)
+        return jnp.concatenate([wide, rows[z]], axis=0)
+
+
+class Rows:
+    def __init__(self, main, edge, head, tail):
+        self.main, self.edge, self.head, self.tail = main, edge, head, tail
+
+    def __getitem__(self, z):
+        rows = self.main.shape[1]
+        middle = self.main[z, self.head * ROWS : rows - self.tail * ROWS]
+        parts = [middle, self.edge[z, self.head * ROWS :]]
+        if self.head:
+            parts = [self.edge[z, : self.head * ROWS]] + parts
+        return jnp.concatenate(parts, axis=0)
+
+
 def extend_kernel(g, *refs):
-    n = 3
-    src = refs[:n]
+    k, xk, fz, fy, fx = refs[:5]
+    n = 5
     y_in = refs[n : n + g.ysides]
     n += g.ysides
     x_in = refs[n : n + g.xsides]
     n += g.xsides
-    pe, ke, se, fz, fy, fx, dinv, token = refs[n : n + 8]
-    hy, ly, xh, xl = refs[n + 8 :]
+    n += 1
+    yp, yk, ys, fz_y, fx_y, fy_e, dinv_e, token = refs[n : n + 8]
+    n += 8
+    relay = refs[n : n + g.zsides]
+    n += g.zsides
+    hy, ly, xh, xl = refs[n:]
+    zi, yi, xi = g.where()
+    Z, Y, X = g.Z, g.Y, g.X
     token[...] = jnp.zeros((ROWS, LANES), F32)
-    zi, yi, xi = g.where()
     gather_rows(g, yi, y_in, hy, ly)
     gather_strips(g, xi, x_in, hy, ly, xh, xl)
-    for q, out in enumerate((pe, ke, se)):
-        for z in range(g.Z):
-            out[z, : g.Y, : g.X] = src[q][z]
-            out[z, g.Y :, : g.X] = row_halo(g, hy, ly, q, z)
+    fill_relay(g, hy, ly, xh, xl, relay, zi)
+    for q, out in enumerate((yp, yk, ys)):
+        for z in range(Z):
+            out[z, :, :X] = row_halo(g, hy, ly, q, z)
             block, at = g.slot(q, z)
-            hi = roll(xh[block], -at, 1)
-            lo = roll(xl[block], -at - DEPTH, 1)
-            out[z, :, g.X :] = strip_tile(g, hi, lo)
-    fy[0], fx[0], _ = side_faces(ke[0])
-    fz[1] = face(ke[1], ke[0])
-
-    def body(z, carry):
-        kz = ke[z]
-        above = face(ke[z + 1], kz)
-        fz[z + 1] = above
-        wy, wx, total = side_faces(kz)
-        fy[z] = wy
-        fx[z] = wx
-        dinv[z] = scale_of(kz, total + fz[z] + above)
-        return carry
-
-    lax.fori_loop(1, g.Z - 1, body, 0)
-    fy[g.Z - 1], fx[g.Z - 1], _ = side_faces(ke[g.Z - 1])
+            hi = roll(xh[block, Y:], -at, 1)
+            lo = roll(xl[block, Y:], -at - DEPTH, 1)
+            out[z, :, X:] = strip_tile(hi, lo)
+
+    def edge_rows(z):
+        first = jnp.concatenate([k[z, :ROWS], xk[z, :ROWS]], axis=1)
+        last = jnp.concatenate([k[z, Y - ROWS :], xk[z, Y - ROWS :]], axis=1)
+        return last, yk[z], first
+
+    for z in range(Z):
+        last, beyond, first = edge_rows(z)
+        tiles = jnp.concatenate([last, beyond, first], axis=0)
+        wy = face(tiles, roll(tiles, 1, 0))
+        fy_e[z, :ROWS] = wy[2 * ROWS :]
+        fy_e[z, ROWS:] = wy[ROWS : 2 * ROWS]
+        wx = face(beyond, roll(beyond, 1, 1))
+        fx_y[z] = wx
+        if z > 0:
+            fz_y[z] = face(beyond, yk[z - 1])
+    for z in range(1, Z - 1):
+        last, beyond, first = edge_rows(z)
+        tiles = jnp.concatenate([last, beyond, first], axis=0)
+        wy = jnp.concatenate(
+            [fy[z, Y - ROWS :], fy_e[z, ROWS:], fy_e[z, :ROWS], fy[z, ROWS : 2 * ROWS]], axis=0
+        )
+        wy = (wy + roll(wy, -1, 0))[: 3 * ROWS]
+        wx = jnp.concatenate([fx[z, Y - ROWS :], fx_y[z], fx[z, :ROWS]], axis=0)
+        wz = [
+            jnp.concatenate([fz[i, Y - ROWS :], fz_y[i], fz[i, :ROWS]], axis=0) for i in (z, z + 1)
+        ]
+        scale = scale_of(tiles, wy + wx + roll(wx, -1, 1) + wz[0] + wz[1])
+        dinv_e[z, :ROWS] = scale[2 * ROWS :]
+        dinv_e[z, ROWS : 2 * ROWS] = scale[:ROWS]
+        dinv_e[z, 2 * ROWS :] = scale[ROWS : 2 * ROWS]
+
+
+def beyond(g, z):
+    return z + DEPTH if z < DEPTH else z - g.Z + 3 * DEPTH
+
+
+def face_at(g, z):
+    return z + DEPTH - 1 if z <= 0 else z - g.Z + DEPTH
+
+
+def scale_at(g, z):
+    return z + DEPTH - 1 if z <= 0 else z - g.Z + 1 + DEPTH
+
+
+def own_weights(refs):
+    fz, fz_y, fx, fx_y, fy, fy_e = refs
+    return Rows(fz, fz_y, 0, 0), Rows(fx, fx_y, 0, 0), Rows(fy, fy_e, 1, 0)
 
 
 def halo_kernel(g, *refs):
-    ke, fy, fx, fz = refs[:4]
-    n = 4
+    own_k = Fields(*refs[:3])
+    fz, fx, fy = own_weights(refs[3:9])
+    n = 9
     near = refs[n : n + g.zsides]
     n += g.zsides
     deep = refs[n : n + g.zsides]
     n += g.zsides
     relay = refs[n : n + g.zsides]
     n += g.zsides
-    ph, sh, hz, hy, hx, hd = refs[n : n + 6]
-    kh = refs[n + 6]
+    n += 1
+    ph, sh, hz, hy, hx, hd, token = refs[n : n + 7]
+    kh = refs[n + 7]
+    token[...] = jnp.zeros((ROWS, LANES), F32)
     zi, yi, xi = g.where()
     Z, Y, X = g.Z, g.Y, g.X
     parts = X // LANES
+    rest = DEPTH - 1
     zero = jnp.zeros((g.YE, g.XE), F32)
 
     def k_at(z):
-        return ke[z] if 0 <= z < Z else kh[z + DEPTH if z < 0 else z - Z + DEPTH]
+        return own_k[z] if 0 <= z < Z else kh[beyond(g, z)]
 
     def own_faces(z):
         wy, wx = fy[z], fx[z]
         return wy + roll(wy, -1, 0) + wx + roll(wx, -1, 1)
 
     def fill(top, side):
-        base = coarse_blocks(g) if side == 0 else 0
-        first = DEPTH if top else 0
-        strip = relay[side][base + 3 * DEPTH * parts :].reshape(g.YE, LANES)
+        strip = relay[side][3 * DEPTH * parts :].reshape(g.YE, LANES)
         for q, out in enumerate((ph, kh, sh)):
             for d in range(DEPTH):
-                rest = DEPTH - 1
+                at = beyond(g, Z + d if top else d - DEPTH)
                 if q < 2 and d == (0 if top else rest):
                     plane = near[side][q]
                 elif q < 2:
@@ -541,71 +670,71 @@
                     continue
                 else:
                     plane = deep[side][q * rest + (d if top else d - 1)]
-                out[first + d, :Y, :X] = plane
+                out[at, :Y, :X] = plane
                 for part in range(parts):
                     lanes = slice(part * LANES, (part + 1) * LANES)
-                    out[first + d, Y:, lanes] = relay[side][base + (q * DEPTH + d) * parts + part]
+                    out[at, Y:, lanes] = relay[side][(q * DEPTH + d) * parts + part]
                 hi = roll(strip, -(q * DEPTH + d) * DEPTH, 1)
                 lo = roll(strip, -((3 + q) * DEPTH + d) * DEPTH - DEPTH, 1)
-                out[first + d, :, X:] = strip_tile(g, hi, lo)
-        if top:
-            layers = range(Z, Z + DEPTH - 1)
-            kz = k_at(Z - 1)
-            below = face(k_at(Z), kz)
-            hz[DEPTH] = below
-            hd[DEPTH] = scale_of(kz, own_faces(Z - 1) + fz[Z - 1] + below)
-            for z in layers:
-                kz = k_at(z)
-                above = face(k_at(z + 1), kz)
-                hz[z + 1 - Z + DEPTH] = above
-                wy, wx, total = side_faces(kz)
-                hy[z - Z + DEPTH] = wy
-                hx[z - Z + DEPTH] = wx
-                hd[z + 1 - Z + DEPTH] = scale_of(kz, total + below + above)
-                below = above
-        else:
-            kz = k_at(0)
-            above = face(kz, k_at(-1))
-            hz[DEPTH - 1] = above
-            hd[DEPTH - 1] = scale_of(kz, own_faces(0) + fz[1] + above)
-            for z in range(-1, -DEPTH, -1):
-                kz = k_at(z)
-                below = face(kz, k_at(z - 1))
-                hz[z + DEPTH - 1] = below
-                wy, wx, total = side_faces(kz)
-                hy[z + DEPTH] = wy
-                hx[z + DEPTH] = wx
-                hd[z + DEPTH - 1] = scale_of(kz, total + below + above)
-                above = below
+                out[at, :, X:] = strip_tile(hi, lo)
+        z = Z - 1 if top else 0
+        step = 1 if top else -1
+        kz = k_at(z)
+        outer = face(k_at(z + step), kz)
+        hz[face_at(g, z + 1 if top else z)] = outer
+        inner = fz[z if top else z + 1]
+        hd[scale_at(g, z)] = scale_of(kz, own_faces(z) + inner + outer)
+        for _ in range(DEPTH - 1):
+            z += step
+            inner = outer
+            kz = k_at(z)
+            outer = face(k_at(z + step), kz)
+            hz[face_at(g, z + 1 if top else z)] = outer
+            wy, wx, total = side_faces(kz)
+            hy[beyond(g, z)] = wy
+            hx[beyond(g, z)] = wx
+            hd[scale_at(g, z)] = scale_of(kz, total + inner + outer)
+
+    def boundary(top):
+        z = Z - 1 if top else 0
+        kz = k_at(z)
+        ph[beyond(g, z + 1 if top else z - 1)] = zero
+        hz[face_at(g, z + 1 if top else z)] = kz
+        hd[scale_at(g, z)] = scale_of(kz, own_faces(z) + fz[z if top else z + 1] + kz)
 
     for side in range(g.zsides):
         above = (zi % 2) == side
         pl.when(above & (zi < g.nz - 1))(functools.partial(fill, True, side))
         pl.when(jnp.logical_not(above) & (zi > 0))(functools.partial(fill, False, side))
-
-    @pl.when(zi == 0)
-    def _():
-        ph[DEPTH - 1] = zero
-        kz = ke[0]
-        hz[DEPTH - 1] = kz
-        hd[DEPTH - 1] = scale_of(kz, own_faces(0) + fz[1] + kz)
-
-    @pl.when(zi == g.nz - 1)
-    def _():
-        ph[DEPTH] = zero
-        kz = ke[Z - 1]
-        hz[DEPTH] = kz
-        hd[DEPTH] = scale_of(kz, own_faces(Z - 1) + fz[Z - 1] + kz)
-
-
-def sweep_kernel(g, sweep, *refs):
-    v, vh, s, fz, fy, fx, dinv, sh, hz, hy, hx, hd = refs[:12]
-    out = refs[12]
-    refs[-1][...] = jnp.zeros((ROWS, LANES), F32)
-    out_halo = refs[13]
-    zi, yi, xi = g.where()
+    pl.when(zi == 0)(functools.partial(boundary, False))
+    pl.when(zi == g.nz - 1)(functools.partial(boundary, True))
+
+
+def sweep_kernel(g, sweep, inside, *refs):
+    refs = list(refs)
     Z = g.Z
     final = sweep == SWEEPS
+    own_s = Fields(*refs[:3])
+    fz, fx, fy = own_weights(refs[3:9])
+    dinv = Rows(refs[9], refs[10], 1, 1)
+    n = 11
+    if sweep == 1:
+        v = Fields(*refs[n : n + 3])
+        n += 3
+    else:
+        v = refs[n]
+        n += 1
+    if not inside:
+        vh, sh, hz, hy, hx, hd = refs[n : n + 6]
+        n += 6
+    if final and inside:
+        out = refs[n]
+    elif final:
+        earlier, out = refs[n : n + 2]
+    else:
+        out = refs[n]
+    refs[-1][...] = jnp.zeros((ROWS, LANES), F32)
+    zi, yi, xi = g.where()
     reach = SWEEPS - sweep
 
     def update(vz, low, high, source, z_low, z_high, wy, wx, scale):
@@ -614,52 +743,66 @@
         total = total + wx * roll(vz, 1, 1) + roll(wx * vz, -1, 1)
         return (1.0 - OMEGA) * vz + scale * total
 
-    def store(z, new):
-        out[z] = new[: g.Y, : g.X] if final else new
-
-    def pick_layer(own, halo, z):
-        return own[z] if 0 <= z < Z else halo[z + DEPTH if z < 0 else z - Z + DEPTH]
+    if inside:
+
+        def body(z, carry):
+            new = update(
+                v[z], v[z - 1], v[z + 1], own_s[z], fz[z], fz[z + 1], fy[z], fx[z], dinv[z]
+            )
+            if final:
+                out[z] = new[: g.Y, : g.X]
+            else:
+                out[z] = new
+            return carry
+
+        lax.fori_loop(sweep, Z - sweep, body, 0)
+        return
+
+    def v_at(z):
+        return v[z] if sweep - 1 <= z <= Z - sweep else vh[beyond(g, z)]
 
     def z_face(z):
-        return fz[z] if 1 <= z < Z else hz[z + DEPTH - 1 if z < 1 else z - Z + DEPTH]
+        return fz[z] if 1 <= z < Z else hz[face_at(g, z)]
 
     def edge(z):
-        scale = dinv[z] if 0 < z < Z - 1 else hd[z + DEPTH - 1 if z < 1 else z - Z + 1 + DEPTH]
-        return update(
-            pick_layer(v, vh, z),
-            pick_layer(v, vh, z - 1),
-            pick_layer(v, vh, z + 1),
-            pick_layer(s, sh, z),
+        own = 0 <= z < Z
+        at = beyond(g, z)
+        new = update(
+            v_at(z),
+            v_at(z - 1),
+            v_at(z + 1),
+            own_s[z] if own else sh[at],
             z_face(z),
             z_face(z + 1),
-            pick_layer(fy, hy, z),
-            pick_layer(fx, hx, z),
-            scale,
+            fy[z] if own else hy[at],
+            fx[z] if own else hx[at],
+            dinv[z] if 0 < z < Z - 1 else hd[scale_at(g, z)],
         )
-
-    store(0, edge(0))
-
-    def body(z, carry):
-        store(z, update(v[z], v[z - 1], v[z + 1], s[z], fz[z], fz[z + 1], fy[z], fx[z], dinv[z]))
-        return carry
-
-    lax.fori_loop(1, Z - 1, body, 0)
-    store(Z - 1, edge(Z - 1))
+        if final:
+            out[z] = new[: g.Y, : g.X]
+        else:
+            out[at] = new
+
+    for z in range(sweep):
+        edge(z)
+        edge(Z - 1 - z)
     if final:
+        for z in range(sweep, Z - sweep):
+            out[z] = earlier[z]
         return
     zero = jnp.zeros((g.YE, g.XE), F32)
 
     def halo(layers):
         for z in layers:
-            out_halo[z + DEPTH if z < 0 else z - Z + DEPTH] = edge(z)
-
-    def outside(at):
-        out_halo[at] = zero
+            edge(z)
+
+    def clear(z):
+        out[beyond(g, z)] = zero
 
     pl.when(zi > 0)(functools.partial(halo, range(-reach, 0)))
     pl.when(zi < g.nz - 1)(functools.partial(halo, range(Z, Z + reach)))
-    pl.when(zi == 0)(functools.partial(outside, DEPTH - 1))
-    pl.when(zi == g.nz - 1)(functools.partial(outside, DEPTH))
+    pl.when(zi == 0)(functools.partial(clear, -1))
+    pl.when(zi == g.nz - 1)(functools.partial(clear, Z))
 
 
 def solve_kernel(g, gathered, fine, out):
@@ -667,7 +810,7 @@
     per = LANES // g.cx
     group = lane_of((ROWS, LANES)) // g.cx
 
-    order = [("gx", 1)] + g.steps()
+    order = g.steps()
 
     def relative(a, b, c):
         apart = {
@@ -776,89 +919,128 @@
 def shards(pressure_start, source, permeability):
     g = Grid(pressure_start.shape)
     Z, Y, X = g.Z, g.Y, g.X
-    fields = [pressure_start, permeability, source]
+    tile = (ROWS, LANES)
     x_shape = (g.blocks, Y, LANES)
     y_shape = (3 * Z // 2 + 1, ROWS, X)
+    sums_shape = (5, g.cz, ROWS, X)
+    main = (Z, Y, g.XE)
+    nr = relay_blocks(g)
+
     sent = run(
         functools.partial(pack_kernel, g),
         [(Z, Y, X)] * 3
         + [(2, Y, X)] * g.zsides
-        + [(3 * (DEPTH - 1), Y, X)] * g.zsides
         + [x_shape] * g.xsides,
-        fields,
-        scratch=[pltpu.SemaphoreType.DMA((3 + 5 * g.zsides,))],
+        [pressure_start, permeability, source],
+        scratch=[pltpu.SemaphoreType.DMA((3 + 2 * g.zsides,))],
         name="pack_faces",
         far=True,
     )
     sent = list(sent)
-    fields, near, deep = sent[:3], sent[3 : 3 + g.zsides], sent[3 + g.zsides : 3 + 2 * g.zsides]
-    x_sent = sent[3 + 2 * g.zsides :]
+    (p, k, s), near, x_sent = sent[:3], sent[3 : 3 + g.zsides], sent[3 + g.zsides :]
     near_got = exchange(near, "gx", g.nz, "gz")
     x_got = exchange(x_sent, "gz", g.nx)
-    deep_got = exchange(deep, "gx", g.nz, "gz")
+    sums, token = run(
+        functools.partial(local_kernel, g),
+        [sums_shape, tile],
+        [p, k, s],
+        us=US["local"],
+        name="local_sums",
+    )
     y_sent = run(
-        functools.partial(pack_rows_kernel, g), [y_shape] * g.ysides, fields + x_got + near_got, name="pack_rows"
+        functools.partial(pack_rows_kernel, g),
+        [y_shape] * g.ysides,
+        [p, k, s] + x_got + near_got + [token],
+        us=US["rows"],
+        name="pack_rows",
     )
     y_got = exchange(y_sent, "gy", g.ny, "gz")
-
-    halo_scratch = [
-        pltpu.VMEM(y_shape, F32),
-        pltpu.VMEM(y_shape, F32),
-        pltpu.VMEM((g.blocks, g.YE, LANES), F32),
-        pltpu.VMEM((g.blocks, g.YE, LANES), F32),
-    ]
-    nc, nr = coarse_blocks(g), relay_blocks(g)
-    packed = run(
+    sums, xp, xk, xs, token = run(
+        functools.partial(side_kernel, g),
+        [sums_shape] + [(Z, Y, LANES)] * 3 + [tile],
+        [p, k, s, sums] + x_got + x_sent + list(y_sent),
+        scratch=[pltpu.VMEM(x_shape, F32)] * 2,
+        us=US["side"],
+        name="side",
+    )
+    deep = run(
+        functools.partial(deep_kernel, g),
+        [(3 * (DEPTH - 1), Y, X)] * g.zsides,
+        [p, k, s, token],
+        us=0.1,
+        name="pack_deep",
+    )
+    deep_got = exchange(deep, "gx", g.nz, "gz")
+    fz, fy, fx, dinv, token = run(
+        functools.partial(weights_kernel, g),
+        [main] * 4 + [tile],
+        [k, xk, token],
+        us=US["weights"],
+        name="weights",
+    )
+    (cells,) = run(
         functools.partial(restrict_kernel, g),
-        [(nc + nr, ROWS, LANES)] + [(nr, ROWS, LANES)] * (g.zsides - 1),
-        fields + near_got + y_got + x_got + x_sent,
-        scratch=halo_scratch,
+        [(1, coarse_blocks(g)) + tile],
+        [p, k, sums] + near_got + list(y_got) + [token],
+        us=US["restrict"],
         name="restrict",
     )
-    relay = exchange(packed, "gx", g.nz, "gz")
-    tile = (ROWS, LANES)
-    own = (Z, g.YE, g.XE)
-    far = (2 * DEPTH, g.YE, g.XE)
-    pe, ke, se, fz, fy, fx, dinv, token = run(
+    rows = (Z, ROWS, g.XE)
+    halo_scratch = [pltpu.VMEM(y_shape, F32)] * 2 + [pltpu.VMEM((g.blocks, g.YE, LANES), F32)] * 2
+    extended = run(
         functools.partial(extend_kernel, g),
-        [own] * 7 + [tile],
-        fields + y_got + x_got,
+        [rows] * 5 + [(Z, 2 * ROWS, g.XE), (Z, 3 * ROWS, g.XE), tile] + [(nr,) + tile] * g.zsides,
+        [k, xk, fz, fy, fx] + list(y_got) + x_got + [cells],
         scratch=halo_scratch,
-        us=0.5,
+        us=US["extend"],
         name="extend",
     )
-    ph, sh, hz, hy, hx, hd = run(
+    yp, yk, ys, fz_y, fx_y, fy_e, dinv_e, token = extended[:8]
+    relay = exchange(extended[8:], "gx", g.nz, "gz")
+    weights = [fz, fz_y, fx, fx_y, fy, fy_e]
+    common = [s, xs, ys] + weights + [dinv, dinv_e]
+    own = (Z, g.YE, g.XE)
+    far = (4 * DEPTH, g.YE, g.XE)
+    far8 = (2 * DEPTH, g.YE, g.XE)
+    inner, tokens = [[p, xp, yp]], []
+    for sweep in range(1, SWEEPS + 1):
+        v, token = run(
+            functools.partial(sweep_kernel, g, sweep, True),
+            [(Z, Y, X) if sweep == SWEEPS else own, tile],
+            common + inner[-1],
+            us=US["sweep"] * (Z - 2 * sweep) / Z,
+            name=f"inner_{sweep}",
+        )
+        inner.append([v])
+        tokens.append(token)
+    vh, sh, hz, hy, hx, hd, token = run(
         functools.partial(halo_kernel, g),
-        [far] * 6,
-        [ke, fy, fx, fz] + near_got + deep_got + relay,
+        [far, far, far8, far, far, far8, tile],
+        [k, xk, yk] + weights + near_got + deep_got + relay + [tokens[2]],
         scratch=[pltpu.VMEM(far, F32)],
-        us=0.1,
+        us=US["halo"],
         name="halo",
     )
-    cells = merge(packed[0][None, :nc], relay[0][None, :nc], token)
-    v, vh = pe, ph
+    for sweep in range(1, SWEEPS + 1):
+        final = sweep == SWEEPS
+        vh, token = run(
+            functools.partial(sweep_kernel, g, sweep, False),
+            [(Z, Y, X) if final else far, tile],
+            common + inner[sweep - 1] + [vh, sh, hz, hy, hx, hd] + (inner[sweep] if final else []),
+            us=US["outer"],
+            name=f"outer_{sweep}",
+        )
+        tokens.append(token)
     steps = g.steps()
-    for number in range(max(len(steps), SWEEPS)):
-        if number < len(steps):
-            axis, bit = steps[number]
-            got = lax.ppermute(cells, axis, flips(lax.axis_size(axis), bit))
-        if number < SWEEPS:
-            final = number == SWEEPS - 1
-            result = run(
-                functools.partial(sweep_kernel, g, number + 1),
-                ([(Z, Y, X)] if final else [own, far]) + [tile],
-                [v, vh, se, fz, fy, fx, dinv, sh, hz, hy, hx, hd],
-                us=0.5,
-                name=f"sweep_{number + 1}",
-            )
-            v, vh, token = result[0], result[1], result[-1]
-        if number < len(steps):
-            cells = merge(cells, got, token)
+    plan = [0, 1, 3, 5, 6]
+    for number, (axis, bit) in enumerate(steps):
+        got = lax.ppermute(cells, axis, flips(lax.axis_size(axis), bit))
+        cells = merge(cells, got, tokens[plan[max(0, number - len(steps) + len(plan))]])
     (out,) = run(
         functools.partial(solve_kernel, g),
         [(Z, Y, X)],
-        [cells, v],
-        us=2.0,
+        [cells, vh],
+        us=US["solve"],
         name="solve",
         spaces=[jax.ShapeDtypeStruct((Z, Y, X), F32)],
     )

time: 48.8 us -> 43.8 us (0.90)
  waiting for transfers between devices: 13.6 us -> 2.81 us
  starting transfers between devices: 14 us -> 18 us
  Pallas kernels: 21 us -> 22.7 us
    ppermute x5, waiting for transfers between devices: 10.6 us -> 0.01 us  [exchange(): got = [lax.ppermute(bufs[0], axis, pairs(count, 0))]]
    ppermute x4 -> x5, starting transfers between devices: 6.81 us -> 9 us  [shards(): got = lax.ppermute(cells, axis, flips(lax.axis_size(axis), bit))]
    pallas_call x15 -> x23, Pallas kernels: 21 us -> 22.7 us  [run(): pl.pallas_call(kernel, out_shape=shapes, in_specs=[pl.BlockSpec(memory_sp...]
    ppermute x1, waiting for transfers between devices: 2.58 us -> 1.58 us  [exchange(): got.append(lax.ppermute(bufs[1], axis, pairs(count, 1)))]
    ppermute x1, starting transfers between devices: 0.32 us -> 1.26 us  [exchange(): got.append(lax.ppermute(bufs[1], (axis, beside), perm))]
    ppermute x5, starting transfers between devices: 5.73 us -> 6.62 us  [exchange(): got = [lax.ppermute(bufs[0], axis, pairs(count, 0))]]
    ppermute x4 -> x5, waiting for transfers between devices: 0.41 us -> 1.21 us  [shards(): got = lax.ppermute(cells, axis, flips(lax.axis_size(axis), bit))]
  transfers between devices with their start and end apart: 11 -> 12, of which waited for: 4 -> 2; matrix products, arithmetic and copies ran while one was open for 0% -> 0% of each run, Pallas kernels for 34% -> 39%
where the time goes in v3:
time: 43.8 us; the launch traced here: 43.7 us
  Pallas kernels  22.7 us (52%)
  starting transfers between devices  18 us (41%)
  waiting for transfers between devices  2.81 us (6%)
    pallas_call x23, Pallas kernels, run(): pl.pallas_call(kernel, out_shape=shapes, in_specs=[pl.BlockSpec(memory_sp...  22.7 us
    ppermute x5, starting transfers between devices, shards(): got = lax.ppermute(cells, axis, flips(lax.axis_size(axis), bit))  9 us
    ppermute x5, starting transfers between devices, exchange(): got = [lax.ppermute(bufs[0], axis, pairs(count, 0))]  6.62 us
    ppermute x1, waiting for transfers between devices, exchange(): got.append(lax.ppermute(bufs[1], axis, pairs(count, 1)))  1.58 us
    ppermute x1, starting transfers between devices, exchange(): got.append(lax.ppermute(bufs[1], (axis, beside), perm))  1.26 us
    ppermute x5, waiting for transfers between devices, shards(): got = lax.ppermute(cells, axis, flips(lax.axis_size(axis), bit))  1.21 us
    ppermute x1, starting transfers between devices, exchange(): got.append(lax.ppermute(bufs[1], axis, pairs(count, 1)))  1.13 us
  transfers between devices with their start and end apart: 12, of which 2 were waited for; matrix products, arithmetic and copies ran while one was open for 0% of the time, Pallas kernels for 39%

profile of v3, /device:TPU:1, one launch (start us, length us, event | category | flops | bytes accessed | tf_op | source)
XLA Modules:
  0.0 43.7 jit_solution(2545433140466592966)
XLA Ops:
  0.0 2.3 %pack_faces.1 = (f32[16,64,256]{2,1,0:T(8,128)S(1)}, f32[16,64,256]{2,1,0:T(8,128)S(1)}, f32[16,64,256]{2,1,0:T(8,128)S(1)}, f32[2,64,256]{2,1,0:T(8,128)S(1)}, ...) custom-call(f32[16,64,256]{2,1,0:T(8,128)} %refs_0_.1, f32[16,64,256]{2,1,0:T(8,128)} %refs_1_.1, f32[16,64,256]{2,1,0:T(8,128)} %refs_2_.1), custom_call_target="tpu_custom_call" | custom-call | flops 1000 | bytes 3500000 | tf_op jit(solution)/shard_map/pack_faces/pallas_call | solution.py:57
  2.3 2.1 %collective-permute-start.2 = (f32[2,64,256]{2,1,0:T(8,128)S(1)}, f32[2,64,256]{2,1,0:T(8,128)S(1)}, u32[]{:S(2)}, u32[]{:S(2)}) collective-permute-start(f32[2,64,256]{2,1,0:T(8,128)S(1)} %get-tuple-element.59), channel_id=1, source_target_pairs={{0,16},{16,0},{1,17},{17,1},{2,18},{18,2},{3,19},{19,3},{4,20},{20... | collective-permute-start | bytes 393224 | tf_op jit(solution)/shard_map/ppermute | solution.py:909
  4.4 1.0 %collective-permute-start = (f32[2,64,128]{2,1,0:T(8,128)S(1)}, f32[2,64,128]{2,1,0:T(8,128)S(1)}, u32[]{:S(2)}, u32[]{:S(2)}) collective-permute-start(f32[2,64,128]{2,1,0:T(8,128)S(1)} %get-tuple-element.57.refs_6_), channel_id=1, source_target_pairs={{0,1},{1,0},{2,3},{3,2},{4,5},{5,4},{6,7},{7,6},{8,9},{9,8},{10,11... | collective-permute-start | bytes 196616 | tf_op jit(solution)/shard_map/ppermute | solution.py:909
  5.3 1.1 %collective-permute-start.1 = (f32[2,64,128]{2,1,0:T(8,128)S(1)}, f32[2,64,128]{2,1,0:T(8,128)S(1)}, u32[]{:S(2)}, u32[]{:S(2)}) collective-permute-start(f32[2,64,128]{2,1,0:T(8,128)S(1)} %get-tuple-element.58.refs_7_), channel_id=1, source_target_pairs={{1,2},{2,1},{3,0},{0,3},{5,6},{6,5},{7,4},{4,7},{9,10},{10,9},{11,... | collective-permute-start | bytes 196616 | tf_op jit(solution)/shard_map/ppermute | solution.py:912
  6.5 1.0 %local_sums.1 = (f32[5,2,8,256]{3,2,1,0:T(8,128)S(1)}, f32[8,128]{1,0:T(8,128)S(1)}) custom-call(f32[16,64,256]{2,1,0:T(8,128)S(1)} %get-tuple-element.53.p.refs_0_.refs_11_, f32[16,64,256]{2,1,0:T(8,128)S(1)} %get-tuple-element.54.k.refs_1_.refs_0_, f32[16,64,256]{2,1,0:T(8,128)S(1)} %get-tuple-element.55.s.refs_2_.refs_0_), custom_call_target="tpu_custom_call" | custom-call | flops 1000 | bytes 4200000 | tf_op jit(solution)/shard_map/local_sums/pallas_call | solution.py:57
  7.5 1.6 %collective-permute-done.1.refs_4_.refs_5_.refs_8_ = f32[2,64,128]{2,1,0:T(8,128)S(1)} collective-permute-done((f32[2,64,128]{2,1,0:T(8,128)S(1)}, f32[2,64,128]{2,1,0:T(8,128)S(1)}, u32[]{:S(2)}, u32[]{:S(2)}) %collective-permute-start.1) | collective-permute-done | bytes 65568 | tf_op jit(solution)/shard_map/ppermute | solution.py:912
  9.1 1.0 %side.1 = (f32[5,2,8,256]{3,2,1,0:T(8,128)S(1)}, f32[16,64,128]{2,1,0:T(8,128)S(1)}, f32[16,64,128]{2,1,0:T(8,128)S(1)}, f32[16,64,128]{2,1,0:T(8,128)S(1)}, f32[8,128]{1,0:T(8,128)S(1)}) custom-call(f32[16,64,256]{2,1,0:T(8,128)S(1)} %get-tuple-element.53.p.refs_0_.refs_11_, f32[16,64,256]{2,1,0:T(8,128)S(1)} %get-tuple-element.54.k.refs_1_.refs_0_, ...), custom_call_target="tpu_custom_call" | custom-call | flops 1000 | bytes 2800000 | tf_op jit(solution)/shard_map/side/pallas_call | solution.py:57
  10.7 1.4 %collective-permute-start.3 = (f32[25,8,256]{2,1,0:T(8,128)S(1)}, f32[25,8,256]{2,1,0:T(8,128)S(1)}, u32[]{:S(2)}, u32[]{:S(2)}) collective-permute-start(f32[25,8,256]{2,1,0:T(8,128)S(1)} %get-tuple-element.61.refs_8_), channel_id=1, source_target_pairs={{0,4},{4,0},{8,12},{12,8},{1,5},{5,1},{9,13},{13,9},{2,6},{6,2},{1... | collective-permute-start | bytes 614408 | tf_op jit(solution)/shard_map/ppermute | solution.py:909
  12.1 1.3 %collective-permute-start.4 = (f32[25,8,256]{2,1,0:T(8,128)S(1)}, f32[25,8,256]{2,1,0:T(8,128)S(1)}, u32[]{:S(2)}, u32[]{:S(2)}) collective-permute-start(f32[25,8,256]{2,1,0:T(8,128)S(1)} %get-tuple-element.62.refs_9_), channel_id=1, source_target_pairs={{0,1},{1,0},{2,3},{3,2},{4,8},{5,9},{6,10},{7,11},{8,4},{9,5},{10,... | collective-permute-start | bytes 614408 | tf_op jit(solution)/shard_map/ppermute | solution.py:915
  13.3 3.2 %weights.1 = (f32[16,64,384]{2,1,0:T(8,128)S(1)}, f32[16,64,384]{2,1,0:T(8,128)S(1)}, f32[16,64,384]{2,1,0:T(8,128)S(1)}, f32[16,64,384]{2,1,0:T(8,128)S(1)}, f32[8,128]{1,0:T(8,128)S(1)}) custom-call(f32[16,64,256]{2,1,0:T(8,128)S(1)} %get-tuple-element.54.k.refs_1_.refs_0_, f32[16,64,128]{2,1,0:T(8,128)S(1)} %get-tuple-element.64.xk.refs_1_, ...), custom_call_target="tpu_custom_call" | custom-call | flops 1000 | bytes 11200000 | tf_op jit(solution)/shard_map/weights/pallas_call | solution.py:57
  16.9 3.2 %collective-permute-start.5 = (f32[1,3,8,128]{3,2,1,0:T(8,128)S(1)}, f32[1,3,8,128]{3,2,1,0:T(8,128)S(1)}, u32[]{:S(2)}, u32[]{:S(2)}) collective-permute-start(f32[1,3,8,128]{3,2,1,0:T(8,128)S(1)} %restrict.1.refs_9_.cells), channel_id=1, source_target_pairs={{0,8},{4,12},{8,0},{12,4},{1,9},{5,13},{9,1},{13,5},{2,10},{6,14},... | collective-permute-start | bytes 36872 | tf_op jit(solution)/shard_map/ppermute | solution.py:1037
  21.1 2.0 %inner_1.1 = (f32[16,72,384]{2,1,0:T(8,128)S(1)}, f32[8,128]{1,0:T(8,128)S(1)}) custom-call(f32[16,64,256]{2,1,0:T(8,128)S(1)} %get-tuple-element.55.s.refs_2_.refs_0_, f32[16,64,128]{2,1,0:T(8,128)S(1)} %get-tuple-element.67.refs_1_, f32[16,8,384]{2,1,0:T(8,128)S(1)} %get-tuple-element.71.refs_2_, f32[16,64,384]{2,1,0:T(8,128)S(1)} %get-tuple-element.68.refs_2_.refs_3_, ...), custom_call_target="tpu_custom_call" | custom-call | flops 1000 | bytes 6737500 | tf_op jit(solution)/shard_map/inner_1/pallas_call | solution.py:57
  23.1 1.3 %collective-permute-start.6 = (f32[2,3,8,128]{3,2,1,0:T(8,128)S(1)}, f32[2,3,8,128]{3,2,1,0:T(8,128)S(1)}, u32[]{:S(2)}, u32[]{:S(2)}) collective-permute-start(f32[2,3,8,128]{3,2,1,0:T(8,128)S(1)} %merge.5.cells), channel_id=1, source_target_pairs={{0,2},{1,3},{2,0},{3,1},{4,6},{5,7},{6,4},{7,5},{8,10},{9,11},{10,... | collective-permute-start | bytes 73736 | tf_op jit(solution)/shard_map/ppermute | solution.py:1037
  24.4 1.8 %inner_2.1 = (f32[16,72,384]{2,1,0:T(8,128)S(1)}, f32[8,128]{1,0:T(8,128)S(1)}) custom-call(f32[16,64,256]{2,1,0:T(8,128)S(1)} %get-tuple-element.55.s.refs_2_.refs_0_, f32[16,64,128]{2,1,0:T(8,128)S(1)} %get-tuple-element.67.refs_1_, f32[16,8,384]{2,1,0:T(8,128)S(1)} %get-tuple-element.71.refs_2_, f32[16,64,384]{2,1,0:T(8,128)S(1)} %get-tuple-element.68.refs_2_.refs_3_, ...), custom_call_target="tpu_custom_call" | custom-call | flops 1000 | bytes 5775000 | tf_op jit(solution)/shard_map/inner_2/pallas_call | solution.py:57
  26.5 1.7 %collective-permute-start.10 = (f32[33,8,128]{2,1,0:T(8,128)S(1)}, f32[33,8,128]{2,1,0:T(8,128)S(1)}, u32[]{:S(2)}, u32[]{:S(2)}) collective-permute-start(f32[33,8,128]{2,1,0:T(8,128)S(1)} %get-tuple-element.86), channel_id=1, source_target_pairs={{0,16},{16,0},{1,17},{17,1},{2,18},{18,2},{3,19},{19,3},{4,20},{20... | collective-permute-start | bytes 405512 | tf_op jit(solution)/shard_map/ppermute | solution.py:909
  28.2 1.5 %inner_3.1 = (f32[16,72,384]{2,1,0:T(8,128)S(1)}, f32[8,128]{1,0:T(8,128)S(1)}) custom-call(f32[16,64,256]{2,1,0:T(8,128)S(1)} %get-tuple-element.55.s.refs_2_.refs_0_, f32[16,64,128]{2,1,0:T(8,128)S(1)} %get-tuple-element.67.refs_1_, f32[16,8,384]{2,1,0:T(8,128)S(1)} %get-tuple-element.71.refs_2_, f32[16,64,384]{2,1,0:T(8,128)S(1)} %get-tuple-element.68.refs_2_.refs_3_, ...), custom_call_target="tpu_custom_call" | custom-call | flops 1000 | bytes 4812500 | tf_op jit(solution)/shard_map/inner_3/pallas_call | solution.py:57
  29.7 1.0 %inner_4.1 = (f32[16,64,256]{2,1,0:T(8,128)S(1)}, f32[8,128]{1,0:T(8,128)S(1)}) custom-call(f32[16,64,256]{2,1,0:T(8,128)S(1)} %get-tuple-element.55.s.refs_2_.refs_0_, f32[16,64,128]{2,1,0:T(8,128)S(1)} %get-tuple-element.67.refs_1_, f32[16,8,384]{2,1,0:T(8,128)S(1)} %get-tuple-element.71.refs_2_, f32[16,64,384]{2,1,0:T(8,128)S(1)} %get-tuple-element.68.refs_2_.refs_3_, ...), custom_call_target="tpu_custom_call" | custom-call | flops 1000 | bytes 3850000 | tf_op jit(solution)/shard_map/inner_4/pallas_call | solution.py:57
  30.9 1.4 %halo.1 = (f32[16,72,384]{2,1,0:T(8,128)S(1)}, f32[16,72,384]{2,1,0:T(8,128)S(1)}, f32[8,72,384]{2,1,0:T(8,128)S(1)}, f32[16,72,384]{2,1,0:T(8,128)S(1)}, f32[16...) custom-call(f32[16,64,256]{2,1,0:T(8,128)S(1)} %get-tuple-element.54.k.refs_1_.refs_0_, ...), custom_call_target="tpu_custom_call" | custom-call | flops 1000 | bytes 4900000 | tf_op jit(solution)/shard_map/halo/pallas_call | solution.py:57
  32.3 1.2 %outer_1.1 = (f32[16,72,384]{2,1,0:T(8,128)S(1)}, f32[8,128]{1,0:T(8,128)}) custom-call(f32[16,64,256]{2,1,0:T(8,128)S(1)} %get-tuple-element.55.s.refs_2_.refs_0_, f32[16,64,128]{2,1,0:T(8,128)S(1)} %get-tuple-element.67.refs_1_, f32[16,8,384]{2,1,0:T(8,128)S(1)} %get-tuple-element.71.refs_2_, f32[16,64,384]{2,1,0:T(8,128)S(1)} %get-tuple-element.68.refs_2_.refs_3_, ...), custom_call_target="tpu_custom_call" | custom-call | flops 1000 | bytes 2800000 | tf_op jit(solution)/shard_map/outer_1/pallas_call | solution.py:57
  34.3 1.2 %collective-permute-done.8.got = f32[8,3,8,128]{3,2,1,0:T(8,128)S(1)} collective-permute-done((f32[8,3,8,128]{3,2,1,0:T(8,128)S(1)}, f32[8,3,8,128]{3,2,1,0:T(8,128)S(1)}, u32[]{:S(2)}, u32[]{:S(2)}) %collective-permute-start.8) | collective-permute-done | bytes 98336 | tf_op jit(solution)/shard_map/ppermute | solution.py:1037
  35.5 4.0 %collective-permute-start.11 = (f32[16,3,8,128]{3,2,1,0:T(8,128)S(1)}, f32[16,3,8,128]{3,2,1,0:T(8,128)S(1)}, u32[]{:S(2)}, u32[]{:S(2)}) collective-permute-start(f32[16,3,8,128]{3,2,1,0:T(8,128)S(1)} %merge.8.cells), channel_id=1, source_target_pairs={{0,1},{1,0},{2,3},{3,2},{4,5},{5,4},{6,7},{7,6},{8,9},{9,8},{10,11... | collective-permute-start | bytes 589832 | tf_op jit(solution)/shard_map/ppermute | solution.py:1037
  39.5 0.9 %outer_3.1 = (f32[16,72,384]{2,1,0:T(8,128)S(1)}, f32[8,128]{1,0:T(8,128)S(1)}) custom-call(f32[16,64,256]{2,1,0:T(8,128)S(1)} %get-tuple-element.55.s.refs_2_.refs_0_, f32[16,64,128]{2,1,0:T(8,128)S(1)} %get-tuple-element.67.refs_1_, f32[16,8,384]{2,1,0:T(8,128)S(1)} %get-tuple-element.71.refs_2_, f32[16,64,384]{2,1,0:T(8,128)S(1)} %get-tuple-element.68.refs_2_.refs_3_, ...), custom_call_target="tpu_custom_call" | custom-call | flops 1000 | bytes 2800000 | tf_op jit(solution)/shard_map/outer_3/pallas_call | solution.py:57
  40.4 1.1 %outer_4.1 = (f32[16,64,256]{2,1,0:T(8,128)S(1)}, f32[8,128]{1,0:T(8,128)}) custom-call(f32[16,64,256]{2,1,0:T(8,128)S(1)} %get-tuple-element.55.s.refs_2_.refs_0_, f32[16,64,128]{2,1,0:T(8,128)S(1)} %get-tuple-element.67.refs_1_, f32[16,8,384]{2,1,0:T(8,128)S(1)} %get-tuple-element.71.refs_2_, f32[16,64,384]{2,1,0:T(8,128)S(1)} %get-tuple-element.68.refs_2_.refs_3_, ...), custom_call_target="tpu_custom_call" | custom-call | flops 1000 | bytes 2800000 | tf_op jit(solution)/shard_map/outer_4/pallas_call | solution.py:57
  41.5 2.2 %solve.1 = f32[16,64,256]{2,1,0:T(8,128)} custom-call(f32[32,3,8,128]{3,2,1,0:T(8,128)S(1)} %merge.9.gathered, f32[16,64,256]{2,1,0:T(8,128)S(1)} %get-tuple-element.100.fine), custom_call_target="tpu_custom_call" | custom-call | flops 1000 | bytes 7700000 | tf_op jit(solution)/shard_map/solve/pallas_call | solution.py:57
  (23 shorter events, 3.3 us)
Async XLA Ops:
  2.3 6.8 %collective-permute-start.2 = (f32[2,64,256]{2,1,0:T(8,128)S(1)}, f32[2,64,256]{2,1,0:T(8,128)S(1)}, u32[]{:S(2)}, u32[]{:S(2)}) collective-permute-start(f32[2,64,256]{2,1,0:T(8,128)S(1)} %get-tuple-element.59), channel_id=1, source_target_pairs={{0,16},{16,0},{1,17},{17,1},{2,18},{18,2},{3,19},{19,3},{4,20},{20... | collective-permute-start | bytes 393224 | tf_op jit(solution)/shard_map/ppermute | solution.py:909
  4.4 3.1 %collective-permute-start = (f32[2,64,128]{2,1,0:T(8,128)S(1)}, f32[2,64,128]{2,1,0:T(8,128)S(1)}, u32[]{:S(2)}, u32[]{:S(2)}) collective-permute-start(f32[2,64,128]{2,1,0:T(8,128)S(1)} %get-tuple-element.57.refs_6_), channel_id=1, source_target_pairs={{0,1},{1,0},{2,3},{3,2},{4,5},{5,4},{6,7},{7,6},{8,9},{9,8},{10,11... | collective-permute-start | bytes 196616 | tf_op jit(solution)/shard_map/ppermute | solution.py:909
  5.3 3.7 %collective-permute-start.1 = (f32[2,64,128]{2,1,0:T(8,128)S(1)}, f32[2,64,128]{2,1,0:T(8,128)S(1)}, u32[]{:S(2)}, u32[]{:S(2)}) collective-permute-start(f32[2,64,128]{2,1,0:T(8,128)S(1)} %get-tuple-element.58.refs_7_), channel_id=1, source_target_pairs={{1,2},{2,1},{3,0},{0,3},{5,6},{6,5},{7,4},{4,7},{9,10},{10,9},{11,... | collective-permute-start | bytes 196616 | tf_op jit(solution)/shard_map/ppermute | solution.py:912
  10.2 20.7 %collective-permute-start.9 = (f32[9,64,256]{2,1,0:T(8,128)S(1)}, f32[9,64,256]{2,1,0:T(8,128)S(1)}, u32[]{:S(2)}, u32[]{:S(2)}) collective-permute-start(f32[9,64,256]{2,1,0:T(8,128)S(1)} %pack_deep.1), channel_id=1, source_target_pairs={{0,16},{16,0},{1,17},{17,1},{2,18},{18,2},{3,19},{19,3},{4,20},{20... | collective-permute-start | bytes 1769480 | tf_op jit(solution)/shard_map/ppermute | solution.py:909
  10.7 5.8 %collective-permute-start.3 = (f32[25,8,256]{2,1,0:T(8,128)S(1)}, f32[25,8,256]{2,1,0:T(8,128)S(1)}, u32[]{:S(2)}, u32[]{:S(2)}) collective-permute-start(f32[25,8,256]{2,1,0:T(8,128)S(1)} %get-tuple-element.61.refs_8_), channel_id=1, source_target_pairs={{0,4},{4,0},{8,12},{12,8},{1,5},{5,1},{9,13},{13,9},{2,6},{6,2},{1... | collective-permute-start | bytes 614408 | tf_op jit(solution)/shard_map/ppermute | solution.py:909
  12.1 4.4 %collective-permute-start.4 = (f32[25,8,256]{2,1,0:T(8,128)S(1)}, f32[25,8,256]{2,1,0:T(8,128)S(1)}, u32[]{:S(2)}, u32[]{:S(2)}) collective-permute-start(f32[25,8,256]{2,1,0:T(8,128)S(1)} %get-tuple-element.62.refs_9_), channel_id=1, source_target_pairs={{0,1},{1,0},{2,3},{3,2},{4,8},{5,9},{6,10},{7,11},{8,4},{9,5},{10,... | collective-permute-start | bytes 614408 | tf_op jit(solution)/shard_map/ppermute | solution.py:915
  16.9 6.1 %collective-permute-start.5 = (f32[1,3,8,128]{3,2,1,0:T(8,128)S(1)}, f32[1,3,8,128]{3,2,1,0:T(8,128)S(1)}, u32[]{:S(2)}, u32[]{:S(2)}) collective-permute-start(f32[1,3,8,128]{3,2,1,0:T(8,128)S(1)} %restrict.1.refs_9_.cells), channel_id=1, source_target_pairs={{0,8},{4,12},{8,0},{12,4},{1,9},{5,13},{9,1},{13,5},{2,10},{6,14},... | collective-permute-start | bytes 36872 | tf_op jit(solution)/shard_map/ppermute | solution.py:1037
  23.1 3.1 %collective-permute-start.6 = (f32[2,3,8,128]{3,2,1,0:T(8,128)S(1)}, f32[2,3,8,128]{3,2,1,0:T(8,128)S(1)}, u32[]{:S(2)}, u32[]{:S(2)}) collective-permute-start(f32[2,3,8,128]{3,2,1,0:T(8,128)S(1)} %merge.5.cells), channel_id=1, source_target_pairs={{0,2},{1,3},{2,0},{3,1},{4,6},{5,7},{6,4},{7,5},{8,10},{9,11},{10,... | collective-permute-start | bytes 73736 | tf_op jit(solution)/shard_map/ppermute | solution.py:1037
  26.2 4.5 %collective-permute-start.7 = (f32[4,3,8,128]{3,2,1,0:T(8,128)S(1)}, f32[4,3,8,128]{3,2,1,0:T(8,128)S(1)}, u32[]{:S(2)}, u32[]{:S(2)}) collective-permute-start(f32[4,3,8,128]{3,2,1,0:T(8,128)S(1)} %merge.6.cells), channel_id=1, source_target_pairs={{0,4},{4,0},{8,12},{12,8},{1,5},{5,1},{9,13},{13,9},{2,6},{6,2},{1... | collective-permute-start | bytes 147464 | tf_op jit(solution)/shard_map/ppermute | solution.py:1037
  26.5 4.4 %collective-permute-start.10 = (f32[33,8,128]{2,1,0:T(8,128)S(1)}, f32[33,8,128]{2,1,0:T(8,128)S(1)}, u32[]{:S(2)}, u32[]{:S(2)}) collective-permute-start(f32[33,8,128]{2,1,0:T(8,128)S(1)} %get-tuple-element.86), channel_id=1, source_target_pairs={{0,16},{16,0},{1,17},{17,1},{2,18},{18,2},{3,19},{19,3},{4,20},{20... | collective-permute-start | bytes 405512 | tf_op jit(solution)/shard_map/ppermute | solution.py:909
  30.7 4.8 %collective-permute-start.8 = (f32[8,3,8,128]{3,2,1,0:T(8,128)S(1)}, f32[8,3,8,128]{3,2,1,0:T(8,128)S(1)}, u32[]{:S(2)}, u32[]{:S(2)}) collective-permute-start(f32[8,3,8,128]{3,2,1,0:T(8,128)S(1)} %merge.7.cells), channel_id=1, source_target_pairs={{0,16},{16,0},{1,17},{17,1},{2,18},{18,2},{3,19},{19,3},{4,20},{20... | collective-permute-start | bytes 294920 | tf_op jit(solution)/shard_map/ppermute | solution.py:1037
  35.5 5.9 %collective-permute-start.11 = (f32[16,3,8,128]{3,2,1,0:T(8,128)S(1)}, f32[16,3,8,128]{3,2,1,0:T(8,128)S(1)}, u32[]{:S(2)}, u32[]{:S(2)}) collective-permute-start(f32[16,3,8,128]{3,2,1,0:T(8,128)S(1)} %merge.8.cells), channel_id=1, source_target_pairs={{0,1},{1,0},{2,3},{3,2},{4,5},{5,4},{6,7},{7,6},{8,9},{9,8},{10,11... | collective-permute-start | bytes 589832 | tf_op jit(solution)/shard_map/ppermute | solution.py:1037

commit v4 on v3

--- a/solution.py
+++ b/solution.py
@@ -130,10 +130,11 @@
         return lax.axis_index("gx"), lax.axis_index("gy"), lax.axis_index("gz")
 
     def steps(self):
-        bits = [("gx", 1 << i) for i in reversed(range(1, self.nz.bit_length() - 1))]
-        bits += [("gy", 1 << i) for i in reversed(range(1, self.ny.bit_length() - 1))]
+        bits = [("gy", 1 << i) for i in reversed(range(1, self.ny.bit_length() - 1))]
         bits += [("gz", 1 << i) for i in reversed(range(1, self.nx.bit_length() - 1))]
-        return bits + [("gy", 1), ("gx", 1), ("gz", 1)]
+        bits += [("gy", 1)]
+        bits += [("gx", 1 << i) for i in reversed(range(self.nz.bit_length() - 1))]
+        return bits + [("gz", 1)]
 
     def slot(self, q, z):
         index = q * self.Z + z
@@ -147,7 +148,9 @@
     near = refs[n : n + g.zsides]
     n += g.zsides
     x_out = refs[n : n + g.xsides]
-    sems = refs[n + g.xsides]
+    n += g.xsides
+    y_out = refs[n : n + g.ysides]
+    sems = refs[n + g.ysides]
     zi, yi, xi = g.where()
     copies = []
 
@@ -175,6 +178,13 @@
             hi_pack[block] = jnp.where(keep, moved, hi_pack[block])
             moved = roll(fields[q][z, :, :LANES], at, 1)
             lo_pack[block] = jnp.where(keep, moved, lo_pack[block])
+        if q < 2:
+            for at in range(0, g.Z, ROWS):
+                layers = range(at, at + ROWS)
+                hi = jnp.concatenate([fields[q][z, g.Y - 1 :, :] for z in layers], axis=0)
+                lo = jnp.concatenate([fields[q][z, :1, :] for z in layers], axis=0)
+                for side, out in enumerate(y_out):
+                    out[q, at : at + ROWS] = jnp.where((yi % 2) == side, hi, lo)
     even = (xi % 2) == 0
     for block in range(g.blocks):
         for side, out in enumerate(x_out):
@@ -255,7 +265,8 @@
     return jnp.concatenate([hy[block, at : at + DEPTH], ly[block, at : at + DEPTH]], axis=0)
 
 
-def deep_kernel(g, p, k, s, after, *deep):
+def deep_kernel(g, p, k, s, *refs):
+    deep = refs[len(refs) - g.zsides :]
     rest = DEPTH - 1
     zi = g.where()[0]
     for side in range(g.zsides):
@@ -317,29 +328,91 @@
 
 
 def side_kernel(g, *refs):
-    p, k, s, sums = refs[:4]
-    n = 4
+    x_in = refs[: g.xsides]
+    xp, xk, xs, token, xh, xl = refs[g.xsides + 1 :]
+    xi = g.where()[2]
+    Z = g.Z
+    token[...] = jnp.zeros((ROWS, LANES), F32)
+    for block in range(g.blocks):
+        xh[block] = from_high(xi, g.nx, x_in, lambda r: r[block])
+        xl[block] = from_low(xi, g.nx, x_in, lambda r: r[block])
+
+    for q, dst in enumerate((xp, xk, xs)):
+        for z in range(Z):
+            block, at = g.slot(q, z)
+            hi = roll(xh[block], -at, 1)
+            lo = roll(xl[block], -at - DEPTH, 1)
+            dst[z] = strip_tile(hi, lo)
+
+
+def weights_kernel(g, k, xk, after, fz, fy, fx, dinv, token):
+    token[...] = jnp.zeros((ROWS, LANES), F32)
+    Z = g.Z
+
+    def k_at(z):
+        return jnp.concatenate([k[z], xk[z]], axis=1)
+
+    fy[0], fx[0], _ = side_faces(k_at(0))
+    below = face(k_at(1), k_at(0))
+    fz[1] = below
+    for z in range(1, Z - 1):
+        kz = k_at(z)
+        above = face(k_at(z + 1), kz)
+        fz[z + 1] = above
+        wy, wx, total = side_faces(kz)
+        fy[z] = wy
+        fx[z] = wx
+        dinv[z] = scale_of(kz, total + below + above)
+        below = above
+    fy[Z - 1], fx[Z - 1], _ = side_faces(k_at(Z - 1))
+
+
+def own_sides(bufs, even, view):
+    if len(bufs) == 1:
+        return view(bufs[0]), view(bufs[0])
+    first, second = view(bufs[0]), view(bufs[1])
+    return jnp.where(even, first, second), jnp.where(even, second, first)
+
+
+def restrict_kernel(g, *refs):
+    p, k, sums = refs[:3]
+    n = 3
+    near = refs[n : n + g.zsides]
+    n += g.zsides
+    y_in = refs[n : n + g.ysides]
+    n += g.ysides
+    y_own = refs[n : n + g.ysides]
+    n += g.ysides
     x_in = refs[n : n + g.xsides]
     n += g.xsides
     x_own = refs[n : n + g.xsides]
     n += g.xsides
-    n += g.ysides
-    out, xp, xk, xs, token = refs[n : n + 5]
-    xh, xl = refs[n + 5 :]
+    out, token = refs[n:]
+    token[...] = jnp.zeros((ROWS, LANES), F32)
     zi, yi, xi = g.where()
     Z, Y, X = g.Z, g.Y, g.X
-    token[...] = jnp.zeros((ROWS, LANES), F32)
-    for block in range(g.blocks):
-        xh[block] = from_high(xi, g.nx, x_in, lambda r: r[block])
-        xl[block] = from_low(xi, g.nx, x_in, lambda r: r[block])
+
+    p0, k0 = (from_low(zi, g.nz, near, lambda r, q=q: r[q]) for q in range(2))
+    w = face(k0, k[0])
+    low_wz, low_fz = group_rows(w), group_rows(w * (p[0] - p0))
+    p1, k1 = (from_high(zi, g.nz, near, lambda r, q=q: r[q]) for q in range(2))
+    w = face(k[Z - 1], k1)
+    top_wz, top_fz = group_rows(w), group_rows(w * (p1 - p[Z - 1]))
+
+    (p_hi, p_lo), (k_hi, k_lo) = (
+        own_sides(y_own, (yi % 2) == 0, lambda r, q=q: r[q]) for q in range(2)
+    )
+    p0, k0 = (from_low(yi, g.ny, y_in, lambda r, q=q: r[q]) for q in range(2))
+    low_wy = face(k0, k_lo)
+    low_fy = low_wy * (p_lo - p0)
+    p1, k1 = (from_high(yi, g.ny, y_in, lambda r, q=q: r[q]) for q in range(2))
+    top_wy = face(k_hi, k1)
+    top_fy = top_wy * (p1 - p_hi)
 
     lane = lane_of((Y, LANES))
-    even = (xi % 2) == 0
-    if g.xsides == 1:
-        own_hi = own_lo = x_own[0][0]
-    else:
-        own_hi = jnp.where(even, x_own[0][0], x_own[1][0])
-        own_lo = jnp.where(even, x_own[1][0], x_own[0][0])
+    own_hi, own_lo = own_sides(x_own, (xi % 2) == 0, lambda r: r[0])
+    next_hi = from_high(xi, g.nx, x_in, lambda r: r[0])
+    next_lo = from_low(xi, g.nx, x_in, lambda r: r[0])
 
     def side_sums(own, other, lane_in, flip):
         wk = face(roll(own, -Z * DEPTH, 1), roll(other, -Z * DEPTH, 1))
@@ -356,103 +429,29 @@
             result.append(total)
         return result
 
-    low_w, low_f = side_sums(own_lo, roll(xl[0], -(DEPTH - 1), 1), 0, False)
-    high_w, high_f = side_sums(own_hi, roll(xh[0], DEPTH - 1, 1), DEPTH - 1, True)
+    low_wx, low_fx = side_sums(own_lo, roll(next_lo, -(DEPTH - 1), 1), 0, False)
+    top_wx, top_fx = side_sums(own_hi, roll(next_hi, DEPTH - 1, 1), DEPTH - 1, True)
     lane8 = lane_of((ROWS, X))
+    row8 = row_of((ROWS, X))
 
     def widen(value, at, cell):
         moved = roll(value, (at % LANES) - cell, 1)
         wide = jnp.concatenate([moved] * (X // LANES), axis=1)
         return jnp.where(lane8 == at, wide, 0.0)
 
+    def at_row(row, values, cz):
+        total = values[cz * RATIO : (cz + 1) * RATIO].sum(axis=0, keepdims=True)
+        return jnp.where(row8 == row, jnp.broadcast_to(total, (ROWS, X)), 0.0)
+
+    items = []
     for cz in range(g.cz):
         cell = cz * RATIO * DEPTH
-        x_low = widen(low_w, 0, cell)
-        x_high = widen(high_w, X - 1, cell + DEPTH - 1)
-        f_low = widen(low_f, 0, cell)
-        f_high = widen(high_f, X - 1, cell + DEPTH - 1)
-        out[0, cz] = sums[0, cz] - (f_low - f_high)
-        out[1, cz] = sums[1, cz] + x_low + x_high
-        out[2, cz] = sums[2, cz]
-        out[3, cz] = sums[3, cz]
-        out[4, cz] = sums[4, cz] + x_low
-
-    for q, dst in enumerate((xp, xk, xs)):
-        for z in range(Z):
-            block, at = g.slot(q, z)
-            hi = roll(xh[block], -at, 1)
-            lo = roll(xl[block], -at - DEPTH, 1)
-            dst[z] = strip_tile(hi, lo)
-
-
-def weights_kernel(g, k, xk, after, fz, fy, fx, dinv, token):
-    token[...] = jnp.zeros((ROWS, LANES), F32)
-    Z = g.Z
-
-    def k_at(z):
-        return jnp.concatenate([k[z], xk[z]], axis=1)
-
-    fy[0], fx[0], _ = side_faces(k_at(0))
-    fz[1] = face(k_at(1), k_at(0))
-
-    def body(z, carry):
-        kz = k_at(z)
-        above = face(k_at(z + 1), kz)
-        fz[z + 1] = above
-        wy, wx, total = side_faces(kz)
-        fy[z] = wy
-        fx[z] = wx
-        dinv[z] = scale_of(kz, total + fz[z] + above)
-        return carry
-
-    lax.fori_loop(1, Z - 1, body, 0)
-    fy[Z - 1], fx[Z - 1], _ = side_faces(k_at(Z - 1))
-
-
-def restrict_kernel(g, *refs):
-    p, k, sums = refs[:3]
-    n = 3
-    near = refs[n : n + g.zsides]
-    n += g.zsides
-    y_in = refs[n : n + g.ysides]
-    n += g.ysides
-    out = refs[n + 1]
-    zi, yi, xi = g.where()
-    Z, Y, X = g.Z, g.Y, g.X
-    half = Z // 2
-    row8 = row_of((ROWS, X))
-    p0, k0 = (from_low(zi, g.nz, near, lambda r, q=q: r[q]) for q in range(2))
-    w = face(k0, k[0])
-    low_wz, low_fz = group_rows(w), group_rows(w * (p[0] - p0))
-    p1, k1 = (from_high(zi, g.nz, near, lambda r, q=q: r[q]) for q in range(2))
-    w = face(k[Z - 1], k1)
-    top_wz, top_fz = group_rows(w), group_rows(w * (p1 - p[Z - 1]))
-    items = []
-    for cz in range(g.cz):
-        low_w = low_f = top_w = top_f = jnp.zeros((1, X), F32)
-        for z in range(cz * RATIO, (cz + 1) * RATIO):
-            at = (z % 2) * DEPTH
-            below, above = [], []
-            for q in range(2):
-                block = q * half + z // 2
-                row = at + DEPTH - 1
-                below.append(from_low(yi, g.ny, y_in, lambda r: r[block, row : row + 1, :]))
-                above.append(from_high(yi, g.ny, y_in, lambda r: r[block, at : at + 1, :]))
-            kz, pz = k[z, 0:1, :], p[z, 0:1, :]
-            w = face(kz, below[1])
-            low_w = low_w + w
-            low_f = low_f + w * (pz - below[0])
-            kz, pz = k[z, Y - 1 :, :], p[z, Y - 1 :, :]
-            w = face(kz, above[1])
-            top_w = top_w + w
-            top_f = top_f + w * (above[0] - pz)
-
-        def at_row(row, value):
-            return jnp.where(row8 == row, jnp.broadcast_to(value, (ROWS, X)), 0.0)
-
-        low_wy = at_row(0, low_w)
-        rhs = sums[0, cz] - at_row(0, low_f) + at_row(g.cy - 1, top_f)
-        diagonal = sums[1, cz] + low_wy + at_row(g.cy - 1, top_w)
+        x_low = widen(low_wx, 0, cell)
+        y_low = at_row(0, low_wy, cz)
+        rhs = sums[0, cz] - at_row(0, low_fy, cz) + at_row(g.cy - 1, top_fy, cz)
+        rhs = rhs - widen(low_fx, 0, cell) + widen(top_fx, X - 1, cell + DEPTH - 1)
+        diagonal = sums[1, cz] + y_low + at_row(g.cy - 1, top_wy, cz)
+        diagonal = diagonal + x_low + widen(top_wx, X - 1, cell + DEPTH - 1)
         wz = sums[2, cz]
         if cz == 0:
             rhs = rhs - low_fz
@@ -461,7 +460,7 @@
         if cz == g.cz - 1:
             rhs = rhs + top_fz
             diagonal = diagonal + top_wz
-        items.append([rhs, diagonal, wz, sums[3, cz] + low_wy, sums[4, cz]])
+        items.append([rhs, diagonal, wz, sums[3, cz] + y_low, sums[4, cz] + x_low])
     items = [items[cz][q] for q in range(5) for cz in range(g.cz)]
     onehot = (
         lax.broadcasted_iota(jnp.int32, (X, LANES), 0) // RATIO
@@ -486,14 +485,23 @@
 
         def fill(top, out=out):
             first = Z - DEPTH if top else 0
+            pieces = []
             for q in range(3):
                 for d in range(DEPTH):
-                    part = row_halo(g, hy, ly, q, first + d)
-                    for half_lane in range(X // LANES):
-                        out[(q * DEPTH + d) * (X // LANES) + half_lane] = part[
-                            :, half_lane * LANES : (half_lane + 1) * LANES
-                        ]
-            at_block = 3 * DEPTH * (X // LANES)
+                    count = relay_rows(q, d)
+                    if count:
+                        part = row_halo(g, hy, ly, q, Z - 1 - d if top else d)
+                        pieces += [part[:count], part[ROWS - count :]]
+            missing = relay_tiles() * ROWS - sum(piece.shape[0] for piece in pieces)
+            if missing:
+                pieces.append(jnp.zeros((missing, X), F32))
+            packed = jnp.concatenate(pieces, axis=0)
+            for tile in range(relay_tiles()):
+                for part in range(X // LANES):
+                    out[tile * (X // LANES) + part] = packed[
+                        tile * ROWS : (tile + 1) * ROWS, part * LANES : (part + 1) * LANES
+                    ]
+            at_block = relay_tiles() * (X // LANES)
             wide = lane_of((g.YE, LANES))
             acc = jnp.zeros((g.YE, LANES), F32)
             span = DEPTH * DEPTH
@@ -512,8 +520,17 @@
     return -(-5 * g.cz // per)
 
 
+def relay_rows(q, d):
+    return max(0, DEPTH - 1 - d - (q == 2))
+
+
+def relay_tiles():
+    rows = sum(2 * relay_rows(q, d) for q in range(3) for d in range(DEPTH))
+    return -(-rows // ROWS)
+
+
 def relay_blocks(g):
-    return 3 * DEPTH * (g.X // LANES) + g.YE // ROWS
+    return relay_tiles() * (g.X // LANES) + g.YE // ROWS
 
 
 def strip_tile(hi, lo):
@@ -617,12 +634,36 @@
     return z + DEPTH if z < DEPTH else z - g.Z + 3 * DEPTH
 
 
-def face_at(g, z):
-    return z + DEPTH - 1 if z <= 0 else z - g.Z + DEPTH
-
-
-def scale_at(g, z):
-    return z + DEPTH - 1 if z <= 0 else z - g.Z + 1 + DEPTH
+def either(top, high, low):
+    return (high if top else low) if isinstance(top, bool) else jnp.where(top, high, low)
+
+
+def halo_at(top, d):
+    return either(top, 3 * DEPTH + d, DEPTH - 1 - d)
+
+
+def face_at(top, d):
+    return either(top, DEPTH + d, DEPTH - 1 - d)
+
+
+def scale_at(top, d):
+    return either(top, DEPTH + 1 + d, DEPTH - 2 - d)
+
+
+def on_sides(g, zi, act):
+    if g.zsides == 1:
+        act(zi == 0)
+    else:
+        pl.when(zi < g.nz - 1)(functools.partial(act, True))
+        pl.when(zi > 0)(functools.partial(act, False))
+
+
+def on_ends(g, zi, act):
+    if g.zsides == 1:
+        act(zi != 0)
+    else:
+        pl.when(zi == g.nz - 1)(functools.partial(act, True))
+        pl.when(zi == 0)(functools.partial(act, False))
 
 
 def own_weights(refs):
@@ -650,64 +691,83 @@
     rest = DEPTH - 1
     zero = jnp.zeros((g.YE, g.XE), F32)
 
-    def k_at(z):
-        return own_k[z] if 0 <= z < Z else kh[beyond(g, z)]
-
     def own_faces(z):
         wy, wx = fy[z], fx[z]
         return wy + roll(wy, -1, 0) + wx + roll(wx, -1, 1)
 
-    def fill(top, side):
-        strip = relay[side][3 * DEPTH * parts :].reshape(g.YE, LANES)
+    def fill(top):
+        def received(bufs, at):
+            if len(bufs) == 1:
+                return bufs[0][at]
+            return jnp.where((zi % 2 == 0) == top, bufs[0][at], bufs[1][at])
+
+        count = relay_tiles() * parts
+        tiles = [received(relay, i) for i in range(relay_blocks(g))]
+        strip = jnp.concatenate(tiles[count:], axis=0)
+        packed = jnp.concatenate(
+            [
+                jnp.concatenate(tiles[i : i + parts], axis=1)
+                for i in range(0, count, parts)
+            ],
+            axis=0,
+        )
+        start = 0
         for q, out in enumerate((ph, kh, sh)):
-            for d in range(DEPTH):
-                at = beyond(g, Z + d if top else d - DEPTH)
-                if q < 2 and d == (0 if top else rest):
-                    plane = near[side][q]
-                elif q < 2:
-                    plane = deep[side][q * rest + (d - 1 if top else d)]
-                elif d == (rest if top else 0):
-                    continue
+            for d in range(DEPTH if q < 2 else rest):
+                at = halo_at(top, d)
+                layer = either(top, d, rest - d)
+                if q == 2:
+                    plane = received(deep, 2 * rest + either(top, d, rest - 1 - d))
+                elif d == 0:
+                    plane = received(near, q)
                 else:
-                    plane = deep[side][q * rest + (d if top else d - 1)]
+                    plane = received(deep, q * rest + either(top, d - 1, rest - d))
                 out[at, :Y, :X] = plane
-                for part in range(parts):
-                    lanes = slice(part * LANES, (part + 1) * LANES)
-                    out[at, Y:, lanes] = relay[side][(q * DEPTH + d) * parts + part]
-                hi = roll(strip, -(q * DEPTH + d) * DEPTH, 1)
-                lo = roll(strip, -((3 + q) * DEPTH + d) * DEPTH - DEPTH, 1)
+                used = relay_rows(q, d)
+                if used:
+                    rows = [packed[start : start + used], packed[start + used : start + 2 * used]]
+                    if 2 * used < ROWS:
+                        rows.insert(1, jnp.zeros((ROWS - 2 * used, X), F32))
+                    out[at, Y:, :X] = jnp.concatenate(rows, axis=0)
+                    start += 2 * used
+                else:
+                    out[at, Y:, :X] = jnp.zeros((ROWS, X), F32)
+                hi = turn(strip, -(q * DEPTH + layer) * DEPTH)
+                lo = turn(strip, -((3 + q) * DEPTH + layer) * DEPTH - DEPTH)
                 out[at, :, X:] = strip_tile(hi, lo)
-        z = Z - 1 if top else 0
-        step = 1 if top else -1
-        kz = k_at(z)
-        outer = face(k_at(z + step), kz)
-        hz[face_at(g, z + 1 if top else z)] = outer
-        inner = fz[z if top else z + 1]
-        hd[scale_at(g, z)] = scale_of(kz, own_faces(z) + inner + outer)
-        for _ in range(DEPTH - 1):
-            z += step
+        z = either(top, Z - 1, 0)
+        kz = own_k[z]
+        beyond_k = kh[halo_at(top, 0)]
+        outer = face(beyond_k, kz)
+        hz[face_at(top, 0)] = outer
+        inner = fz[either(top, Z - 1, 1)]
+        hd[scale_at(top, -1)] = scale_of(kz, own_faces(z) + inner + outer)
+        for d in range(DEPTH - 1):
             inner = outer
-            kz = k_at(z)
-            outer = face(k_at(z + step), kz)
-            hz[face_at(g, z + 1 if top else z)] = outer
+            kz = beyond_k
+            beyond_k = kh[halo_at(top, d + 1)]
+            outer = face(beyond_k, kz)
+            hz[face_at(top, d + 1)] = outer
             wy, wx, total = side_faces(kz)
-            hy[beyond(g, z)] = wy
-            hx[beyond(g, z)] = wx
-            hd[scale_at(g, z)] = scale_of(kz, total + inner + outer)
-
-    def boundary(top):
-        z = Z - 1 if top else 0
-        kz = k_at(z)
-        ph[beyond(g, z + 1 if top else z - 1)] = zero
-        hz[face_at(g, z + 1 if top else z)] = kz
-        hd[scale_at(g, z)] = scale_of(kz, own_faces(z) + fz[z if top else z + 1] + kz)
-
-    for side in range(g.zsides):
-        above = (zi % 2) == side
-        pl.when(above & (zi < g.nz - 1))(functools.partial(fill, True, side))
-        pl.when(jnp.logical_not(above) & (zi > 0))(functools.partial(fill, False, side))
-    pl.when(zi == 0)(functools.partial(boundary, False))
-    pl.when(zi == g.nz - 1)(functools.partial(boundary, True))
+            hy[halo_at(top, d)] = wy
+            hx[halo_at(top, d)] = wx
+            hd[scale_at(top, d)] = scale_of(kz, total + inner + outer)
+
+    def end(top):
+        z = either(top, Z - 1, 0)
+        kz = own_k[z]
+        ph[halo_at(top, 0)] = zero
+        hz[face_at(top, 0)] = kz
+        hd[scale_at(top, -1)] = scale_of(kz, own_faces(z) + fz[either(top, Z - 1, 1)] + kz)
+
+    on_sides(g, zi, fill)
+    on_ends(g, zi, end)
+
+
+def turn(values, shift):
+    if isinstance(shift, int):
+        return roll(values, shift, 1)
+    return pltpu.roll(values, lax.rem(shift + 8 * LANES, LANES), 1)
 
 
 def sweep_kernel(g, sweep, inside, *refs):
@@ -727,12 +787,7 @@
     if not inside:
         vh, sh, hz, hy, hx, hd = refs[n : n + 6]
         n += 6
-    if final and inside:
-        out = refs[n]
-    elif final:
-        earlier, out = refs[n : n + 2]
-    else:
-        out = refs[n]
+    out = refs[-2]
     refs[-1][...] = jnp.zeros((ROWS, LANES), F32)
     zi, yi, xi = g.where()
     reach = SWEEPS - sweep
@@ -745,7 +800,7 @@
 
     if inside:
 
-        def body(z, carry):
+        for z in range(sweep, Z - sweep):
             new = update(
                 v[z], v[z - 1], v[z + 1], own_s[z], fz[z], fz[z + 1], fy[z], fx[z], dinv[z]
             )
@@ -753,59 +808,56 @@
                 out[z] = new[: g.Y, : g.X]
             else:
                 out[z] = new
-            return carry
-
-        lax.fori_loop(sweep, Z - sweep, body, 0)
         return
 
     def v_at(z):
         return v[z] if sweep - 1 <= z <= Z - sweep else vh[beyond(g, z)]
 
     def z_face(z):
-        return fz[z] if 1 <= z < Z else hz[face_at(g, z)]
-
-    def edge(z):
-        own = 0 <= z < Z
-        at = beyond(g, z)
+        return fz[z] if 1 <= z < Z else hz[face_at(z >= Z, 0)]
+
+    def own_edge(z):
         new = update(
             v_at(z),
             v_at(z - 1),
             v_at(z + 1),
-            own_s[z] if own else sh[at],
+            own_s[z],
             z_face(z),
             z_face(z + 1),
-            fy[z] if own else hy[at],
-            fx[z] if own else hx[at],
-            dinv[z] if 0 < z < Z - 1 else hd[scale_at(g, z)],
+            fy[z],
+            fx[z],
+            dinv[z] if 0 < z < Z - 1 else hd[scale_at(z > 0, -1)],
         )
         if final:
-            out[z] = new[: g.Y, : g.X]
+            out[beyond(g, z) - DEPTH] = new[: g.Y, : g.X]
         else:
-            out[at] = new
+            out[beyond(g, z)] = new
+
+    def halo(top):
+        inner = v[either(top, Z - 1, 0)] if sweep == 1 else vh[halo_at(top, -1)]
+        vz = vh[halo_at(top, 0)]
+        for d in range(reach):
+            at = halo_at(top, d)
+            outer = vh[halo_at(top, d + 1)]
+            z_inner, z_outer = hz[face_at(top, d)], hz[face_at(top, d + 1)]
+            out[at] = update(
+                vz, inner, outer, sh[at], z_inner, z_outer, hy[at], hx[at], hd[scale_at(top, d)]
+            )
+            inner, vz = vz, outer
+
+    def clear(top):
+        out[halo_at(top, 0)] = jnp.zeros((g.YE, g.XE), F32)
 
     for z in range(sweep):
-        edge(z)
-        edge(Z - 1 - z)
+        own_edge(z)
+        own_edge(Z - 1 - z)
     if final:
-        for z in range(sweep, Z - sweep):
-            out[z] = earlier[z]
         return
-    zero = jnp.zeros((g.YE, g.XE), F32)
-
-    def halo(layers):
-        for z in layers:
-            edge(z)
-
-    def clear(z):
-        out[beyond(g, z)] = zero
-
-    pl.when(zi > 0)(functools.partial(halo, range(-reach, 0)))
-    pl.when(zi < g.nz - 1)(functools.partial(halo, range(Z, Z + reach)))
-    pl.when(zi == 0)(functools.partial(clear, -1))
-    pl.when(zi == g.nz - 1)(functools.partial(clear, Z))
-
-
-def solve_kernel(g, gathered, fine, out):
+    on_sides(g, zi, halo)
+    on_ends(g, zi, clear)
+
+
+def solve_kernel(g, gathered, fine, edges, out):
     zi, yi, xi = g.where()
     per = LANES // g.cx
     group = lane_of((ROWS, LANES)) // g.cx
@@ -890,7 +942,10 @@
         block = wide[cz * ROWS : (cz + 1) * ROWS]
         spread = jnp.broadcast_to(block[:, None, :], (g.cy, RATIO, g.X)).reshape(g.Y, g.X)
         for z in range(cz * RATIO, (cz + 1) * RATIO):
-            out[z] = fine[z] + spread
+            if DEPTH <= z < g.Z - DEPTH:
+                out[z] = fine[z] + spread
+            else:
+                out[z] = edges[beyond(g, z) - DEPTH] + spread
 
 
 def merge_kernel(cells, got, token, out):
@@ -930,22 +985,32 @@
         functools.partial(pack_kernel, g),
         [(Z, Y, X)] * 3
         + [(2, Y, X)] * g.zsides
-        + [x_shape] * g.xsides,
+        + [x_shape] * g.xsides
+        + [(2, Z, X)] * g.ysides,
         [pressure_start, permeability, source],
         scratch=[pltpu.SemaphoreType.DMA((3 + 2 * g.zsides,))],
         name="pack_faces",
         far=True,
     )
     sent = list(sent)
-    (p, k, s), near, x_sent = sent[:3], sent[3 : 3 + g.zsides], sent[3 + g.zsides :]
+    (p, k, s), near, sent = sent[:3], sent[3 : 3 + g.zsides], sent[3 + g.zsides :]
+    x_sent, row_sent = sent[: g.xsides], sent[g.xsides :]
     near_got = exchange(near, "gx", g.nz, "gz")
     x_got = exchange(x_sent, "gz", g.nx)
-    sums, token = run(
+    row_got = exchange(row_sent, "gy", g.ny, "gz")
+    sums, token_l = run(
         functools.partial(local_kernel, g),
         [sums_shape, tile],
         [p, k, s],
         us=US["local"],
         name="local_sums",
+    )
+    cells, token = run(
+        functools.partial(restrict_kernel, g),
+        [(1, coarse_blocks(g)) + tile, tile],
+        [p, k, sums] + near_got + row_got + row_sent + x_got + x_sent,
+        us=US["restrict"],
+        name="restrict",
     )
     y_sent = run(
         functools.partial(pack_rows_kernel, g),
@@ -955,10 +1020,10 @@
         name="pack_rows",
     )
     y_got = exchange(y_sent, "gy", g.ny, "gz")
-    sums, xp, xk, xs, token = run(
+    xp, xk, xs, token = run(
         functools.partial(side_kernel, g),
-        [sums_shape] + [(Z, Y, LANES)] * 3 + [tile],
-        [p, k, s, sums] + x_got + x_sent + list(y_sent),
+        [(Z, Y, LANES)] * 3 + [tile],
+        x_got + [y_sent[0]],
         scratch=[pltpu.VMEM(x_shape, F32)] * 2,
         us=US["side"],
         name="side",
@@ -966,31 +1031,24 @@
     deep = run(
         functools.partial(deep_kernel, g),
         [(3 * (DEPTH - 1), Y, X)] * g.zsides,
-        [p, k, s, token],
+        [p, k, s, token_l] + near_got + row_got + x_got,
         us=0.1,
         name="pack_deep",
     )
     deep_got = exchange(deep, "gx", g.nz, "gz")
-    fz, fy, fx, dinv, token = run(
+    fz, fy, fx, dinv, token_w = run(
         functools.partial(weights_kernel, g),
         [main] * 4 + [tile],
         [k, xk, token],
         us=US["weights"],
         name="weights",
     )
-    (cells,) = run(
-        functools.partial(restrict_kernel, g),
-        [(1, coarse_blocks(g)) + tile],
-        [p, k, sums] + near_got + list(y_got) + [token],
-        us=US["restrict"],
-        name="restrict",
-    )
     rows = (Z, ROWS, g.XE)
     halo_scratch = [pltpu.VMEM(y_shape, F32)] * 2 + [pltpu.VMEM((g.blocks, g.YE, LANES), F32)] * 2
     extended = run(
         functools.partial(extend_kernel, g),
         [rows] * 5 + [(Z, 2 * ROWS, g.XE), (Z, 3 * ROWS, g.XE), tile] + [(nr,) + tile] * g.zsides,
-        [k, xk, fz, fy, fx] + list(y_got) + x_got + [cells],
+        [k, xk, fz, fy, fx] + list(y_got) + x_got + [token_w],
         scratch=halo_scratch,
         us=US["extend"],
         name="extend",
@@ -1007,7 +1065,7 @@
         v, token = run(
             functools.partial(sweep_kernel, g, sweep, True),
             [(Z, Y, X) if sweep == SWEEPS else own, tile],
-            common + inner[-1],
+            common + inner[-1] + (relay[:1] if sweep == 3 else []),
             us=US["sweep"] * (Z - 2 * sweep) / Z,
             name=f"inner_{sweep}",
         )
@@ -1025,8 +1083,8 @@
         final = sweep == SWEEPS
         vh, token = run(
             functools.partial(sweep_kernel, g, sweep, False),
-            [(Z, Y, X) if final else far, tile],
-            common + inner[sweep - 1] + [vh, sh, hz, hy, hx, hd] + (inner[sweep] if final else []),
+            [(2 * DEPTH, Y, X) if final else far, tile],
+            common + inner[sweep - 1] + [vh, sh, hz, hy, hx, hd],
             us=US["outer"],
             name=f"outer_{sweep}",
         )
@@ -1039,7 +1097,7 @@
     (out,) = run(
         functools.partial(solve_kernel, g),
         [(Z, Y, X)],
-        [cells, vh],
+        [cells, v, vh],
         us=US["solve"],
         name="solve",
         spaces=[jax.ShapeDtypeStruct((Z, Y, X), F32)],

time: 43.8 us -> 39.7 us (0.906)
  waiting for transfers between devices: 2.81 us -> 0.06 us
  Pallas kernels: 22.7 us -> 20.3 us
  starting transfers between devices: 18 us -> 19 us
    pallas_call x23, Pallas kernels: 22.7 us -> 20.3 us  [run(): pl.pallas_call(kernel, out_shape=shapes, in_specs=[pl.BlockSpec(memory_sp...]
    ppermute x5, starting transfers between devices: 9 us -> 6.86 us  [shards(): got = lax.ppermute(cells, axis, flips(lax.axis_size(axis), bit))]
    ppermute x1 -> x2, starting transfers between devices: 1.26 us -> 2.87 us  [exchange(): got.append(lax.ppermute(bufs[1], (axis, beside), perm))]
    ppermute x1, waiting for transfers between devices: 1.58 us -> 0.01 us  [exchange(): got.append(lax.ppermute(bufs[1], axis, pairs(count, 1)))]
    ppermute x5 -> x6, starting transfers between devices: 6.62 us -> 8.16 us  [exchange(): got = [lax.ppermute(bufs[0], axis, pairs(count, 0))]]
    ppermute x5, waiting for transfers between devices: 1.21 us -> 0.03 us  [shards(): got = lax.ppermute(cells, axis, flips(lax.axis_size(axis), bit))]
  transfers between devices with their start and end apart: 12 -> 14, of which waited for: 2 -> 0; matrix products, arithmetic and copies ran while one was open for 0% -> 0% of each run, Pallas kernels for 39% -> 40%
where the time goes in v4:
time: 39.7 us; the launch traced here: 39.6 us
  Pallas kernels  20.3 us (51%)
  starting transfers between devices  19 us (48%)
    pallas_call x23, Pallas kernels, run(): pl.pallas_call(kernel, out_shape=shapes, in_specs=[pl.BlockSpec(memory_sp...  20.3 us
    ppermute x6, starting transfers between devices, exchange(): got = [lax.ppermute(bufs[0], axis, pairs(count, 0))]  8.16 us
    ppermute x5, starting transfers between devices, shards(): got = lax.ppermute(cells, axis, flips(lax.axis_size(axis), bit))  6.86 us
    ppermute x2, starting transfers between devices, exchange(): got.append(lax.ppermute(bufs[1], (axis, beside), perm))  2.87 us
    ppermute x1, starting transfers between devices, exchange(): got.append(lax.ppermute(bufs[1], axis, pairs(count, 1)))  1.13 us
  transfers between devices with their start and end apart: 14, of which 0 were waited for; matrix products, arithmetic and copies ran while one was open for 0% of the time, Pallas kernels for 40%

profile of v4, /device:TPU:1, one launch (start us, length us, event | category | flops | bytes accessed | tf_op | source)
XLA Modules:
  0.0 39.6 jit_solution(10714626884491224439)
XLA Ops:
  0.0 2.3 %pack_faces.1 = (f32[16,64,256]{2,1,0:T(8,128)S(1)}, f32[16,64,256]{2,1,0:T(8,128)S(1)}, f32[16,64,256]{2,1,0:T(8,128)S(1)}, f32[2,64,256]{2,1,0:T(8,128)S(1)}, ...) custom-call(f32[16,64,256]{2,1,0:T(8,128)} %refs_0_.1, ...), custom_call_target="tpu_custom_call" | custom-call | flops 1000 | bytes 3500000 | tf_op jit(solution)/shard_map/pack_faces/pallas_call | solution.py:57
  2.3 2.1 %collective-permute-start = (f32[2,64,256]{2,1,0:T(8,128)S(1)}, f32[2,64,256]{2,1,0:T(8,128)S(1)}, u32[]{:S(2)}, u32[]{:S(2)}) collective-permute-start(f32[2,64,256]{2,1,0:T(8,128)S(1)} %get-tuple-element.60), channel_id=1, source_target_pairs={{0,16},{16,0},{1,17},{17,1},{2,18},{18,2},{3,19},{19,3},{4,20},{20... | collective-permute-start | bytes 393224 | tf_op jit(solution)/shard_map/ppermute | solution.py:964
  4.4 1.0 %collective-permute-start.3 = (f32[2,64,128]{2,1,0:T(8,128)S(1)}, f32[2,64,128]{2,1,0:T(8,128)S(1)}, u32[]{:S(2)}, u32[]{:S(2)}) collective-permute-start(f32[2,64,128]{2,1,0:T(8,128)S(1)} %get-tuple-element.63.refs_10_), channel_id=1, source_target_pairs={{0,1},{1,0},{2,3},{3,2},{4,5},{5,4},{6,7},{7,6},{8,9},{9,8},{10,11... | collective-permute-start | bytes 196616 | tf_op jit(solution)/shard_map/ppermute | solution.py:964
  5.4 1.1 %collective-permute-start.4 = (f32[2,64,128]{2,1,0:T(8,128)S(1)}, f32[2,64,128]{2,1,0:T(8,128)S(1)}, u32[]{:S(2)}, u32[]{:S(2)}) collective-permute-start(f32[2,64,128]{2,1,0:T(8,128)S(1)} %get-tuple-element.64.refs_11_), channel_id=1, source_target_pairs={{1,2},{2,1},{3,0},{0,3},{5,6},{6,5},{7,4},{4,7},{9,10},{10,9},{11,... | collective-permute-start | bytes 196616 | tf_op jit(solution)/shard_map/ppermute | solution.py:967
  6.5 1.3 %collective-permute-start.1 = (f32[2,16,256]{2,1,0:T(8,128)S(1)}, f32[2,16,256]{2,1,0:T(8,128)S(1)}, u32[]{:S(2)}, u32[]{:S(2)}) collective-permute-start(f32[2,16,256]{2,1,0:T(8,128)S(1)} %get-tuple-element.61.refs_6_), channel_id=1, source_target_pairs={{0,4},{4,0},{8,12},{12,8},{1,5},{5,1},{9,13},{13,9},{2,6},{6,2},{1... | collective-permute-start | bytes 98312 | tf_op jit(solution)/shard_map/ppermute | solution.py:964
  7.8 0.8 %collective-permute-start.2 = (f32[2,16,256]{2,1,0:T(8,128)S(1)}, f32[2,16,256]{2,1,0:T(8,128)S(1)}, u32[]{:S(2)}, u32[]{:S(2)}) collective-permute-start(f32[2,16,256]{2,1,0:T(8,128)S(1)} %get-tuple-element.62.refs_7_), channel_id=1, source_target_pairs={{0,1},{1,0},{2,3},{3,2},{4,8},{5,9},{6,10},{7,11},{8,4},{9,5},{10,... | collective-permute-start | bytes 98312 | tf_op jit(solution)/shard_map/ppermute | solution.py:970
  8.6 1.0 %local_sums.1 = (f32[5,2,8,256]{3,2,1,0:T(8,128)S(1)}, f32[8,128]{1,0:T(8,128)S(1)}) custom-call(f32[16,64,256]{2,1,0:T(8,128)S(1)} %get-tuple-element.56.p.refs_0_.refs_11_, f32[16,64,256]{2,1,0:T(8,128)S(1)} %get-tuple-element.57.k.refs_1_.refs_0_, f32[16,64,256]{2,1,0:T(8,128)S(1)} %get-tuple-element.58.s.refs_2_.refs_0_), custom_call_target="tpu_custom_call" | custom-call | flops 1000 | bytes 4200000 | tf_op jit(solution)/shard_map/local_sums/pallas_call | solution.py:57
  10.8 2.3 %collective-permute-start.6 = (f32[25,8,256]{2,1,0:T(8,128)S(1)}, f32[25,8,256]{2,1,0:T(8,128)S(1)}, u32[]{:S(2)}, u32[]{:S(2)}) collective-permute-start(f32[25,8,256]{2,1,0:T(8,128)S(1)} %get-tuple-element.67.refs_2_), channel_id=1, source_target_pairs={{0,4},{4,0},{8,12},{12,8},{1,5},{5,1},{9,13},{13,9},{2,6},{6,2},{1... | collective-permute-start | bytes 614408 | tf_op jit(solution)/shard_map/ppermute | solution.py:964
  13.1 2.1 %collective-permute-start.7 = (f32[25,8,256]{2,1,0:T(8,128)S(1)}, f32[25,8,256]{2,1,0:T(8,128)S(1)}, u32[]{:S(2)}, u32[]{:S(2)}) collective-permute-start(f32[25,8,256]{2,1,0:T(8,128)S(1)} %get-tuple-element.74), channel_id=1, source_target_pairs={{0,1},{1,0},{2,3},{3,2},{4,8},{5,9},{6,10},{7,11},{8,4},{9,5},{10,... | collective-permute-start | bytes 614408 | tf_op jit(solution)/shard_map/ppermute | solution.py:970
  15.2 0.9 %side.1 = (f32[16,64,128]{2,1,0:T(8,128)S(1)}, f32[16,64,128]{2,1,0:T(8,128)S(1)}, f32[16,64,128]{2,1,0:T(8,128)S(1)}, f32[8,128]{1,0:T(8,128)S(1)}) custom-call(f32[2,64,128]{2,1,0:T(8,128)S(1)} %collective-permute-done.3.refs_8_.refs_3_.refs_0_.refs_7_.refs_4_, f32[2,64,128]{2,1,0:T(8,128)S(1)} %collective-permute-done.4.refs_9_.refs_4_.refs_1_.refs_8_.refs_5_, ...), custom_call_target="tpu_custom_call" | custom-call | flops 1000 | bytes 2800000 | tf_op jit(solution)/shard_map/side/pallas_call | solution.py:57
  16.0 1.8 %weights.1 = (f32[16,64,384]{2,1,0:T(8,128)S(1)}, f32[16,64,384]{2,1,0:T(8,128)S(1)}, f32[16,64,384]{2,1,0:T(8,128)S(1)}, f32[16,64,384]{2,1,0:T(8,128)S(1)}, f32[8,128]{1,0:T(8,128)S(1)}) custom-call(f32[16,64,256]{2,1,0:T(8,128)S(1)} %get-tuple-element.57.k.refs_1_.refs_0_, f32[16,64,128]{2,1,0:T(8,128)S(1)} %get-tuple-element.69.xk.refs_1_, ...), custom_call_target="tpu_custom_call" | custom-call | flops 1000 | bytes 11200000 | tf_op jit(solution)/shard_map/weights/pallas_call | solution.py:57
  17.9 1.1 %extend.1 = (f32[16,8,384]{2,1,0:T(8,128)S(1)}, f32[16,8,384]{2,1,0:T(8,128)S(1)}, f32[16,8,384]{2,1,0:T(8,128)S(1)}, f32[16,8,384]{2,1,0:T(8,128)S(1)}, f32[16,...) custom-call(f32[16,64,256]{2,1,0:T(8,128)S(1)} %get-tuple-element.57, ...), custom_call_target="tpu_custom_call" | custom-call | flops 1000 | bytes 3500000 | tf_op jit(solution)/shard_map/extend/pallas_call | solution.py:57
  19.0 1.8 %inner_1.1 = (f32[16,72,384]{2,1,0:T(8,128)S(1)}, f32[8,128]{1,0:T(8,128)S(1)}) custom-call(f32[16,64,256]{2,1,0:T(8,128)S(1)} %get-tuple-element.58.s.refs_2_.refs_0_, f32[16,64,128]{2,1,0:T(8,128)S(1)} %get-tuple-element.68.refs_1_, f32[16,8,384]{2,1,0:T(8,128)S(1)} %get-tuple-element.76.refs_2_, f32[16,64,384]{2,1,0:T(8,128)S(1)} %get-tuple-element.71.refs_2_.refs_3_, ...), custom_call_target="tpu_custom_call" | custom-call | flops 1000 | bytes 6737500 | tf_op jit(solution)/shard_map/inner_1/pallas_call | solution.py:57
  21.1 1.2 %collective-permute-start.10 = (f32[17,8,128]{2,1,0:T(8,128)S(1)}, f32[17,8,128]{2,1,0:T(8,128)S(1)}, u32[]{:S(2)}, u32[]{:S(2)}) collective-permute-start(f32[17,8,128]{2,1,0:T(8,128)S(1)} %get-tuple-element.88), channel_id=1, source_target_pairs={{0,16},{16,0},{1,17},{17,1},{2,18},{18,2},{3,19},{19,3},{4,20},{20... | collective-permute-start | bytes 208904 | tf_op jit(solution)/shard_map/ppermute | solution.py:964
  22.3 1.5 %inner_2.1 = (f32[16,72,384]{2,1,0:T(8,128)S(1)}, f32[8,128]{1,0:T(8,128)S(1)}) custom-call(f32[16,64,256]{2,1,0:T(8,128)S(1)} %get-tuple-element.58.s.refs_2_.refs_0_, f32[16,64,128]{2,1,0:T(8,128)S(1)} %get-tuple-element.68.refs_1_, f32[16,8,384]{2,1,0:T(8,128)S(1)} %get-tuple-element.76.refs_2_, f32[16,64,384]{2,1,0:T(8,128)S(1)} %get-tuple-element.71.refs_2_.refs_3_, ...), custom_call_target="tpu_custom_call" | custom-call | flops 1000 | bytes 5775000 | tf_op jit(solution)/shard_map/inner_2/pallas_call | solution.py:57
  23.8 2.9 %collective-permute-start.9 = (f32[4,3,8,128]{3,2,1,0:T(8,128)S(1)}, f32[4,3,8,128]{3,2,1,0:T(8,128)S(1)}, u32[]{:S(2)}, u32[]{:S(2)}) collective-permute-start(f32[4,3,8,128]{3,2,1,0:T(8,128)S(1)} %merge.6.cells), channel_id=1, source_target_pairs={{0,4},{4,0},{8,12},{12,8},{1,5},{5,1},{9,13},{13,9},{2,6},{6,2},{1... | collective-permute-start | bytes 147464 | tf_op jit(solution)/shard_map/ppermute | solution.py:1095
  26.8 1.2 %inner_3.1 = (f32[16,72,384]{2,1,0:T(8,128)S(1)}, f32[8,128]{1,0:T(8,128)S(1)}) custom-call(f32[16,64,256]{2,1,0:T(8,128)S(1)} %get-tuple-element.58.s.refs_2_.refs_0_, f32[16,64,128]{2,1,0:T(8,128)S(1)} %get-tuple-element.68.refs_1_, f32[16,8,384]{2,1,0:T(8,128)S(1)} %get-tuple-element.76.refs_2_, f32[16,64,384]{2,1,0:T(8,128)S(1)} %get-tuple-element.71.refs_2_.refs_3_, ...), custom_call_target="tpu_custom_call" | custom-call | flops 1000 | bytes 4812500 | tf_op jit(solution)/shard_map/inner_3/pallas_call | solution.py:57
  28.6 1.0 %collective-permute-start.11 = (f32[8,3,8,128]{3,2,1,0:T(8,128)S(1)}, f32[8,3,8,128]{3,2,1,0:T(8,128)S(1)}, u32[]{:S(2)}, u32[]{:S(2)}) collective-permute-start(f32[8,3,8,128]{3,2,1,0:T(8,128)S(1)} %merge.7.cells), channel_id=1, source_target_pairs={{0,16},{16,0},{1,17},{17,1},{2,18},{18,2},{3,19},{19,3},{4,20},{20... | collective-permute-start | bytes 294920 | tf_op jit(solution)/shard_map/ppermute | solution.py:1095
  29.6 1.3 %halo.1 = (f32[16,72,384]{2,1,0:T(8,128)S(1)}, f32[16,72,384]{2,1,0:T(8,128)S(1)}, f32[8,72,384]{2,1,0:T(8,128)S(1)}, f32[16,72,384]{2,1,0:T(8,128)S(1)}, f32[16...) custom-call(f32[16,64,256]{2,1,0:T(8,128)S(1)} %get-tuple-element.57.k.refs_1_.refs_0_, ...), custom_call_target="tpu_custom_call" | custom-call | flops 1000 | bytes 4900000 | tf_op jit(solution)/shard_map/halo/pallas_call | solution.py:57
  30.9 1.1 %outer_1.1 = (f32[16,72,384]{2,1,0:T(8,128)S(1)}, f32[8,128]{1,0:T(8,128)}) custom-call(f32[16,64,256]{2,1,0:T(8,128)S(1)} %get-tuple-element.58.s.refs_2_.refs_0_, f32[16,64,128]{2,1,0:T(8,128)S(1)} %get-tuple-element.68.refs_1_, f32[16,8,384]{2,1,0:T(8,128)S(1)} %get-tuple-element.76.refs_2_, f32[16,64,384]{2,1,0:T(8,128)S(1)} %get-tuple-element.71.refs_2_.refs_3_, ...), custom_call_target="tpu_custom_call" | custom-call | flops 1000 | bytes 2800000 | tf_op jit(solution)/shard_map/outer_1/pallas_call | solution.py:57
  32.8 2.6 %collective-permute-start.13 = (f32[16,3,8,128]{3,2,1,0:T(8,128)S(1)}, f32[16,3,8,128]{3,2,1,0:T(8,128)S(1)}, u32[]{:S(2)}, u32[]{:S(2)}) collective-permute-start(f32[16,3,8,128]{3,2,1,0:T(8,128)S(1)} %merge.8.cells), channel_id=1, source_target_pairs={{0,1},{1,0},{2,3},{3,2},{4,5},{5,4},{6,7},{7,6},{8,9},{9,8},{10,11... | collective-permute-start | bytes 589832 | tf_op jit(solution)/shard_map/ppermute | solution.py:1095
  35.4 0.8 %outer_3.1 = (f32[16,72,384]{2,1,0:T(8,128)S(1)}, f32[8,128]{1,0:T(8,128)S(1)}) custom-call(f32[16,64,256]{2,1,0:T(8,128)S(1)} %get-tuple-element.58.s.refs_2_.refs_0_, f32[16,64,128]{2,1,0:T(8,128)S(1)} %get-tuple-element.68.refs_1_, f32[16,8,384]{2,1,0:T(8,128)S(1)} %get-tuple-element.76.refs_2_, f32[16,64,384]{2,1,0:T(8,128)S(1)} %get-tuple-element.71.refs_2_.refs_3_, ...), custom_call_target="tpu_custom_call" | custom-call | flops 1000 | bytes 2800000 | tf_op jit(solution)/shard_map/outer_3/pallas_call | solution.py:57
  36.2 1.1 %outer_4.1 = (f32[8,64,256]{2,1,0:T(8,128)S(1)}, f32[8,128]{1,0:T(8,128)}) custom-call(f32[16,64,256]{2,1,0:T(8,128)S(1)} %get-tuple-element.58.s.refs_2_.refs_0_, f32[16,64,128]{2,1,0:T(8,128)S(1)} %get-tuple-element.68.refs_1_, f32[16,8,384]{2,1,0:T(8,128)S(1)} %get-tuple-element.76.refs_2_, f32[16,64,384]{2,1,0:T(8,128)S(1)} %get-tuple-element.71.refs_2_.refs_3_, ...), custom_call_target="tpu_custom_call" | custom-call | flops 1000 | bytes 2800000 | tf_op jit(solution)/shard_map/outer_4/pallas_call | solution.py:57
  37.4 2.2 %solve.1 = f32[16,64,256]{2,1,0:T(8,128)} custom-call(f32[32,3,8,128]{3,2,1,0:T(8,128)S(1)} %merge.9.gathered, f32[16,64,256]{2,1,0:T(8,128)S(1)} %get-tuple-element.104.fine, f32[8,64,256]{2,1,0:T(8,128)S(1)} %get-tuple-element.106.edges), custom_call_target="tpu_custom_call" | custom-call | flops 1000 | bytes 7700000 | tf_op jit(solution)/shard_map/solve/pallas_call | solution.py:57
  (27 shorter events, 3.0 us)
Async XLA Ops:
  2.3 7.3 %collective-permute-start = (f32[2,64,256]{2,1,0:T(8,128)S(1)}, f32[2,64,256]{2,1,0:T(8,128)S(1)}, u32[]{:S(2)}, u32[]{:S(2)}) collective-permute-start(f32[2,64,256]{2,1,0:T(8,128)S(1)} %get-tuple-element.60), channel_id=1, source_target_pairs={{0,16},{16,0},{1,17},{17,1},{2,18},{18,2},{3,19},{19,3},{4,20},{20... | collective-permute-start | bytes 393224 | tf_op jit(solution)/shard_map/ppermute | solution.py:964
  4.4 5.2 %collective-permute-start.3 = (f32[2,64,128]{2,1,0:T(8,128)S(1)}, f32[2,64,128]{2,1,0:T(8,128)S(1)}, u32[]{:S(2)}, u32[]{:S(2)}) collective-permute-start(f32[2,64,128]{2,1,0:T(8,128)S(1)} %get-tuple-element.63.refs_10_), channel_id=1, source_target_pairs={{0,1},{1,0},{2,3},{3,2},{4,5},{5,4},{6,7},{7,6},{8,9},{9,8},{10,11... | collective-permute-start | bytes 196616 | tf_op jit(solution)/shard_map/ppermute | solution.py:964
  5.4 4.2 %collective-permute-start.4 = (f32[2,64,128]{2,1,0:T(8,128)S(1)}, f32[2,64,128]{2,1,0:T(8,128)S(1)}, u32[]{:S(2)}, u32[]{:S(2)}) collective-permute-start(f32[2,64,128]{2,1,0:T(8,128)S(1)} %get-tuple-element.64.refs_11_), channel_id=1, source_target_pairs={{1,2},{2,1},{3,0},{0,3},{5,6},{6,5},{7,4},{4,7},{9,10},{10,9},{11,... | collective-permute-start | bytes 196616 | tf_op jit(solution)/shard_map/ppermute | solution.py:967
  6.5 3.1 %collective-permute-start.1 = (f32[2,16,256]{2,1,0:T(8,128)S(1)}, f32[2,16,256]{2,1,0:T(8,128)S(1)}, u32[]{:S(2)}, u32[]{:S(2)}) collective-permute-start(f32[2,16,256]{2,1,0:T(8,128)S(1)} %get-tuple-element.61.refs_6_), channel_id=1, source_target_pairs={{0,4},{4,0},{8,12},{12,8},{1,5},{5,1},{9,13},{13,9},{2,6},{6,2},{1... | collective-permute-start | bytes 98312 | tf_op jit(solution)/shard_map/ppermute | solution.py:964
  7.8 1.8 %collective-permute-start.2 = (f32[2,16,256]{2,1,0:T(8,128)S(1)}, f32[2,16,256]{2,1,0:T(8,128)S(1)}, u32[]{:S(2)}, u32[]{:S(2)}) collective-permute-start(f32[2,16,256]{2,1,0:T(8,128)S(1)} %get-tuple-element.62.refs_7_), channel_id=1, source_target_pairs={{0,1},{1,0},{2,3},{3,2},{4,8},{5,9},{6,10},{7,11},{8,4},{9,5},{10,... | collective-permute-start | bytes 98312 | tf_op jit(solution)/shard_map/ppermute | solution.py:970
  9.7 19.9 %collective-permute-start.12 = (f32[9,64,256]{2,1,0:T(8,128)S(1)}, f32[9,64,256]{2,1,0:T(8,128)S(1)}, u32[]{:S(2)}, u32[]{:S(2)}) collective-permute-start(f32[9,64,256]{2,1,0:T(8,128)S(1)} %pack_deep.1), channel_id=1, source_target_pairs={{0,16},{16,0},{1,17},{17,1},{2,18},{18,2},{3,19},{19,3},{4,20},{20... | collective-permute-start | bytes 1769480 | tf_op jit(solution)/shard_map/ppermute | solution.py:964
  10.8 7.1 %collective-permute-start.6 = (f32[25,8,256]{2,1,0:T(8,128)S(1)}, f32[25,8,256]{2,1,0:T(8,128)S(1)}, u32[]{:S(2)}, u32[]{:S(2)}) collective-permute-start(f32[25,8,256]{2,1,0:T(8,128)S(1)} %get-tuple-element.67.refs_2_), channel_id=1, source_target_pairs={{0,4},{4,0},{8,12},{12,8},{1,5},{5,1},{9,13},{13,9},{2,6},{6,2},{1... | collective-permute-start | bytes 614408 | tf_op jit(solution)/shard_map/ppermute | solution.py:964
  13.1 4.8 %collective-permute-start.7 = (f32[25,8,256]{2,1,0:T(8,128)S(1)}, f32[25,8,256]{2,1,0:T(8,128)S(1)}, u32[]{:S(2)}, u32[]{:S(2)}) collective-permute-start(f32[25,8,256]{2,1,0:T(8,128)S(1)} %get-tuple-element.74), channel_id=1, source_target_pairs={{0,1},{1,0},{2,3},{3,2},{4,8},{5,9},{6,10},{7,11},{8,4},{9,5},{10,... | collective-permute-start | bytes 614408 | tf_op jit(solution)/shard_map/ppermute | solution.py:970
  15.2 5.6 %collective-permute-start.5 = (f32[1,3,8,128]{3,2,1,0:T(8,128)S(1)}, f32[1,3,8,128]{3,2,1,0:T(8,128)S(1)}, u32[]{:S(2)}, u32[]{:S(2)}) collective-permute-start(f32[1,3,8,128]{3,2,1,0:T(8,128)S(1)} %get-tuple-element.65.cells), channel_id=1, source_target_pairs={{0,8},{4,12},{8,0},{12,4},{1,9},{5,13},{9,1},{13,5},{2,10},{6,14},... | collective-permute-start | bytes 36872 | tf_op jit(solution)/shard_map/ppermute | solution.py:1095
  20.8 3.0 %collective-permute-start.8 = (f32[2,3,8,128]{3,2,1,0:T(8,128)S(1)}, f32[2,3,8,128]{3,2,1,0:T(8,128)S(1)}, u32[]{:S(2)}, u32[]{:S(2)}) collective-permute-start(f32[2,3,8,128]{3,2,1,0:T(8,128)S(1)} %merge.5.cells), channel_id=1, source_target_pairs={{0,2},{1,3},{2,0},{3,1},{4,6},{5,7},{6,4},{7,5},{8,10},{9,11},{10,... | collective-permute-start | bytes 73736 | tf_op jit(solution)/shard_map/ppermute | solution.py:1095
  21.1 5.6 %collective-permute-start.10 = (f32[17,8,128]{2,1,0:T(8,128)S(1)}, f32[17,8,128]{2,1,0:T(8,128)S(1)}, u32[]{:S(2)}, u32[]{:S(2)}) collective-permute-start(f32[17,8,128]{2,1,0:T(8,128)S(1)} %get-tuple-element.88), channel_id=1, source_target_pairs={{0,16},{16,0},{1,17},{17,1},{2,18},{18,2},{3,19},{19,3},{4,20},{20... | collective-permute-start | bytes 208904 | tf_op jit(solution)/shard_map/ppermute | solution.py:964
  23.8 4.8 %collective-permute-start.9 = (f32[4,3,8,128]{3,2,1,0:T(8,128)S(1)}, f32[4,3,8,128]{3,2,1,0:T(8,128)S(1)}, u32[]{:S(2)}, u32[]{:S(2)}) collective-permute-start(f32[4,3,8,128]{3,2,1,0:T(8,128)S(1)} %merge.6.cells), channel_id=1, source_target_pairs={{0,4},{4,0},{8,12},{12,8},{1,5},{5,1},{9,13},{13,9},{2,6},{6,2},{1... | collective-permute-start | bytes 147464 | tf_op jit(solution)/shard_map/ppermute | solution.py:1095
  28.6 4.1 %collective-permute-start.11 = (f32[8,3,8,128]{3,2,1,0:T(8,128)S(1)}, f32[8,3,8,128]{3,2,1,0:T(8,128)S(1)}, u32[]{:S(2)}, u32[]{:S(2)}) collective-permute-start(f32[8,3,8,128]{3,2,1,0:T(8,128)S(1)} %merge.7.cells), channel_id=1, source_target_pairs={{0,16},{16,0},{1,17},{17,1},{2,18},{18,2},{3,19},{19,3},{4,20},{20... | collective-permute-start | bytes 294920 | tf_op jit(solution)/shard_map/ppermute | solution.py:1095
  32.8 4.6 %collective-permute-start.13 = (f32[16,3,8,128]{3,2,1,0:T(8,128)S(1)}, f32[16,3,8,128]{3,2,1,0:T(8,128)S(1)}, u32[]{:S(2)}, u32[]{:S(2)}) collective-permute-start(f32[16,3,8,128]{3,2,1,0:T(8,128)S(1)} %merge.8.cells), channel_id=1, source_target_pairs={{0,1},{1,0},{2,3},{3,2},{4,5},{5,4},{6,7},{7,6},{8,9},{9,8},{10,11... | collective-permute-start | bytes 589832 | tf_op jit(solution)/shard_map/ppermute | solution.py:1095

commit v5 on v4

--- a/solution.py
+++ b/solution.py
@@ -18,7 +18,8 @@
 DEPTH = SWEEPS
 SLOTS = LANES // DEPTH
 F32 = jnp.float32
-VMEM_LIMIT = 12 * 1024 * 1024
+VMEM_LIMIT = 14 * 1024 * 1024
+PLAN = ["W", "I1", "I4", "O2", "O3"]
 US = dict(local=1.2, rows=0.1, side=0.8, weights=3.2, restrict=0.6, extend=1.0, halo=1.4, outer=0.8, sweep=2.2, solve=2.2)
 
 
@@ -130,9 +131,8 @@
         return lax.axis_index("gx"), lax.axis_index("gy"), lax.axis_index("gz")
 
     def steps(self):
-        bits = [("gy", 1 << i) for i in reversed(range(1, self.ny.bit_length() - 1))]
-        bits += [("gz", 1 << i) for i in reversed(range(1, self.nx.bit_length() - 1))]
-        bits += [("gy", 1)]
+        bits = [("gz", 1 << i) for i in reversed(range(1, self.nx.bit_length() - 1))]
+        bits += [("gy", 1 << i) for i in reversed(range(self.ny.bit_length() - 1))]
         bits += [("gx", 1 << i) for i in reversed(range(self.nz.bit_length() - 1))]
         return bits + [("gz", 1)]
 
@@ -167,17 +167,17 @@
     for copy in loads + copies:
         copy.start()
     lane = lane_of((g.Y, LANES))
-    hi_pack = [jnp.zeros((g.Y, LANES), F32) for _ in range(g.blocks)]
-    lo_pack = list(hi_pack)
+    packs = [[jnp.zeros((g.Y, LANES), F32) for _ in range(g.blocks)] for _ in range(2)]
     for q in range(3):
         loads[q].wait()
         for z in range(g.Z):
             block, at = g.slot(q, z)
-            keep = (lane >= at) & (lane < at + DEPTH)
-            moved = roll(fields[q][z, :, g.X - LANES :], at + DEPTH, 1)
-            hi_pack[block] = jnp.where(keep, moved, hi_pack[block])
-            moved = roll(fields[q][z, :, :LANES], at, 1)
-            lo_pack[block] = jnp.where(keep, moved, lo_pack[block])
+            pack = packs[(at // DEPTH) % 2]
+            both = jnp.where(
+                lane < LANES // 2, fields[q][z, :, :LANES], fields[q][z, :, g.X - LANES :]
+            )
+            keep = (lane + (LANES + DEPTH - at)) % LANES < 2 * DEPTH
+            pack[block] = jnp.where(keep, roll(both, at, 1), pack[block])
         if q < 2:
             for at in range(0, g.Z, ROWS):
                 layers = range(at, at + ROWS)
@@ -186,9 +186,12 @@
                 for side, out in enumerate(y_out):
                     out[q, at : at + ROWS] = jnp.where((yi % 2) == side, hi, lo)
     even = (xi % 2) == 0
+    first_half = lane % (2 * DEPTH) < DEPTH
     for block in range(g.blocks):
+        lo = jnp.where(first_half, packs[0][block], packs[1][block])
+        hi = roll(jnp.where(first_half, packs[1][block], packs[0][block]), DEPTH, 1)
         for side, out in enumerate(x_out):
-            out[block] = jnp.where(even == (side == 0), hi_pack[block], lo_pack[block])
+            out[block] = jnp.where(even == (side == 0), hi, lo)
     for copy in copies:
         copy.wait()
 
@@ -372,6 +375,13 @@
         return view(bufs[0]), view(bufs[0])
     first, second = view(bufs[0]), view(bufs[1])
     return jnp.where(even, first, second), jnp.where(even, second, first)
+
+
+def side_weights_kernel(g, *refs):
+    k, x_in = refs[0], refs[1 : 1 + g.xsides + 1]
+    xp, xk, xs, fz, fy, fx, dinv, token, xh, xl = refs[2 + g.xsides :]
+    side_kernel(g, *x_in, xp, xk, xs, token, xh, xl)
+    weights_kernel(g, k, xk, token, fz, fy, fx, dinv, token)
 
 
 def restrict_kernel(g, *refs):
@@ -857,6 +867,47 @@
     on_ends(g, zi, clear)
 
 
+def extend_sweep_kernel(g, count, *refs):
+    p, s, xp, xs, dinv = refs[:5]
+    inputs = refs[5 : 5 + count]
+    n = 5 + count
+    outs = refs[n : n + 8 + g.zsides]
+    n += 8 + g.zsides
+    v = refs[n]
+    scratch = refs[n + 1 :]
+    xk, fz, fy, fx = inputs[1:5]
+    yp, yk, ys, fz_y, fx_y, fy_e, dinv_e, token = outs[:8]
+    extend_kernel(g, *inputs, *outs, *scratch)
+    common = (s, xs, ys, fz, fz_y, fx, fx_y, fy, fy_e, dinv, dinv_e)
+    sweep_kernel(g, 1, True, *common, p, xp, yp, v, token)
+
+
+def inner_sweeps_kernel(g, *refs):
+    common, v = refs[:11], refs[11]
+    between, out, token = refs[-3:]
+    sweep_kernel(g, 3, True, *common, v, between, token)
+    sweep_kernel(g, 4, True, *common, between, out, token)
+
+
+def halo_sweeps_kernel(g, count, *refs):
+    common, start, v = refs[:11], refs[11:14], refs[14]
+    inputs = refs[15 : 15 + count]
+    sh, hz, hy, hx, hd, out, token = refs[15 + count : 22 + count]
+    kh, ph, vh = refs[22 + count :]
+    beyond_own = (sh, hz, hy, hx, hd)
+    halo_kernel(g, *inputs, ph, *beyond_own, token, kh)
+    sweep_kernel(g, 1, False, *common, *start, ph, *beyond_own, vh, token)
+    sweep_kernel(g, 2, False, *common, v, vh, *beyond_own, out, token)
+
+
+def last_sweeps_kernel(g, *refs):
+    common, v = refs[:11], refs[11:13]
+    vh, beyond_own = refs[13], refs[14:19]
+    out, token, between = refs[19:]
+    sweep_kernel(g, 3, False, *common, v[0], vh, *beyond_own, between, token)
+    sweep_kernel(g, 4, False, *common, v[1], between, *beyond_own, out, token)
+
+
 def solve_kernel(g, gathered, fine, edges, out):
     zi, yi, xi = g.where()
     per = LANES // g.cx
@@ -864,16 +915,17 @@
 
     order = g.steps()
 
-    def relative(a, b, c):
-        apart = {
-            "gx": jnp.bitwise_xor(a, zi),
-            "gy": jnp.bitwise_xor(b, yi),
-            "gz": jnp.bitwise_xor(c, xi),
-        }
+    def place(a, b, c):
+        index = {"gx": a, "gy": b, "gz": c}
         at = 0
         for number, (axis, bit) in enumerate(order):
-            at = at + (1 << number) * ((apart[axis] & bit) // bit)
+            at = at + (1 << number) * ((index[axis] & bit) // bit)
         return at
+
+    here = place(zi, yi, xi)
+
+    def relative(a, b, c):
+        return jnp.bitwise_xor(here, place(a, b, c))
 
     layers = g.nz * g.cz
     height = g.ny * g.cy
@@ -1020,13 +1072,13 @@
         name="pack_rows",
     )
     y_got = exchange(y_sent, "gy", g.ny, "gz")
-    xp, xk, xs, token = run(
-        functools.partial(side_kernel, g),
-        [(Z, Y, LANES)] * 3 + [tile],
-        x_got + [y_sent[0]],
+    xp, xk, xs, fz, fy, fx, dinv, token_w = run(
+        functools.partial(side_weights_kernel, g),
+        [(Z, Y, LANES)] * 3 + [main] * 4 + [tile],
+        [k] + x_got + [y_sent[0]],
         scratch=[pltpu.VMEM(x_shape, F32)] * 2,
-        us=US["side"],
-        name="side",
+        us=US["side"] + US["weights"],
+        name="weights",
     )
     deep = run(
         functools.partial(deep_kernel, g),
@@ -1036,61 +1088,63 @@
         name="pack_deep",
     )
     deep_got = exchange(deep, "gx", g.nz, "gz")
-    fz, fy, fx, dinv, token_w = run(
-        functools.partial(weights_kernel, g),
-        [main] * 4 + [tile],
-        [k, xk, token],
-        us=US["weights"],
-        name="weights",
-    )
     rows = (Z, ROWS, g.XE)
     halo_scratch = [pltpu.VMEM(y_shape, F32)] * 2 + [pltpu.VMEM((g.blocks, g.YE, LANES), F32)] * 2
+    inputs = [k, xk, fz, fy, fx] + list(y_got) + x_got + [token_w]
+    own = (Z, g.YE, g.XE)
     extended = run(
-        functools.partial(extend_kernel, g),
-        [rows] * 5 + [(Z, 2 * ROWS, g.XE), (Z, 3 * ROWS, g.XE), tile] + [(nr,) + tile] * g.zsides,
-        [k, xk, fz, fy, fx] + list(y_got) + x_got + [token_w],
+        functools.partial(extend_sweep_kernel, g, len(inputs)),
+        [rows] * 5
+        + [(Z, 2 * ROWS, g.XE), (Z, 3 * ROWS, g.XE), tile]
+        + [(nr,) + tile] * g.zsides
+        + [own],
+        [p, s, xp, xs, dinv] + inputs,
         scratch=halo_scratch,
-        us=US["extend"],
+        us=US["extend"] + US["sweep"],
         name="extend",
     )
-    yp, yk, ys, fz_y, fx_y, fy_e, dinv_e, token = extended[:8]
-    relay = exchange(extended[8:], "gx", g.nz, "gz")
+    yp, yk, ys, fz_y, fx_y, fy_e, dinv_e, token_e = extended[:8]
+    relay = exchange(extended[8:-1], "gx", g.nz, "gz")
     weights = [fz, fz_y, fx, fx_y, fy, fy_e]
     common = [s, xs, ys] + weights + [dinv, dinv_e]
-    own = (Z, g.YE, g.XE)
     far = (4 * DEPTH, g.YE, g.XE)
     far8 = (2 * DEPTH, g.YE, g.XE)
-    inner, tokens = [[p, xp, yp]], []
-    for sweep in range(1, SWEEPS + 1):
-        v, token = run(
-            functools.partial(sweep_kernel, g, sweep, True),
-            [(Z, Y, X) if sweep == SWEEPS else own, tile],
-            common + inner[-1] + (relay[:1] if sweep == 3 else []),
-            us=US["sweep"] * (Z - 2 * sweep) / Z,
-            name=f"inner_{sweep}",
-        )
-        inner.append([v])
-        tokens.append(token)
-    vh, sh, hz, hy, hx, hd, token = run(
-        functools.partial(halo_kernel, g),
-        [far, far, far8, far, far, far8, tile],
-        [k, xk, yk] + weights + near_got + deep_got + relay + [tokens[2]],
+    inner, tokens = [[p, xp, yp], [extended[-1]]], {"W": token_w, "I1": token_e}
+    v, tokens["I2"] = run(
+        functools.partial(sweep_kernel, g, 2, True),
+        [own, tile],
+        common + inner[1],
+        us=US["sweep"],
+        name="inner_2",
+    )
+    inner.append([v])
+    between, v, tokens["I4"] = run(
+        functools.partial(inner_sweeps_kernel, g),
+        [own, (Z, Y, X), tile],
+        common + inner[2] + relay[:1],
+        us=US["sweep"],
+        name="inner_3_4",
+    )
+    inner += [[between], [v]]
+    inputs = [k, xk, yk] + weights + near_got + deep_got + relay + [tokens["I2"]]
+    sh, hz, hy, hx, hd, vh, tokens["O2"] = run(
+        functools.partial(halo_sweeps_kernel, g, len(inputs)),
+        [far, far8, far, far, far8, far, tile],
+        common + inner[0] + inner[1] + inputs,
+        scratch=[pltpu.VMEM(far, F32)] * 3,
+        us=US["halo"] + 2 * US["outer"],
+        name="halo_sweeps",
+    )
+    vh, tokens["O3"] = run(
+        functools.partial(last_sweeps_kernel, g),
+        [(2 * DEPTH, Y, X), tile],
+        common + inner[2] + inner[3] + [vh, sh, hz, hy, hx, hd],
         scratch=[pltpu.VMEM(far, F32)],
-        us=US["halo"],
-        name="halo",
-    )
-    for sweep in range(1, SWEEPS + 1):
-        final = sweep == SWEEPS
-        vh, token = run(
-            functools.partial(sweep_kernel, g, sweep, False),
-            [(2 * DEPTH, Y, X) if final else far, tile],
-            common + inner[sweep - 1] + [vh, sh, hz, hy, hx, hd],
-            us=US["outer"],
-            name=f"outer_{sweep}",
-        )
-        tokens.append(token)
+        us=2 * US["outer"],
+        name="last_sweeps",
+    )
     steps = g.steps()
-    plan = [0, 1, 3, 5, 6]
+    plan = PLAN
     for number, (axis, bit) in enumerate(steps):
         got = lax.ppermute(cells, axis, flips(lax.axis_size(axis), bit))
         cells = merge(cells, got, tokens[plan[max(0, number - len(steps) + len(plan))]])

time: 39.7 us -> 38.5 us (0.970)
  Pallas kernels: 20.3 us -> 18.5 us
  waiting for transfers between devices: 0.06 us -> 0.98 us
    pallas_call x23 -> x17, Pallas kernels: 20.3 us -> 18.5 us  [run(): pl.pallas_call(kernel, out_shape=shapes, in_specs=[pl.BlockSpec(memory_sp...]
    ppermute x5, waiting for transfers between devices: 0.03 us -> 0.95 us  [shards(): got = lax.ppermute(cells, axis, flips(lax.axis_size(axis), bit))]
    ppermute x5, starting transfers between devices: 6.86 us -> 6.44 us  [shards(): got = lax.ppermute(cells, axis, flips(lax.axis_size(axis), bit))]
  transfers between devices with their start and end apart: 14 -> 14, of which waited for: 0 -> 1; matrix products, arithmetic and copies ran while one was open for 0% -> 0% of each run, Pallas kernels for 40% -> 37%
where the time goes in v5:
time: 38.5 us; the launch traced here: 38.4 us
  starting transfers between devices  18.8 us (49%)
  Pallas kernels  18.5 us (48%)
  waiting for transfers between devices  0.98 us (3%)
    pallas_call x17, Pallas kernels, run(): pl.pallas_call(kernel, out_shape=shapes, in_specs=[pl.BlockSpec(memory_sp...  18.5 us
    ppermute x6, starting transfers between devices, exchange(): got = [lax.ppermute(bufs[0], axis, pairs(count, 0))]  8.32 us
    ppermute x5, starting transfers between devices, shards(): got = lax.ppermute(cells, axis, flips(lax.axis_size(axis), bit))  6.44 us
    ppermute x2, starting transfers between devices, exchange(): got.append(lax.ppermute(bufs[1], (axis, beside), perm))  2.87 us
    ppermute x1, starting transfers between devices, exchange(): got.append(lax.ppermute(bufs[1], axis, pairs(count, 1)))  1.13 us
    ppermute x5, waiting for transfers between devices, shards(): got = lax.ppermute(cells, axis, flips(lax.axis_size(axis), bit))  0.95 us
  transfers between devices with their start and end apart: 14, of which 1 were waited for; matrix products, arithmetic and copies ran while one was open for 0% of the time, Pallas kernels for 37%

profile of v5, /device:TPU:1, one launch (start us, length us, event | category | flops | bytes accessed | tf_op | source)
XLA Modules:
  0.0 38.4 jit_solution(3043878506197143749)
XLA Ops:
  0.0 2.2 %pack_faces.1 = (f32[16,64,256]{2,1,0:T(8,128)S(1)}, f32[16,64,256]{2,1,0:T(8,128)S(1)}, f32[16,64,256]{2,1,0:T(8,128)S(1)}, f32[2,64,256]{2,1,0:T(8,128)S(1)}, ...) custom-call(f32[16,64,256]{2,1,0:T(8,128)} %refs_0_.1, ...), custom_call_target="tpu_custom_call" | custom-call | flops 1000 | bytes 3500000 | tf_op jit(solution)/shard_map/pack_faces/pallas_call | solution.py:58
  2.2 2.1 %collective-permute-start = (f32[2,64,256]{2,1,0:T(8,128)S(1)}, f32[2,64,256]{2,1,0:T(8,128)S(1)}, u32[]{:S(2)}, u32[]{:S(2)}) collective-permute-start(f32[2,64,256]{2,1,0:T(8,128)S(1)} %get-tuple-element.55), channel_id=1, source_target_pairs={{0,16},{16,0},{1,17},{17,1},{2,18},{18,2},{3,19},{19,3},{4,20},{20... | collective-permute-start | bytes 393224 | tf_op jit(solution)/shard_map/ppermute | solution.py:1016
  4.3 1.0 %collective-permute-start.3 = (f32[2,64,128]{2,1,0:T(8,128)S(1)}, f32[2,64,128]{2,1,0:T(8,128)S(1)}, u32[]{:S(2)}, u32[]{:S(2)}) collective-permute-start(f32[2,64,128]{2,1,0:T(8,128)S(1)} %get-tuple-element.58.refs_10_), channel_id=1, source_target_pairs={{0,1},{1,0},{2,3},{3,2},{4,5},{5,4},{6,7},{7,6},{8,9},{9,8},{10,11... | collective-permute-start | bytes 196616 | tf_op jit(solution)/shard_map/ppermute | solution.py:1016
  5.2 1.1 %collective-permute-start.4 = (f32[2,64,128]{2,1,0:T(8,128)S(1)}, f32[2,64,128]{2,1,0:T(8,128)S(1)}, u32[]{:S(2)}, u32[]{:S(2)}) collective-permute-start(f32[2,64,128]{2,1,0:T(8,128)S(1)} %get-tuple-element.59.refs_11_), channel_id=1, source_target_pairs={{1,2},{2,1},{3,0},{0,3},{5,6},{6,5},{7,4},{4,7},{9,10},{10,9},{11,... | collective-permute-start | bytes 196616 | tf_op jit(solution)/shard_map/ppermute | solution.py:1019
  6.4 1.3 %collective-permute-start.1 = (f32[2,16,256]{2,1,0:T(8,128)S(1)}, f32[2,16,256]{2,1,0:T(8,128)S(1)}, u32[]{:S(2)}, u32[]{:S(2)}) collective-permute-start(f32[2,16,256]{2,1,0:T(8,128)S(1)} %get-tuple-element.56.refs_6_), channel_id=1, source_target_pairs={{0,4},{4,0},{8,12},{12,8},{1,5},{5,1},{9,13},{13,9},{2,6},{6,2},{1... | collective-permute-start | bytes 98312 | tf_op jit(solution)/shard_map/ppermute | solution.py:1016
  7.7 0.8 %collective-permute-start.2 = (f32[2,16,256]{2,1,0:T(8,128)S(1)}, f32[2,16,256]{2,1,0:T(8,128)S(1)}, u32[]{:S(2)}, u32[]{:S(2)}) collective-permute-start(f32[2,16,256]{2,1,0:T(8,128)S(1)} %get-tuple-element.57.refs_7_), channel_id=1, source_target_pairs={{0,1},{1,0},{2,3},{3,2},{4,8},{5,9},{6,10},{7,11},{8,4},{9,5},{10,... | collective-permute-start | bytes 98312 | tf_op jit(solution)/shard_map/ppermute | solution.py:1022
  8.4 0.9 %local_sums.1 = (f32[5,2,8,256]{3,2,1,0:T(8,128)S(1)}, f32[8,128]{1,0:T(8,128)S(1)}) custom-call(f32[16,64,256]{2,1,0:T(8,128)S(1)} %get-tuple-element.51.p.refs_0_.refs_11_, f32[16,64,256]{2,1,0:T(8,128)S(1)} %get-tuple-element.52.k.refs_1_.refs_0_.refs_5_.refs_15_, f32[16,64,256]{2,1,0:T(8,128)S(1)} %get-tuple-element.53.s.refs_2_.refs_1_.refs_0_), custom_call_target="tpu_custom_call" | custom-call | flops 1000 | bytes 4200000 | tf_op jit(solution)/shard_map/local_sums/pallas_call | solution.py:58
  9.5 0.4 collective-permute-start.12
  9.8 0.7 %restrict.1 = (f32[1,3,8,128]{3,2,1,0:T(8,128)S(1)}, f32[8,128]{1,0:T(8,128)S(1)}) custom-call(f32[16,64,256]{2,1,0:T(8,128)S(1)} %get-tuple-element.51.p.refs_0_.refs_11_, f32[16,64,256]{2,1,0:T(8,128)S(1)} %get-tuple-element.52.k.refs_1_.refs_0_.refs_5_.refs_15_, f32[5,2,8,256]{3,2,1,0:T(8,128)S(1)} %get-tuple-element.54.refs_2_, ...), custom_call_target="tpu_custom_call" | custom-call | flops 1000 | bytes 2100000 | tf_op jit(solution)/shard_map/restrict/pallas_call | solution.py:58
  10.7 2.3 %collective-permute-start.7 = (f32[25,8,256]{2,1,0:T(8,128)S(1)}, f32[25,8,256]{2,1,0:T(8,128)S(1)}, u32[]{:S(2)}, u32[]{:S(2)}) collective-permute-start(f32[25,8,256]{2,1,0:T(8,128)S(1)} %get-tuple-element.62.refs_3_), channel_id=1, source_target_pairs={{0,4},{4,0},{8,12},{12,8},{1,5},{5,1},{9,13},{13,9},{2,6},{6,2},{1... | collective-permute-start | bytes 614408 | tf_op jit(solution)/shard_map/ppermute | solution.py:1016
  13.0 2.1 %collective-permute-start.8 = (f32[25,8,256]{2,1,0:T(8,128)S(1)}, f32[25,8,256]{2,1,0:T(8,128)S(1)}, u32[]{:S(2)}, u32[]{:S(2)}) collective-permute-start(f32[25,8,256]{2,1,0:T(8,128)S(1)} %get-tuple-element.71), channel_id=1, source_target_pairs={{0,1},{1,0},{2,3},{3,2},{4,8},{5,9},{6,10},{7,11},{8,4},{9,5},{10,... | collective-permute-start | bytes 614408 | tf_op jit(solution)/shard_map/ppermute | solution.py:1022
  15.1 0.2 collective-permute-start.5
  15.3 2.6 %weights.1 = (f32[16,64,128]{2,1,0:T(8,128)S(1)}, f32[16,64,128]{2,1,0:T(8,128)S(1)}, f32[16,64,128]{2,1,0:T(8,128)S(1)}, f32[16,64,384]{2,1,0:T(8,128)S(1)}, f3...) custom-call(f32[16,64,256]{2,1,0:T(8,128)S(1)} %get-tuple-element.52.k, ...), custom_call_target="tpu_custom_call" | custom-call | flops 1000 | bytes 14000000 | tf_op jit(solution)/shard_map/weights/pallas_call | solution.py:58
  18.0 2.6 %extend.1 = (f32[16,8,384]{2,1,0:T(8,128)S(1)}, f32[16,8,384]{2,1,0:T(8,128)S(1)}, f32[16,8,384]{2,1,0:T(8,128)S(1)}, f32[16,8,384]{2,1,0:T(8,128)S(1)}, f32[16,...) custom-call(f32[16,64,256]{2,1,0:T(8,128)S(1)} %get-tuple-element.51, ...), custom_call_target="tpu_custom_call" | custom-call | flops 1000 | bytes 11200000 | tf_op jit(solution)/shard_map/extend/pallas_call | solution.py:58
  20.7 1.3 %collective-permute-start.10 = (f32[17,8,128]{2,1,0:T(8,128)S(1)}, f32[17,8,128]{2,1,0:T(8,128)S(1)}, u32[]{:S(2)}, u32[]{:S(2)}) collective-permute-start(f32[17,8,128]{2,1,0:T(8,128)S(1)} %get-tuple-element.80), channel_id=1, source_target_pairs={{0,16},{16,0},{1,17},{17,1},{2,18},{18,2},{3,19},{19,3},{4,20},{20... | collective-permute-start | bytes 208904 | tf_op jit(solution)/shard_map/ppermute | solution.py:1016
  21.9 2.9 %collective-permute-start.9 = (f32[4,3,8,128]{3,2,1,0:T(8,128)S(1)}, f32[4,3,8,128]{3,2,1,0:T(8,128)S(1)}, u32[]{:S(2)}, u32[]{:S(2)}) collective-permute-start(f32[4,3,8,128]{3,2,1,0:T(8,128)S(1)} %merge.6.cells), channel_id=1, source_target_pairs={{0,4},{4,0},{8,12},{12,8},{1,5},{5,1},{9,13},{13,9},{2,6},{6,2},{1... | collective-permute-start | bytes 147464 | tf_op jit(solution)/shard_map/ppermute | solution.py:1149
  24.9 1.6 %inner_2.1 = (f32[16,72,384]{2,1,0:T(8,128)S(1)}, f32[8,128]{1,0:T(8,128)S(1)}) custom-call(f32[16,64,256]{2,1,0:T(8,128)S(1)} %get-tuple-element.53.s.refs_2_.refs_1_.refs_0_, f32[16,64,128]{2,1,0:T(8,128)S(1)} %get-tuple-element.65.refs_3_.refs_1_, f32[16,8,384]{2,1,0:T(8,128)S(1)} %get-tuple-element.73.refs_2_, ...), custom_call_target="tpu_custom_call" | custom-call | flops 1000 | bytes 7700000 | tf_op jit(solution)/shard_map/inner_2/pallas_call | solution.py:58
  26.5 1.8 %inner_3_4.1 = (f32[16,72,384]{2,1,0:T(8,128)S(1)}, f32[16,64,256]{2,1,0:T(8,128)S(1)}, f32[8,128]{1,0:T(8,128)S(1)}) custom-call(f32[16,64,256]{2,1,0:T(8,128)S(1)} %get-tuple-element.53.s.refs_2_.refs_1_.refs_0_, f32[16,64,128]{2,1,0:T(8,128)S(1)} %get-tuple-element.65.refs_3_.refs_1_, f32[16,8,384]{2,1,0:T(8,128)S(1)} %get-tuple-element.73.refs_2_, ...), custom_call_target="tpu_custom_call" | custom-call | flops 1000 | bytes 7700000 | tf_op jit(solution)/shard_map/inner_3_4/pallas_call | solution.py:58
  28.3 0.3 collective-permute-start.11
  28.6 2.2 %halo_sweeps.1 = (f32[16,72,384]{2,1,0:T(8,128)S(1)}, f32[8,72,384]{2,1,0:T(8,128)S(1)}, f32[16,72,384]{2,1,0:T(8,128)S(1)}, f32[16,72,384]{2,1,0:T(8,128)S(1)},...) custom-call(f32[16,64,256]{2,1,0:T(8,128)S(1)} %get-tuple-element.53.s.refs_2_.refs_1_.refs_0_, ...), custom_call_target="tpu_custom_call" | custom-call | flops 1000 | bytes 10500000 | tf_op jit(solution)/shard_map/halo_sweeps/pallas_call | solution.py:58
  30.9 0.9 %collective-permute-done.11.got = f32[8,3,8,128]{3,2,1,0:T(8,128)S(1)} collective-permute-done((f32[8,3,8,128]{3,2,1,0:T(8,128)S(1)}, f32[8,3,8,128]{3,2,1,0:T(8,128)S(1)}, u32[]{:S(2)}, u32[]{:S(2)}) %collective-permute-start.11) | collective-permute-done | bytes 98336 | tf_op jit(solution)/shard_map/ppermute | solution.py:1149
  31.9 2.8 %collective-permute-start.13 = (f32[16,3,8,128]{3,2,1,0:T(8,128)S(1)}, f32[16,3,8,128]{3,2,1,0:T(8,128)S(1)}, u32[]{:S(2)}, u32[]{:S(2)}) collective-permute-start(f32[16,3,8,128]{3,2,1,0:T(8,128)S(1)} %merge.8.cells), channel_id=1, source_target_pairs={{0,1},{1,0},{2,3},{3,2},{4,5},{5,4},{6,7},{7,6},{8,9},{9,8},{10,11... | collective-permute-start | bytes 589832 | tf_op jit(solution)/shard_map/ppermute | solution.py:1149
  34.7 1.5 %last_sweeps.1 = (f32[8,64,256]{2,1,0:T(8,128)S(1)}, f32[8,128]{1,0:T(8,128)S(1)}) custom-call(f32[16,64,256]{2,1,0:T(8,128)S(1)} %get-tuple-element.53.s.refs_2_.refs_1_.refs_0_, f32[16,64,128]{2,1,0:T(8,128)S(1)} %get-tuple-element.65.refs_3_.refs_1_, f32[16,8,384]{2,1,0:T(8,128)S(1)} %get-tuple-element.73.refs_2_, ...), custom_call_target="tpu_custom_call" | custom-call | flops 1000 | bytes 5600000 | tf_op jit(solution)/shard_map/last_sweeps/pallas_call | solution.py:58
  36.2 2.1 %solve.1 = f32[16,64,256]{2,1,0:T(8,128)} custom-call(f32[32,3,8,128]{3,2,1,0:T(8,128)S(1)} %merge.9.gathered, f32[16,64,256]{2,1,0:T(8,128)S(1)} %get-tuple-element.95.fine, f32[8,64,256]{2,1,0:T(8,128)S(1)} %get-tuple-element.96.edges), custom_call_target="tpu_custom_call" | custom-call | flops 1000 | bytes 7700000 | tf_op jit(solution)/shard_map/solve/pallas_call | solution.py:58
  (21 shorter events, 0.4 us)
Async XLA Ops:
  2.2 7.2 %collective-permute-start = (f32[2,64,256]{2,1,0:T(8,128)S(1)}, f32[2,64,256]{2,1,0:T(8,128)S(1)}, u32[]{:S(2)}, u32[]{:S(2)}) collective-permute-start(f32[2,64,256]{2,1,0:T(8,128)S(1)} %get-tuple-element.55), channel_id=1, source_target_pairs={{0,16},{16,0},{1,17},{17,1},{2,18},{18,2},{3,19},{19,3},{4,20},{20... | collective-permute-start | bytes 393224 | tf_op jit(solution)/shard_map/ppermute | solution.py:1016
  4.3 5.1 %collective-permute-start.3 = (f32[2,64,128]{2,1,0:T(8,128)S(1)}, f32[2,64,128]{2,1,0:T(8,128)S(1)}, u32[]{:S(2)}, u32[]{:S(2)}) collective-permute-start(f32[2,64,128]{2,1,0:T(8,128)S(1)} %get-tuple-element.58.refs_10_), channel_id=1, source_target_pairs={{0,1},{1,0},{2,3},{3,2},{4,5},{5,4},{6,7},{7,6},{8,9},{9,8},{10,11... | collective-permute-start | bytes 196616 | tf_op jit(solution)/shard_map/ppermute | solution.py:1016
  5.2 4.1 %collective-permute-start.4 = (f32[2,64,128]{2,1,0:T(8,128)S(1)}, f32[2,64,128]{2,1,0:T(8,128)S(1)}, u32[]{:S(2)}, u32[]{:S(2)}) collective-permute-start(f32[2,64,128]{2,1,0:T(8,128)S(1)} %get-tuple-element.59.refs_11_), channel_id=1, source_target_pairs={{1,2},{2,1},{3,0},{0,3},{5,6},{6,5},{7,4},{4,7},{9,10},{10,9},{11,... | collective-permute-start | bytes 196616 | tf_op jit(solution)/shard_map/ppermute | solution.py:1019
  6.4 3.0 %collective-permute-start.1 = (f32[2,16,256]{2,1,0:T(8,128)S(1)}, f32[2,16,256]{2,1,0:T(8,128)S(1)}, u32[]{:S(2)}, u32[]{:S(2)}) collective-permute-start(f32[2,16,256]{2,1,0:T(8,128)S(1)} %get-tuple-element.56.refs_6_), channel_id=1, source_target_pairs={{0,4},{4,0},{8,12},{12,8},{1,5},{5,1},{9,13},{13,9},{2,6},{6,2},{1... | collective-permute-start | bytes 98312 | tf_op jit(solution)/shard_map/ppermute | solution.py:1016
  7.7 1.7 %collective-permute-start.2 = (f32[2,16,256]{2,1,0:T(8,128)S(1)}, f32[2,16,256]{2,1,0:T(8,128)S(1)}, u32[]{:S(2)}, u32[]{:S(2)}) collective-permute-start(f32[2,16,256]{2,1,0:T(8,128)S(1)} %get-tuple-element.57.refs_7_), channel_id=1, source_target_pairs={{0,1},{1,0},{2,3},{3,2},{4,8},{5,9},{6,10},{7,11},{8,4},{9,5},{10,... | collective-permute-start | bytes 98312 | tf_op jit(solution)/shard_map/ppermute | solution.py:1022
  9.5 19.2 %collective-permute-start.12 = (f32[9,64,256]{2,1,0:T(8,128)S(1)}, f32[9,64,256]{2,1,0:T(8,128)S(1)}, u32[]{:S(2)}, u32[]{:S(2)}) collective-permute-start(f32[9,64,256]{2,1,0:T(8,128)S(1)} %pack_deep.1), channel_id=1, source_target_pairs={{0,16},{16,0},{1,17},{17,1},{2,18},{18,2},{3,19},{19,3},{4,20},{20... | collective-permute-start | bytes 1769480 | tf_op jit(solution)/shard_map/ppermute | solution.py:1016
  10.7 7.4 %collective-permute-start.7 = (f32[25,8,256]{2,1,0:T(8,128)S(1)}, f32[25,8,256]{2,1,0:T(8,128)S(1)}, u32[]{:S(2)}, u32[]{:S(2)}) collective-permute-start(f32[25,8,256]{2,1,0:T(8,128)S(1)} %get-tuple-element.62.refs_3_), channel_id=1, source_target_pairs={{0,4},{4,0},{8,12},{12,8},{1,5},{5,1},{9,13},{13,9},{2,6},{6,2},{1... | collective-permute-start | bytes 614408 | tf_op jit(solution)/shard_map/ppermute | solution.py:1016
  13.0 5.1 %collective-permute-start.8 = (f32[25,8,256]{2,1,0:T(8,128)S(1)}, f32[25,8,256]{2,1,0:T(8,128)S(1)}, u32[]{:S(2)}, u32[]{:S(2)}) collective-permute-start(f32[25,8,256]{2,1,0:T(8,128)S(1)} %get-tuple-element.71), channel_id=1, source_target_pairs={{0,1},{1,0},{2,3},{3,2},{4,8},{5,9},{6,10},{7,11},{8,4},{9,5},{10,... | collective-permute-start | bytes 614408 | tf_op jit(solution)/shard_map/ppermute | solution.py:1022
  15.1 2.8 %collective-permute-start.5 = (f32[1,3,8,128]{3,2,1,0:T(8,128)S(1)}, f32[1,3,8,128]{3,2,1,0:T(8,128)S(1)}, u32[]{:S(2)}, u32[]{:S(2)}) collective-permute-start(f32[1,3,8,128]{3,2,1,0:T(8,128)S(1)} %get-tuple-element.60.cells), channel_id=1, source_target_pairs={{0,2},{1,3},{2,0},{3,1},{4,6},{5,7},{6,4},{7,5},{8,10},{9,11},{10,... | collective-permute-start | bytes 36872 | tf_op jit(solution)/shard_map/ppermute | solution.py:1149
  17.9 4.0 %collective-permute-start.6 = (f32[2,3,8,128]{3,2,1,0:T(8,128)S(1)}, f32[2,3,8,128]{3,2,1,0:T(8,128)S(1)}, u32[]{:S(2)}, u32[]{:S(2)}) collective-permute-start(f32[2,3,8,128]{3,2,1,0:T(8,128)S(1)} %merge.5.cells), channel_id=1, source_target_pairs={{0,8},{4,12},{8,0},{12,4},{1,9},{5,13},{9,1},{13,5},{2,10},{6,14},... | collective-permute-start | bytes 73736 | tf_op jit(solution)/shard_map/ppermute | solution.py:1149
  20.7 5.8 %collective-permute-start.10 = (f32[17,8,128]{2,1,0:T(8,128)S(1)}, f32[17,8,128]{2,1,0:T(8,128)S(1)}, u32[]{:S(2)}, u32[]{:S(2)}) collective-permute-start(f32[17,8,128]{2,1,0:T(8,128)S(1)} %get-tuple-element.80), channel_id=1, source_target_pairs={{0,16},{16,0},{1,17},{17,1},{2,18},{18,2},{3,19},{19,3},{4,20},{20... | collective-permute-start | bytes 208904 | tf_op jit(solution)/shard_map/ppermute | solution.py:1016
  21.9 6.3 %collective-permute-start.9 = (f32[4,3,8,128]{3,2,1,0:T(8,128)S(1)}, f32[4,3,8,128]{3,2,1,0:T(8,128)S(1)}, u32[]{:S(2)}, u32[]{:S(2)}) collective-permute-start(f32[4,3,8,128]{3,2,1,0:T(8,128)S(1)} %merge.6.cells), channel_id=1, source_target_pairs={{0,4},{4,0},{8,12},{12,8},{1,5},{5,1},{9,13},{13,9},{2,6},{6,2},{1... | collective-permute-start | bytes 147464 | tf_op jit(solution)/shard_map/ppermute | solution.py:1149
  28.3 3.5 %collective-permute-start.11 = (f32[8,3,8,128]{3,2,1,0:T(8,128)S(1)}, f32[8,3,8,128]{3,2,1,0:T(8,128)S(1)}, u32[]{:S(2)}, u32[]{:S(2)}) collective-permute-start(f32[8,3,8,128]{3,2,1,0:T(8,128)S(1)} %merge.7.cells), channel_id=1, source_target_pairs={{0,16},{16,0},{1,17},{17,1},{2,18},{18,2},{3,19},{19,3},{4,20},{20... | collective-permute-start | bytes 294920 | tf_op jit(solution)/shard_map/ppermute | solution.py:1149
  31.9 4.3 %collective-permute-start.13 = (f32[16,3,8,128]{3,2,1,0:T(8,128)S(1)}, f32[16,3,8,128]{3,2,1,0:T(8,128)S(1)}, u32[]{:S(2)}, u32[]{:S(2)}) collective-permute-start(f32[16,3,8,128]{3,2,1,0:T(8,128)S(1)} %merge.8.cells), channel_id=1, source_target_pairs={{0,1},{1,0},{2,3},{3,2},{4,5},{5,4},{6,7},{7,6},{8,9},{9,8},{10,11... | collective-permute-start | bytes 589832 | tf_op jit(solution)/shard_map/ppermute | solution.py:1149

commit v6 on v5

--- a/solution.py
+++ b/solution.py
@@ -19,7 +19,7 @@
 SLOTS = LANES // DEPTH
 F32 = jnp.float32
 VMEM_LIMIT = 14 * 1024 * 1024
-PLAN = ["W", "I1", "I4", "O2", "O3"]
+PLAN = ["I4", "O2", "O3"]
 US = dict(local=1.2, rows=0.1, side=0.8, weights=3.2, restrict=0.6, extend=1.0, halo=1.4, outer=0.8, sweep=2.2, solve=2.2)
 
 
@@ -131,10 +131,10 @@
         return lax.axis_index("gx"), lax.axis_index("gy"), lax.axis_index("gz")
 
     def steps(self):
-        bits = [("gz", 1 << i) for i in reversed(range(1, self.nx.bit_length() - 1))]
-        bits += [("gy", 1 << i) for i in reversed(range(self.ny.bit_length() - 1))]
-        bits += [("gx", 1 << i) for i in reversed(range(self.nz.bit_length() - 1))]
-        return bits + [("gz", 1)]
+        before = [("gz", 1 << i) for i in reversed(range(1, self.nx.bit_length() - 1))]
+        before += [("gy", 1 << i) for i in reversed(range(1, self.ny.bit_length() - 1))]
+        after = [("gx", 1 << i) for i in reversed(range(1, self.nz.bit_length() - 1))]
+        return before, [("gx", 1)], after + [("gy", 1), ("gz", 1)]
 
     def slot(self, q, z):
         index = q * self.Z + z
@@ -712,7 +712,9 @@
             return jnp.where((zi % 2 == 0) == top, bufs[0][at], bufs[1][at])
 
         count = relay_tiles() * parts
-        tiles = [received(relay, i) for i in range(relay_blocks(g))]
+        skip = relay[0].shape[0] - relay_blocks(g)
+        bufs = [relay[0].at[skip:]] + list(relay[1:])
+        tiles = [received(bufs, i) for i in range(relay_blocks(g))]
         strip = jnp.concatenate(tiles[count:], axis=0)
         packed = jnp.concatenate(
             [
@@ -913,7 +915,7 @@
     per = LANES // g.cx
     group = lane_of((ROWS, LANES)) // g.cx
 
-    order = g.steps()
+    order = sum(g.steps(), [])
 
     def place(a, b, c):
         index = {"gx": a, "gy": b, "gz": c}
@@ -1000,10 +1002,31 @@
                 out[z] = edges[beyond(g, z) - DEPTH] + spread
 
 
+def copy_kernel(source, out):
+    out[...] = source[...]
+
+
 def merge_kernel(cells, got, token, out):
     count = cells.shape[0]
     out[:count] = cells[...]
     out[count:] = got[...]
+
+
+def join_kernel(g, cells, got, relay, out):
+    nc = coarse_blocks(g)
+    count = cells.shape[0]
+    for at in range(count):
+        out[at * nc : (at + 1) * nc] = cells[at]
+        out[(count + at) * nc : (count + at + 1) * nc] = got[at]
+    out[2 * count * nc :] = relay[...]
+
+
+def split_kernel(g, joined, got, token, out):
+    nc = coarse_blocks(g)
+    count = out.shape[0] // 2
+    for at in range(count):
+        out[at] = joined[at * nc : (at + 1) * nc]
+        out[count + at] = got[at * nc : (at + 1) * nc]
 
 
 def merge(cells, got, token):
@@ -1031,7 +1054,7 @@
     y_shape = (3 * Z // 2 + 1, ROWS, X)
     sums_shape = (5, g.cz, ROWS, X)
     main = (Z, Y, g.XE)
-    nr = relay_blocks(g)
+    nc, nr = coarse_blocks(g), relay_blocks(g)
 
     sent = run(
         functools.partial(pack_kernel, g),
@@ -1072,6 +1095,8 @@
         name="pack_rows",
     )
     y_got = exchange(y_sent, "gy", g.ny, "gz")
+    y_got = list(y_got)
+    y_got[:1] = run(copy_kernel, [y_shape], y_got[:1], us=0.05, name="first_rows")
     xp, xk, xs, fz, fy, fx, dinv, token_w = run(
         functools.partial(side_weights_kernel, g),
         [(Z, Y, LANES)] * 3 + [main] * 4 + [tile],
@@ -1104,7 +1129,20 @@
         name="extend",
     )
     yp, yk, ys, fz_y, fx_y, fy_e, dinv_e, token_e = extended[:8]
-    relay = exchange(extended[8:-1], "gx", g.nz, "gz")
+    before, _, after = g.steps()
+    for number, (axis, bit) in enumerate(before):
+        got = lax.ppermute(cells, axis, flips(lax.axis_size(axis), bit))
+        if number < len(before) - 1:
+            cells = merge(cells, got, token_w)
+    count = 2 * cells.shape[0]
+    (joined,) = run(
+        functools.partial(join_kernel, g),
+        [(count * nc + nr,) + tile],
+        [cells, got, extended[8]],
+        us=0.05,
+        name="join",
+    )
+    relay = exchange([joined] + list(extended[9:-1]), "gx", g.nz, "gz")
     weights = [fz, fz_y, fx, fx_y, fy, fy_e]
     common = [s, xs, ys] + weights + [dinv, dinv_e]
     far = (4 * DEPTH, g.YE, g.XE)
@@ -1121,7 +1159,7 @@
     between, v, tokens["I4"] = run(
         functools.partial(inner_sweeps_kernel, g),
         [own, (Z, Y, X), tile],
-        common + inner[2] + relay[:1],
+        common + inner[2],
         us=US["sweep"],
         name="inner_3_4",
     )
@@ -1143,11 +1181,17 @@
         us=2 * US["outer"],
         name="last_sweeps",
     )
-    steps = g.steps()
-    plan = PLAN
-    for number, (axis, bit) in enumerate(steps):
+    (cells,) = run(
+        functools.partial(split_kernel, g),
+        [(2 * count, nc) + tile],
+        [joined, relay[0], tokens[PLAN[0]]],
+        us=0.05,
+        name="split",
+    )
+    for number, (axis, bit) in enumerate(after):
         got = lax.ppermute(cells, axis, flips(lax.axis_size(axis), bit))
-        cells = merge(cells, got, tokens[plan[max(0, number - len(steps) + len(plan))]])
+        name = PLAN[max(1, number - len(after) + len(PLAN))]
+        cells = merge(cells, got, tokens[name])
     (out,) = run(
         functools.partial(solve_kernel, g),
         [(Z, Y, X)],

time: 38.5 us -> 37.1 us (0.964)
  starting transfers between devices: 18.8 us -> 17.6 us
  waiting for transfers between devices: 0.98 us -> 0.44 us
    ppermute x5 -> x4, starting transfers between devices: 6.44 us -> 5.24 us  [shards(): got = lax.ppermute(cells, axis, flips(lax.axis_size(axis), bit))]
    ppermute x5 -> x4, waiting for transfers between devices: 0.95 us -> 0.41 us  [shards(): got = lax.ppermute(cells, axis, flips(lax.axis_size(axis), bit))]
    pallas_call x17 -> x18, Pallas kernels: 18.5 us -> 18.8 us  [run(): pl.pallas_call(kernel, out_shape=shapes, in_specs=[pl.BlockSpec(memory_sp...]
  transfers between devices with their start and end apart: 14 -> 13, of which waited for: 1 -> 1; matrix products, arithmetic and copies ran while one was open for 0% -> 0% of each run, Pallas kernels for 37% -> 39%
where the time goes in v6:
time: 37.1 us; the launch traced here: 36.9 us
  Pallas kernels  18.8 us (51%)
  starting transfers between devices  17.6 us (47%)
  waiting for transfers between devices  0.44 us (1%)
    pallas_call x18, Pallas kernels, run(): pl.pallas_call(kernel, out_shape=shapes, in_specs=[pl.BlockSpec(memory_sp...  18.8 us
    ppermute x6, starting transfers between devices, exchange(): got = [lax.ppermute(bufs[0], axis, pairs(count, 0))]  8.33 us
    ppermute x4, starting transfers between devices, shards(): got = lax.ppermute(cells, axis, flips(lax.axis_size(axis), bit))  5.24 us
    ppermute x2, starting transfers between devices, exchange(): got.append(lax.ppermute(bufs[1], (axis, beside), perm))  2.87 us
    ppermute x1, starting transfers between devices, exchange(): got.append(lax.ppermute(bufs[1], axis, pairs(count, 1)))  1.13 us
  transfers between devices with their start and end apart: 13, of which 1 were waited for; matrix products, arithmetic and copies ran while one was open for 0% of the time, Pallas kernels for 39%

profile of v6, /device:TPU:1, one launch (start us, length us, event | category | flops | bytes accessed | tf_op | source)
XLA Modules:
  0.0 36.9 jit_solution(5602847402505283142)
XLA Ops:
  0.0 2.2 %pack_faces.1 = (f32[16,64,256]{2,1,0:T(8,128)S(1)}, f32[16,64,256]{2,1,0:T(8,128)S(1)}, f32[16,64,256]{2,1,0:T(8,128)S(1)}, f32[2,64,256]{2,1,0:T(8,128)S(1)}, ...) custom-call(f32[16,64,256]{2,1,0:T(8,128)} %refs_0_.1, ...), custom_call_target="tpu_custom_call" | custom-call | flops 1000 | bytes 3500000 | tf_op jit(solution)/shard_map/pack_faces/pallas_call | solution.py:58
  2.2 2.1 %collective-permute-start = (f32[2,64,256]{2,1,0:T(8,128)S(1)}, f32[2,64,256]{2,1,0:T(8,128)S(1)}, u32[]{:S(2)}, u32[]{:S(2)}) collective-permute-start(f32[2,64,256]{2,1,0:T(8,128)S(1)} %get-tuple-element.54), channel_id=1, source_target_pairs={{0,16},{16,0},{1,17},{17,1},{2,18},{18,2},{3,19},{19,3},{4,20},{20... | collective-permute-start | bytes 393224 | tf_op jit(solution)/shard_map/ppermute | solution.py:1039
  4.3 1.0 %collective-permute-start.3 = (f32[2,64,128]{2,1,0:T(8,128)S(1)}, f32[2,64,128]{2,1,0:T(8,128)S(1)}, u32[]{:S(2)}, u32[]{:S(2)}) collective-permute-start(f32[2,64,128]{2,1,0:T(8,128)S(1)} %get-tuple-element.57.refs_10_), channel_id=1, source_target_pairs={{0,1},{1,0},{2,3},{3,2},{4,5},{5,4},{6,7},{7,6},{8,9},{9,8},{10,11... | collective-permute-start | bytes 196616 | tf_op jit(solution)/shard_map/ppermute | solution.py:1039
  5.2 1.1 %collective-permute-start.4 = (f32[2,64,128]{2,1,0:T(8,128)S(1)}, f32[2,64,128]{2,1,0:T(8,128)S(1)}, u32[]{:S(2)}, u32[]{:S(2)}) collective-permute-start(f32[2,64,128]{2,1,0:T(8,128)S(1)} %get-tuple-element.58.refs_11_), channel_id=1, source_target_pairs={{1,2},{2,1},{3,0},{0,3},{5,6},{6,5},{7,4},{4,7},{9,10},{10,9},{11,... | collective-permute-start | bytes 196616 | tf_op jit(solution)/shard_map/ppermute | solution.py:1042
  6.4 1.3 %collective-permute-start.1 = (f32[2,16,256]{2,1,0:T(8,128)S(1)}, f32[2,16,256]{2,1,0:T(8,128)S(1)}, u32[]{:S(2)}, u32[]{:S(2)}) collective-permute-start(f32[2,16,256]{2,1,0:T(8,128)S(1)} %get-tuple-element.55.refs_6_), channel_id=1, source_target_pairs={{0,4},{4,0},{8,12},{12,8},{1,5},{5,1},{9,13},{13,9},{2,6},{6,2},{1... | collective-permute-start | bytes 98312 | tf_op jit(solution)/shard_map/ppermute | solution.py:1039
  7.7 0.8 %collective-permute-start.2 = (f32[2,16,256]{2,1,0:T(8,128)S(1)}, f32[2,16,256]{2,1,0:T(8,128)S(1)}, u32[]{:S(2)}, u32[]{:S(2)}) collective-permute-start(f32[2,16,256]{2,1,0:T(8,128)S(1)} %get-tuple-element.56.refs_7_), channel_id=1, source_target_pairs={{0,1},{1,0},{2,3},{3,2},{4,8},{5,9},{6,10},{7,11},{8,4},{9,5},{10,... | collective-permute-start | bytes 98312 | tf_op jit(solution)/shard_map/ppermute | solution.py:1045
  8.4 0.9 %local_sums.1 = (f32[5,2,8,256]{3,2,1,0:T(8,128)S(1)}, f32[8,128]{1,0:T(8,128)S(1)}) custom-call(f32[16,64,256]{2,1,0:T(8,128)S(1)} %get-tuple-element.50.p.refs_0_.refs_11_, f32[16,64,256]{2,1,0:T(8,128)S(1)} %get-tuple-element.51.k.refs_1_.refs_0_.refs_5_.refs_15_, f32[16,64,256]{2,1,0:T(8,128)S(1)} %get-tuple-element.52.s.refs_2_.refs_1_.refs_0_), custom_call_target="tpu_custom_call" | custom-call | flops 1000 | bytes 4200000 | tf_op jit(solution)/shard_map/local_sums/pallas_call | solution.py:58
  9.5 0.4 %collective-permute-start.11 = (f32[9,64,256]{2,1,0:T(8,128)S(1)}, f32[9,64,256]{2,1,0:T(8,128)S(1)}, u32[]{:S(2)}, u32[]{:S(2)}) collective-permute-start(f32[9,64,256]{2,1,0:T(8,128)S(1)} %pack_deep.1), channel_id=1, source_target_pairs={{0,16},{16,0},{1,17},{17,1},{2,18},{18,2},{3,19},{19,3},{4,20},{20... | collective-permute-start | bytes 1769480 | tf_op jit(solution)/shard_map/ppermute | solution.py:1039
  9.8 0.7 %restrict.1 = (f32[1,3,8,128]{3,2,1,0:T(8,128)S(1)}, f32[8,128]{1,0:T(8,128)S(1)}) custom-call(f32[16,64,256]{2,1,0:T(8,128)S(1)} %get-tuple-element.50.p.refs_0_.refs_11_, f32[16,64,256]{2,1,0:T(8,128)S(1)} %get-tuple-element.51.k.refs_1_.refs_0_.refs_5_.refs_15_, f32[5,2,8,256]{3,2,1,0:T(8,128)S(1)} %get-tuple-element.53.refs_2_, ...), custom_call_target="tpu_custom_call" | custom-call | flops 1000 | bytes 2100000 | tf_op jit(solution)/shard_map/restrict/pallas_call | solution.py:58
  10.7 2.3 %collective-permute-start.7 = (f32[25,8,256]{2,1,0:T(8,128)S(1)}, f32[25,8,256]{2,1,0:T(8,128)S(1)}, u32[]{:S(2)}, u32[]{:S(2)}) collective-permute-start(f32[25,8,256]{2,1,0:T(8,128)S(1)} %get-tuple-element.61.refs_3_), channel_id=1, source_target_pairs={{0,4},{4,0},{8,12},{12,8},{1,5},{5,1},{9,13},{13,9},{2,6},{6,2},{1... | collective-permute-start | bytes 614408 | tf_op jit(solution)/shard_map/ppermute | solution.py:1039
  13.0 2.1 %collective-permute-start.8 = (f32[25,8,256]{2,1,0:T(8,128)S(1)}, f32[25,8,256]{2,1,0:T(8,128)S(1)}, u32[]{:S(2)}, u32[]{:S(2)}) collective-permute-start(f32[25,8,256]{2,1,0:T(8,128)S(1)} %get-tuple-element.70), channel_id=1, source_target_pairs={{0,1},{1,0},{2,3},{3,2},{4,8},{5,9},{6,10},{7,11},{8,4},{9,5},{10,... | collective-permute-start | bytes 614408 | tf_op jit(solution)/shard_map/ppermute | solution.py:1045
  15.1 0.2 collective-permute-start.5
  15.3 2.6 %weights.1 = (f32[16,64,128]{2,1,0:T(8,128)S(1)}, f32[16,64,128]{2,1,0:T(8,128)S(1)}, f32[16,64,128]{2,1,0:T(8,128)S(1)}, f32[16,64,384]{2,1,0:T(8,128)S(1)}, f3...) custom-call(f32[16,64,256]{2,1,0:T(8,128)S(1)} %get-tuple-element.51.k, ...), custom_call_target="tpu_custom_call" | custom-call | flops 1000 | bytes 14000000 | tf_op jit(solution)/shard_map/weights/pallas_call | solution.py:58
  17.9 0.1 collective-permute-start.6
  18.1 3.1 %extend.1 = (f32[16,8,384]{2,1,0:T(8,128)S(1)}, f32[16,8,384]{2,1,0:T(8,128)S(1)}, f32[16,8,384]{2,1,0:T(8,128)S(1)}, f32[16,8,384]{2,1,0:T(8,128)S(1)}, f32[16,...) custom-call(f32[16,64,256]{2,1,0:T(8,128)S(1)} %get-tuple-element.50, ...), custom_call_target="tpu_custom_call" | custom-call | flops 1000 | bytes 11200000 | tf_op jit(solution)/shard_map/extend/pallas_call | solution.py:58
  21.2 0.4 %collective-permute-done.6.got = f32[2,3,8,128]{3,2,1,0:T(8,128)S(1)} collective-permute-done((f32[2,3,8,128]{3,2,1,0:T(8,128)S(1)}, f32[2,3,8,128]{3,2,1,0:T(8,128)S(1)}, u32[]{:S(2)}, u32[]{:S(2)}) %collective-permute-start.6) | collective-permute-done | bytes 24608 | tf_op jit(solution)/shard_map/ppermute | solution.py:1134
  21.6 1.3 %collective-permute-start.9 = (f32[29,8,128]{2,1,0:T(8,128)S(1)}, f32[29,8,128]{2,1,0:T(8,128)S(1)}, u32[]{:S(2)}, u32[]{:S(2)}) collective-permute-start(f32[29,8,128]{2,1,0:T(8,128)S(1)} %join.1.joined), channel_id=1, source_target_pairs={{0,16},{16,0},{1,17},{17,1},{2,18},{18,2},{3,19},{19,3},{4,20},{20... | collective-permute-start | bytes 356360 | tf_op jit(solution)/shard_map/ppermute | solution.py:1039
  22.9 1.5 %inner_2.1 = (f32[16,72,384]{2,1,0:T(8,128)S(1)}, f32[8,128]{1,0:T(8,128)S(1)}) custom-call(f32[16,64,256]{2,1,0:T(8,128)S(1)} %get-tuple-element.52.s.refs_2_.refs_1_.refs_0_, f32[16,64,128]{2,1,0:T(8,128)S(1)} %get-tuple-element.64.refs_3_.refs_1_, f32[16,8,384]{2,1,0:T(8,128)S(1)} %get-tuple-element.72.refs_2_, ...), custom_call_target="tpu_custom_call" | custom-call | flops 1000 | bytes 7700000 | tf_op jit(solution)/shard_map/inner_2/pallas_call | solution.py:58
  24.3 1.7 %inner_3_4.1 = (f32[16,72,384]{2,1,0:T(8,128)S(1)}, f32[16,64,256]{2,1,0:T(8,128)S(1)}, f32[8,128]{1,0:T(8,128)S(1)}) custom-call(f32[16,64,256]{2,1,0:T(8,128)S(1)} %get-tuple-element.52.s.refs_2_.refs_1_.refs_0_, f32[16,64,128]{2,1,0:T(8,128)S(1)} %get-tuple-element.64.refs_3_.refs_1_, f32[16,8,384]{2,1,0:T(8,128)S(1)} %get-tuple-element.72.refs_2_, ...), custom_call_target="tpu_custom_call" | custom-call | flops 1000 | bytes 7700000 | tf_op jit(solution)/shard_map/inner_3_4/pallas_call | solution.py:58
  26.1 2.5 %collective-permute-start.10 = (f32[8,3,8,128]{3,2,1,0:T(8,128)S(1)}, f32[8,3,8,128]{3,2,1,0:T(8,128)S(1)}, u32[]{:S(2)}, u32[]{:S(2)}) collective-permute-start(f32[8,3,8,128]{3,2,1,0:T(8,128)S(1)} %split.1.cells), channel_id=1, source_target_pairs={{0,4},{4,0},{8,12},{12,8},{1,5},{5,1},{9,13},{13,9},{2,6},{6,2},{1... | collective-permute-start | bytes 294920 | tf_op jit(solution)/shard_map/ppermute | solution.py:1192
  28.6 2.2 %halo_sweeps.1 = (f32[16,72,384]{2,1,0:T(8,128)S(1)}, f32[8,72,384]{2,1,0:T(8,128)S(1)}, f32[16,72,384]{2,1,0:T(8,128)S(1)}, f32[16,72,384]{2,1,0:T(8,128)S(1)},...) custom-call(f32[16,64,256]{2,1,0:T(8,128)S(1)} %get-tuple-element.52.s.refs_2_.refs_1_.refs_0_, ...), custom_call_target="tpu_custom_call" | custom-call | flops 1000 | bytes 10500000 | tf_op jit(solution)/shard_map/halo_sweeps/pallas_call | solution.py:58
  30.9 2.4 %collective-permute-start.12 = (f32[16,3,8,128]{3,2,1,0:T(8,128)S(1)}, f32[16,3,8,128]{3,2,1,0:T(8,128)S(1)}, u32[]{:S(2)}, u32[]{:S(2)}) collective-permute-start(f32[16,3,8,128]{3,2,1,0:T(8,128)S(1)} %merge.4.cells), channel_id=1, source_target_pairs={{0,1},{1,0},{2,3},{3,2},{4,5},{5,4},{6,7},{7,6},{8,9},{9,8},{10,11... | collective-permute-start | bytes 589832 | tf_op jit(solution)/shard_map/ppermute | solution.py:1192
  33.3 1.5 %last_sweeps.1 = (f32[8,64,256]{2,1,0:T(8,128)S(1)}, f32[8,128]{1,0:T(8,128)S(1)}) custom-call(f32[16,64,256]{2,1,0:T(8,128)S(1)} %get-tuple-element.52.s.refs_2_.refs_1_.refs_0_, f32[16,64,128]{2,1,0:T(8,128)S(1)} %get-tuple-element.64.refs_3_.refs_1_, f32[16,8,384]{2,1,0:T(8,128)S(1)} %get-tuple-element.72.refs_2_, ...), custom_call_target="tpu_custom_call" | custom-call | flops 1000 | bytes 5600000 | tf_op jit(solution)/shard_map/last_sweeps/pallas_call | solution.py:58
  34.8 2.1 %solve.1 = f32[16,64,256]{2,1,0:T(8,128)} custom-call(f32[32,3,8,128]{3,2,1,0:T(8,128)S(1)} %merge.5.gathered, f32[16,64,256]{2,1,0:T(8,128)S(1)} %get-tuple-element.93.fine, f32[8,64,256]{2,1,0:T(8,128)S(1)} %get-tuple-element.94.edges), custom_call_target="tpu_custom_call" | custom-call | flops 1000 | bytes 7700000 | tf_op jit(solution)/shard_map/solve/pallas_call | solution.py:58
  (20 shorter events, 0.3 us)
Async XLA Ops:
  2.2 7.2 %collective-permute-start = (f32[2,64,256]{2,1,0:T(8,128)S(1)}, f32[2,64,256]{2,1,0:T(8,128)S(1)}, u32[]{:S(2)}, u32[]{:S(2)}) collective-permute-start(f32[2,64,256]{2,1,0:T(8,128)S(1)} %get-tuple-element.54), channel_id=1, source_target_pairs={{0,16},{16,0},{1,17},{17,1},{2,18},{18,2},{3,19},{19,3},{4,20},{20... | collective-permute-start | bytes 393224 | tf_op jit(solution)/shard_map/ppermute | solution.py:1039
  4.3 5.1 %collective-permute-start.3 = (f32[2,64,128]{2,1,0:T(8,128)S(1)}, f32[2,64,128]{2,1,0:T(8,128)S(1)}, u32[]{:S(2)}, u32[]{:S(2)}) collective-permute-start(f32[2,64,128]{2,1,0:T(8,128)S(1)} %get-tuple-element.57.refs_10_), channel_id=1, source_target_pairs={{0,1},{1,0},{2,3},{3,2},{4,5},{5,4},{6,7},{7,6},{8,9},{9,8},{10,11... | collective-permute-start | bytes 196616 | tf_op jit(solution)/shard_map/ppermute | solution.py:1039
  5.2 4.1 %collective-permute-start.4 = (f32[2,64,128]{2,1,0:T(8,128)S(1)}, f32[2,64,128]{2,1,0:T(8,128)S(1)}, u32[]{:S(2)}, u32[]{:S(2)}) collective-permute-start(f32[2,64,128]{2,1,0:T(8,128)S(1)} %get-tuple-element.58.refs_11_), channel_id=1, source_target_pairs={{1,2},{2,1},{3,0},{0,3},{5,6},{6,5},{7,4},{4,7},{9,10},{10,9},{11,... | collective-permute-start | bytes 196616 | tf_op jit(solution)/shard_map/ppermute | solution.py:1042
  6.4 3.0 %collective-permute-start.1 = (f32[2,16,256]{2,1,0:T(8,128)S(1)}, f32[2,16,256]{2,1,0:T(8,128)S(1)}, u32[]{:S(2)}, u32[]{:S(2)}) collective-permute-start(f32[2,16,256]{2,1,0:T(8,128)S(1)} %get-tuple-element.55.refs_6_), channel_id=1, source_target_pairs={{0,4},{4,0},{8,12},{12,8},{1,5},{5,1},{9,13},{13,9},{2,6},{6,2},{1... | collective-permute-start | bytes 98312 | tf_op jit(solution)/shard_map/ppermute | solution.py:1039
  7.7 1.7 %collective-permute-start.2 = (f32[2,16,256]{2,1,0:T(8,128)S(1)}, f32[2,16,256]{2,1,0:T(8,128)S(1)}, u32[]{:S(2)}, u32[]{:S(2)}) collective-permute-start(f32[2,16,256]{2,1,0:T(8,128)S(1)} %get-tuple-element.56.refs_7_), channel_id=1, source_target_pairs={{0,1},{1,0},{2,3},{3,2},{4,8},{5,9},{6,10},{7,11},{8,4},{9,5},{10,... | collective-permute-start | bytes 98312 | tf_op jit(solution)/shard_map/ppermute | solution.py:1045
  9.5 19.2 %collective-permute-start.11 = (f32[9,64,256]{2,1,0:T(8,128)S(1)}, f32[9,64,256]{2,1,0:T(8,128)S(1)}, u32[]{:S(2)}, u32[]{:S(2)}) collective-permute-start(f32[9,64,256]{2,1,0:T(8,128)S(1)} %pack_deep.1), channel_id=1, source_target_pairs={{0,16},{16,0},{1,17},{17,1},{2,18},{18,2},{3,19},{19,3},{4,20},{20... | collective-permute-start | bytes 1769480 | tf_op jit(solution)/shard_map/ppermute | solution.py:1039
  10.7 7.4 %collective-permute-start.7 = (f32[25,8,256]{2,1,0:T(8,128)S(1)}, f32[25,8,256]{2,1,0:T(8,128)S(1)}, u32[]{:S(2)}, u32[]{:S(2)}) collective-permute-start(f32[25,8,256]{2,1,0:T(8,128)S(1)} %get-tuple-element.61.refs_3_), channel_id=1, source_target_pairs={{0,4},{4,0},{8,12},{12,8},{1,5},{5,1},{9,13},{13,9},{2,6},{6,2},{1... | collective-permute-start | bytes 614408 | tf_op jit(solution)/shard_map/ppermute | solution.py:1039
  13.0 5.1 %collective-permute-start.8 = (f32[25,8,256]{2,1,0:T(8,128)S(1)}, f32[25,8,256]{2,1,0:T(8,128)S(1)}, u32[]{:S(2)}, u32[]{:S(2)}) collective-permute-start(f32[25,8,256]{2,1,0:T(8,128)S(1)} %get-tuple-element.70), channel_id=1, source_target_pairs={{0,1},{1,0},{2,3},{3,2},{4,8},{5,9},{6,10},{7,11},{8,4},{9,5},{10,... | collective-permute-start | bytes 614408 | tf_op jit(solution)/shard_map/ppermute | solution.py:1045
  15.1 2.8 %collective-permute-start.5 = (f32[1,3,8,128]{3,2,1,0:T(8,128)S(1)}, f32[1,3,8,128]{3,2,1,0:T(8,128)S(1)}, u32[]{:S(2)}, u32[]{:S(2)}) collective-permute-start(f32[1,3,8,128]{3,2,1,0:T(8,128)S(1)} %get-tuple-element.59.cells), channel_id=1, source_target_pairs={{0,2},{1,3},{2,0},{3,1},{4,6},{5,7},{6,4},{7,5},{8,10},{9,11},{10,... | collective-permute-start | bytes 36872 | tf_op jit(solution)/shard_map/ppermute | solution.py:1134
  17.9 3.6 %collective-permute-start.6 = (f32[2,3,8,128]{3,2,1,0:T(8,128)S(1)}, f32[2,3,8,128]{3,2,1,0:T(8,128)S(1)}, u32[]{:S(2)}, u32[]{:S(2)}) collective-permute-start(f32[2,3,8,128]{3,2,1,0:T(8,128)S(1)} %merge.3.cells), channel_id=1, source_target_pairs={{0,8},{4,12},{8,0},{12,4},{1,9},{5,13},{9,1},{13,5},{2,10},{6,14},... | collective-permute-start | bytes 73736 | tf_op jit(solution)/shard_map/ppermute | solution.py:1134
  21.6 4.5 %collective-permute-start.9 = (f32[29,8,128]{2,1,0:T(8,128)S(1)}, f32[29,8,128]{2,1,0:T(8,128)S(1)}, u32[]{:S(2)}, u32[]{:S(2)}) collective-permute-start(f32[29,8,128]{2,1,0:T(8,128)S(1)} %join.1.joined), channel_id=1, source_target_pairs={{0,16},{16,0},{1,17},{17,1},{2,18},{18,2},{3,19},{19,3},{4,20},{20... | collective-permute-start | bytes 356360 | tf_op jit(solution)/shard_map/ppermute | solution.py:1039
  26.1 4.8 %collective-permute-start.10 = (f32[8,3,8,128]{3,2,1,0:T(8,128)S(1)}, f32[8,3,8,128]{3,2,1,0:T(8,128)S(1)}, u32[]{:S(2)}, u32[]{:S(2)}) collective-permute-start(f32[8,3,8,128]{3,2,1,0:T(8,128)S(1)} %split.1.cells), channel_id=1, source_target_pairs={{0,4},{4,0},{8,12},{12,8},{1,5},{5,1},{9,13},{13,9},{2,6},{6,2},{1... | collective-permute-start | bytes 294920 | tf_op jit(solution)/shard_map/ppermute | solution.py:1192
  30.9 3.9 %collective-permute-start.12 = (f32[16,3,8,128]{3,2,1,0:T(8,128)S(1)}, f32[16,3,8,128]{3,2,1,0:T(8,128)S(1)}, u32[]{:S(2)}, u32[]{:S(2)}) collective-permute-start(f32[16,3,8,128]{3,2,1,0:T(8,128)S(1)} %merge.4.cells), channel_id=1, source_target_pairs={{0,1},{1,0},{2,3},{3,2},{4,5},{5,4},{6,7},{7,6},{8,9},{9,8},{10,11... | collective-permute-start | bytes 589832 | tf_op jit(solution)/shard_map/ppermute | solution.py:1192

commit v7 on v6

--- a/solution.py
+++ b/solution.py
@@ -52,14 +52,14 @@
     return pltpu.with_memory_space_constraint(value, pltpu.VMEM)
 
 
-def run(kernel, outs, args, scratch=(), us=1.0, name=None, spaces=None, far=False, aliases=None):
+def run(kernel, outs, args, scratch=(), us=1.0, name=None, spaces=None, far=False, far_out=False, aliases=None):
     whole = pl.BlockSpec(memory_space=pltpu.VMEM)
     shapes = [pltpu.VMEM(shape, F32) for shape in outs] if spaces is None else spaces
     return pl.pallas_call(
         kernel,
         out_shape=shapes,
         in_specs=[pl.BlockSpec(memory_space=pltpu.HBM) if far else whole] * len(args),
-        out_specs=[whole] * len(outs),
+        out_specs=[pl.BlockSpec(memory_space=pltpu.HBM) if far_out else whole] * len(outs),
         scratch_shapes=list(scratch),
         input_output_aliases=aliases or {},
         compiler_params=pltpu.CompilerParams(vmem_limit_bytes=VMEM_LIMIT),
@@ -126,6 +126,7 @@
         assert 2 * DEPTH == ROWS and 2 * self.Z <= SLOTS and self.Z % 2 == 0
         assert self.blocks * LANES <= self.X and self.cy == ROWS
         assert self.cx * self.nx == LANES
+        assert 2 * (5 * self.cz % self.nx) == self.nx and self.nx == 4 and self.ny > 2
 
     def where(self):
         return lax.axis_index("gx"), lax.axis_index("gy"), lax.axis_index("gz")
@@ -528,6 +529,10 @@
 def coarse_blocks(g):
     per = LANES // g.cx
     return -(-5 * g.cz // per)
+
+
+def pair_blocks(g):
+    return 2 * coarse_blocks(g) - 1
 
 
 def relay_rows(q, d):
@@ -910,7 +915,7 @@
     sweep_kernel(g, 4, False, *common, v[1], between, *beyond_own, out, token)
 
 
-def solve_kernel(g, gathered, fine, edges, out):
+def solve_kernel(g, gathered, fine, edges, out, buffer, sems):
     zi, yi, xi = g.where()
     per = LANES // g.cx
     group = lane_of((ROWS, LANES)) // g.cx
@@ -928,6 +933,11 @@
 
     def relative(a, b, c):
         return jnp.bitwise_xor(here, place(a, b, c))
+
+    last = coarse_blocks(g) - 1
+
+    def block_of(at, block):
+        return gathered[at >> 1, 2 * last if block == last else (at & 1) * last + block]
 
     layers = g.nz * g.cz
     height = g.ny * g.cy
@@ -939,10 +949,10 @@
             m = q * g.cz + cz
             tiles = []
             for b in range(g.ny):
-                value = gathered[relative(a, b, 0), m // per]
+                value = block_of(relative(a, b, 0), m // per)
                 for c in range(1, g.nx):
                     value = jnp.where(
-                        group == (m % per + c) % per, gathered[relative(a, b, c), m // per], value
+                        group == (m % per + c) % per, block_of(relative(a, b, c), m // per), value
                     )
                 tiles.append(roll(value, -(m % per) * g.cx, 1))
             planes.append(jnp.concatenate(tiles, axis=0))
@@ -967,10 +977,26 @@
             result.append(total)
         return result
 
-    e = [sc * r for sc, r in zip(scale, rhs)]
+    start = [sc * r for sc, r in zip(scale, rhs)]
+    below_y = [sc * w for sc, w in zip(scale, wy)]
+    above_y = [sc * roll(w, -1, 0) for sc, w in zip(scale, wy)]
+    below_x = [sc * w for sc, w in zip(scale, wx)]
+    above_x = [sc * roll(w, -1, 1) for sc, w in zip(scale, wx)]
+    below_z = [sc * w for sc, w in zip(scale, wz)]
+    above_z = [sc * w for sc, w in zip(scale, wz[1:])]
+    e = start
     for _ in range(COARSE_SWEEPS - 1):
-        f = flux(e)
-        e = [(1.0 - OMEGA_COARSE) * e[i] + scale[i] * (rhs[i] + f[i]) for i in range(layers)]
+        new = []
+        for i in range(layers):
+            total = start[i] + (1.0 - OMEGA_COARSE) * e[i]
+            if i > 0:
+                total = total + below_z[i] * e[i - 1]
+            if i < layers - 1:
+                total = total + above_z[i] * e[i + 1]
+            total = total + below_y[i] * roll(e[i], 1, 0) + above_y[i] * roll(e[i], -1, 0)
+            total = total + below_x[i] * roll(e[i], 1, 1) + above_x[i] * roll(e[i], -1, 1)
+            new.append(total)
+        e = new
     f = flux(e)
     left = zero
     total = zero
@@ -992,14 +1018,22 @@
         == xi * g.cx + lax.broadcasted_iota(jnp.int32, (LANES, g.X), 1) // RATIO
     ).astype(jnp.bfloat16)
     wide = exact_dot(jnp.concatenate(own, axis=0), onehot) + shift
+    copies = []
     for cz in range(g.cz):
         block = wide[cz * ROWS : (cz + 1) * ROWS]
         spread = jnp.broadcast_to(block[:, None, :], (g.cy, RATIO, g.X)).reshape(g.Y, g.X)
         for z in range(cz * RATIO, (cz + 1) * RATIO):
             if DEPTH <= z < g.Z - DEPTH:
-                out[z] = fine[z] + spread
+                buffer[z] = fine[z] + spread
             else:
-                out[z] = edges[beyond(g, z) - DEPTH] + spread
+                buffer[z] = edges[beyond(g, z) - DEPTH] + spread
+            if z % DEPTH == DEPTH - 1:
+                part = pl.ds(z + 1 - DEPTH, DEPTH)
+                copy = pltpu.make_async_copy(buffer.at[part], out.at[part], sems.at[z // DEPTH])
+                copy.start()
+                copies.append(copy)
+    for copy in copies:
+        copy.wait()
 
 
 def copy_kernel(source, out):
@@ -1012,8 +1046,16 @@
     out[count:] = got[...]
 
 
+def pair_kernel(g, cells, got, token, out):
+    last = coarse_blocks(g) - 1
+    for block in range(last):
+        out[0, block] = cells[0, block]
+        out[0, last + block] = got[0, block]
+    out[0, 2 * last] = cells[0, last] + got[0, last]
+
+
 def join_kernel(g, cells, got, relay, out):
-    nc = coarse_blocks(g)
+    nc = pair_blocks(g)
     count = cells.shape[0]
     for at in range(count):
         out[at * nc : (at + 1) * nc] = cells[at]
@@ -1022,7 +1064,7 @@
 
 
 def split_kernel(g, joined, got, token, out):
-    nc = coarse_blocks(g)
+    nc = pair_blocks(g)
     count = out.shape[0] // 2
     for at in range(count):
         out[at] = joined[at * nc : (at + 1) * nc]
@@ -1054,7 +1096,7 @@
     y_shape = (3 * Z // 2 + 1, ROWS, X)
     sums_shape = (5, g.cz, ROWS, X)
     main = (Z, Y, g.XE)
-    nc, nr = coarse_blocks(g), relay_blocks(g)
+    nc, nr = pair_blocks(g), relay_blocks(g)
 
     sent = run(
         functools.partial(pack_kernel, g),
@@ -1132,8 +1174,14 @@
     before, _, after = g.steps()
     for number, (axis, bit) in enumerate(before):
         got = lax.ppermute(cells, axis, flips(lax.axis_size(axis), bit))
-        if number < len(before) - 1:
-            cells = merge(cells, got, token_w)
+        if number == 0:
+            (cells,) = run(
+                functools.partial(pair_kernel, g),
+                [(1, nc) + tile],
+                [cells, got, token_w],
+                us=0.05,
+                name="pair",
+            )
     count = 2 * cells.shape[0]
     (joined,) = run(
         functools.partial(join_kernel, g),
@@ -1197,7 +1245,9 @@
         [(Z, Y, X)],
         [cells, v, vh],
         us=US["solve"],
+        scratch=[pltpu.VMEM((Z, Y, X), F32), pltpu.SemaphoreType.DMA((Z // DEPTH,))],
         name="solve",
+        far_out=True,
         spaces=[jax.ShapeDtypeStruct((Z, Y, X), F32)],
     )
     return out

time: 37.1 us -> 36.8 us (level)
  no operation moved by 1% of the time
where the time goes in v7:
time: 36.8 us; the launch traced here: 36.7 us
  Pallas kernels  18.7 us (51%)
  starting transfers between devices  17.3 us (47%)
  waiting for transfers between devices  0.44 us (1%)
    pallas_call x18, Pallas kernels, run(): pl.pallas_call(kernel, out_shape=shapes, in_specs=[pl.BlockSpec(memory_sp...  18.7 us
    ppermute x6, starting transfers between devices, exchange(): got = [lax.ppermute(bufs[0], axis, pairs(count, 0))]  8.32 us
    ppermute x4, starting transfers between devices, shards(): got = lax.ppermute(cells, axis, flips(lax.axis_size(axis), bit))  4.94 us
    ppermute x2, starting transfers between devices, exchange(): got.append(lax.ppermute(bufs[1], (axis, beside), perm))  2.87 us
    ppermute x1, starting transfers between devices, exchange(): got.append(lax.ppermute(bufs[1], axis, pairs(count, 1)))  1.13 us
  transfers between devices with their start and end apart: 13, of which 1 were waited for; matrix products, arithmetic and copies ran while one was open for 0% of the time, Pallas kernels for 39%

profile of v7, /device:TPU:1, one launch (start us, length us, event | category | flops | bytes accessed | tf_op | source)
XLA Modules:
  0.0 36.7 jit_solution(16671689191363290192)
XLA Ops:
  0.0 2.2 %pack_faces.1 = (f32[16,64,256]{2,1,0:T(8,128)S(1)}, f32[16,64,256]{2,1,0:T(8,128)S(1)}, f32[16,64,256]{2,1,0:T(8,128)S(1)}, f32[2,64,256]{2,1,0:T(8,128)S(1)}, ...) custom-call(f32[16,64,256]{2,1,0:T(8,128)} %refs_0_.1, ...), custom_call_target="tpu_custom_call" | custom-call | flops 1000 | bytes 3500000 | tf_op jit(solution)/shard_map/pack_faces/pallas_call | solution.py:58
  2.2 2.1 %collective-permute-start = (f32[2,64,256]{2,1,0:T(8,128)S(1)}, f32[2,64,256]{2,1,0:T(8,128)S(1)}, u32[]{:S(2)}, u32[]{:S(2)}) collective-permute-start(f32[2,64,256]{2,1,0:T(8,128)S(1)} %get-tuple-element.54), channel_id=1, source_target_pairs={{0,16},{16,0},{1,17},{17,1},{2,18},{18,2},{3,19},{19,3},{4,20},{20... | collective-permute-start | bytes 393224 | tf_op jit(solution)/shard_map/ppermute | solution.py:1081
  4.3 1.0 %collective-permute-start.3 = (f32[2,64,128]{2,1,0:T(8,128)S(1)}, f32[2,64,128]{2,1,0:T(8,128)S(1)}, u32[]{:S(2)}, u32[]{:S(2)}) collective-permute-start(f32[2,64,128]{2,1,0:T(8,128)S(1)} %get-tuple-element.57.refs_10_), channel_id=1, source_target_pairs={{0,1},{1,0},{2,3},{3,2},{4,5},{5,4},{6,7},{7,6},{8,9},{9,8},{10,11... | collective-permute-start | bytes 196616 | tf_op jit(solution)/shard_map/ppermute | solution.py:1081
  5.2 1.1 %collective-permute-start.4 = (f32[2,64,128]{2,1,0:T(8,128)S(1)}, f32[2,64,128]{2,1,0:T(8,128)S(1)}, u32[]{:S(2)}, u32[]{:S(2)}) collective-permute-start(f32[2,64,128]{2,1,0:T(8,128)S(1)} %get-tuple-element.58.refs_11_), channel_id=1, source_target_pairs={{1,2},{2,1},{3,0},{0,3},{5,6},{6,5},{7,4},{4,7},{9,10},{10,9},{11,... | collective-permute-start | bytes 196616 | tf_op jit(solution)/shard_map/ppermute | solution.py:1084
  6.4 1.3 %collective-permute-start.1 = (f32[2,16,256]{2,1,0:T(8,128)S(1)}, f32[2,16,256]{2,1,0:T(8,128)S(1)}, u32[]{:S(2)}, u32[]{:S(2)}) collective-permute-start(f32[2,16,256]{2,1,0:T(8,128)S(1)} %get-tuple-element.55.refs_6_), channel_id=1, source_target_pairs={{0,4},{4,0},{8,12},{12,8},{1,5},{5,1},{9,13},{13,9},{2,6},{6,2},{1... | collective-permute-start | bytes 98312 | tf_op jit(solution)/shard_map/ppermute | solution.py:1081
  7.7 0.8 %collective-permute-start.2 = (f32[2,16,256]{2,1,0:T(8,128)S(1)}, f32[2,16,256]{2,1,0:T(8,128)S(1)}, u32[]{:S(2)}, u32[]{:S(2)}) collective-permute-start(f32[2,16,256]{2,1,0:T(8,128)S(1)} %get-tuple-element.56.refs_7_), channel_id=1, source_target_pairs={{0,1},{1,0},{2,3},{3,2},{4,8},{5,9},{6,10},{7,11},{8,4},{9,5},{10,... | collective-permute-start | bytes 98312 | tf_op jit(solution)/shard_map/ppermute | solution.py:1087
  8.4 0.9 %local_sums.1 = (f32[5,2,8,256]{3,2,1,0:T(8,128)S(1)}, f32[8,128]{1,0:T(8,128)S(1)}) custom-call(f32[16,64,256]{2,1,0:T(8,128)S(1)} %get-tuple-element.50.p.refs_0_.refs_11_, f32[16,64,256]{2,1,0:T(8,128)S(1)} %get-tuple-element.51.k.refs_1_.refs_0_.refs_5_.refs_15_, f32[16,64,256]{2,1,0:T(8,128)S(1)} %get-tuple-element.52.s.refs_2_.refs_1_.refs_0_), custom_call_target="tpu_custom_call" | custom-call | flops 1000 | bytes 4200000 | tf_op jit(solution)/shard_map/local_sums/pallas_call | solution.py:58
  9.5 0.4 %collective-permute-start.11 = (f32[9,64,256]{2,1,0:T(8,128)S(1)}, f32[9,64,256]{2,1,0:T(8,128)S(1)}, u32[]{:S(2)}, u32[]{:S(2)}) collective-permute-start(f32[9,64,256]{2,1,0:T(8,128)S(1)} %pack_deep.1), channel_id=1, source_target_pairs={{0,16},{16,0},{1,17},{17,1},{2,18},{18,2},{3,19},{19,3},{4,20},{20... | collective-permute-start | bytes 1769480 | tf_op jit(solution)/shard_map/ppermute | solution.py:1081
  9.8 0.7 %restrict.1 = (f32[1,3,8,128]{3,2,1,0:T(8,128)S(1)}, f32[8,128]{1,0:T(8,128)S(1)}) custom-call(f32[16,64,256]{2,1,0:T(8,128)S(1)} %get-tuple-element.50.p.refs_0_.refs_11_, f32[16,64,256]{2,1,0:T(8,128)S(1)} %get-tuple-element.51.k.refs_1_.refs_0_.refs_5_.refs_15_, f32[5,2,8,256]{3,2,1,0:T(8,128)S(1)} %get-tuple-element.53.refs_2_, ...), custom_call_target="tpu_custom_call" | custom-call | flops 1000 | bytes 2100000 | tf_op jit(solution)/shard_map/restrict/pallas_call | solution.py:58
  10.7 2.3 %collective-permute-start.7 = (f32[25,8,256]{2,1,0:T(8,128)S(1)}, f32[25,8,256]{2,1,0:T(8,128)S(1)}, u32[]{:S(2)}, u32[]{:S(2)}) collective-permute-start(f32[25,8,256]{2,1,0:T(8,128)S(1)} %get-tuple-element.61.refs_3_), channel_id=1, source_target_pairs={{0,4},{4,0},{8,12},{12,8},{1,5},{5,1},{9,13},{13,9},{2,6},{6,2},{1... | collective-permute-start | bytes 614408 | tf_op jit(solution)/shard_map/ppermute | solution.py:1081
  13.0 2.1 %collective-permute-start.8 = (f32[25,8,256]{2,1,0:T(8,128)S(1)}, f32[25,8,256]{2,1,0:T(8,128)S(1)}, u32[]{:S(2)}, u32[]{:S(2)}) collective-permute-start(f32[25,8,256]{2,1,0:T(8,128)S(1)} %get-tuple-element.70), channel_id=1, source_target_pairs={{0,1},{1,0},{2,3},{3,2},{4,8},{5,9},{6,10},{7,11},{8,4},{9,5},{10,... | collective-permute-start | bytes 614408 | tf_op jit(solution)/shard_map/ppermute | solution.py:1087
  15.1 0.2 collective-permute-start.5
  15.3 2.6 %weights.1 = (f32[16,64,128]{2,1,0:T(8,128)S(1)}, f32[16,64,128]{2,1,0:T(8,128)S(1)}, f32[16,64,128]{2,1,0:T(8,128)S(1)}, f32[16,64,384]{2,1,0:T(8,128)S(1)}, f3...) custom-call(f32[16,64,256]{2,1,0:T(8,128)S(1)} %get-tuple-element.51.k, ...), custom_call_target="tpu_custom_call" | custom-call | flops 1000 | bytes 14000000 | tf_op jit(solution)/shard_map/weights/pallas_call | solution.py:58
  17.9 0.1 collective-permute-start.6
  18.1 3.0 %extend.1 = (f32[16,8,384]{2,1,0:T(8,128)S(1)}, f32[16,8,384]{2,1,0:T(8,128)S(1)}, f32[16,8,384]{2,1,0:T(8,128)S(1)}, f32[16,8,384]{2,1,0:T(8,128)S(1)}, f32[16,...) custom-call(f32[16,64,256]{2,1,0:T(8,128)S(1)} %get-tuple-element.50, ...), custom_call_target="tpu_custom_call" | custom-call | flops 1000 | bytes 11200000 | tf_op jit(solution)/shard_map/extend/pallas_call | solution.py:58
  21.1 0.4 %collective-permute-done.6.got = f32[1,5,8,128]{3,2,1,0:T(8,128)S(1)} collective-permute-done((f32[1,5,8,128]{3,2,1,0:T(8,128)S(1)}, f32[1,5,8,128]{3,2,1,0:T(8,128)S(1)}, u32[]{:S(2)}, u32[]{:S(2)}) %collective-permute-start.6) | collective-permute-done | bytes 20512 | tf_op jit(solution)/shard_map/ppermute | solution.py:1176
  21.5 1.3 %collective-permute-start.9 = (f32[27,8,128]{2,1,0:T(8,128)S(1)}, f32[27,8,128]{2,1,0:T(8,128)S(1)}, u32[]{:S(2)}, u32[]{:S(2)}) collective-permute-start(f32[27,8,128]{2,1,0:T(8,128)S(1)} %join.1.joined), channel_id=1, source_target_pairs={{0,16},{16,0},{1,17},{17,1},{2,18},{18,2},{3,19},{19,3},{4,20},{20... | collective-permute-start | bytes 331784 | tf_op jit(solution)/shard_map/ppermute | solution.py:1081
  22.8 1.5 %inner_2.1 = (f32[16,72,384]{2,1,0:T(8,128)S(1)}, f32[8,128]{1,0:T(8,128)S(1)}) custom-call(f32[16,64,256]{2,1,0:T(8,128)S(1)} %get-tuple-element.52.s.refs_2_.refs_1_.refs_0_, f32[16,64,128]{2,1,0:T(8,128)S(1)} %get-tuple-element.64.refs_3_.refs_1_, f32[16,8,384]{2,1,0:T(8,128)S(1)} %get-tuple-element.72.refs_2_, ...), custom_call_target="tpu_custom_call" | custom-call | flops 1000 | bytes 7700000 | tf_op jit(solution)/shard_map/inner_2/pallas_call | solution.py:58
  24.3 1.8 %inner_3_4.1 = (f32[16,72,384]{2,1,0:T(8,128)S(1)}, f32[16,64,256]{2,1,0:T(8,128)S(1)}, f32[8,128]{1,0:T(8,128)S(1)}) custom-call(f32[16,64,256]{2,1,0:T(8,128)S(1)} %get-tuple-element.52.s.refs_2_.refs_1_.refs_0_, f32[16,64,128]{2,1,0:T(8,128)S(1)} %get-tuple-element.64.refs_3_.refs_1_, f32[16,8,384]{2,1,0:T(8,128)S(1)} %get-tuple-element.72.refs_2_, ...), custom_call_target="tpu_custom_call" | custom-call | flops 1000 | bytes 7700000 | tf_op jit(solution)/shard_map/inner_3_4/pallas_call | solution.py:58
  26.1 2.5 %collective-permute-start.10 = (f32[4,5,8,128]{3,2,1,0:T(8,128)S(1)}, f32[4,5,8,128]{3,2,1,0:T(8,128)S(1)}, u32[]{:S(2)}, u32[]{:S(2)}) collective-permute-start(f32[4,5,8,128]{3,2,1,0:T(8,128)S(1)} %split.1.cells), channel_id=1, source_target_pairs={{0,4},{4,0},{8,12},{12,8},{1,5},{5,1},{9,13},{13,9},{2,6},{6,2},{1... | collective-permute-start | bytes 245768 | tf_op jit(solution)/shard_map/ppermute | solution.py:1240
  28.6 2.2 %halo_sweeps.1 = (f32[16,72,384]{2,1,0:T(8,128)S(1)}, f32[8,72,384]{2,1,0:T(8,128)S(1)}, f32[16,72,384]{2,1,0:T(8,128)S(1)}, f32[16,72,384]{2,1,0:T(8,128)S(1)},...) custom-call(f32[16,64,256]{2,1,0:T(8,128)S(1)} %get-tuple-element.52.s.refs_2_.refs_1_.refs_0_, ...), custom_call_target="tpu_custom_call" | custom-call | flops 1000 | bytes 10500000 | tf_op jit(solution)/shard_map/halo_sweeps/pallas_call | solution.py:58
  30.9 2.1 %collective-permute-start.12 = (f32[8,5,8,128]{3,2,1,0:T(8,128)S(1)}, f32[8,5,8,128]{3,2,1,0:T(8,128)S(1)}, u32[]{:S(2)}, u32[]{:S(2)}) collective-permute-start(f32[8,5,8,128]{3,2,1,0:T(8,128)S(1)} %merge.2.cells), channel_id=1, source_target_pairs={{0,1},{1,0},{2,3},{3,2},{4,5},{5,4},{6,7},{7,6},{8,9},{9,8},{10,11... | collective-permute-start | bytes 491528 | tf_op jit(solution)/shard_map/ppermute | solution.py:1240
  33.0 1.5 %last_sweeps.1 = (f32[8,64,256]{2,1,0:T(8,128)S(1)}, f32[8,128]{1,0:T(8,128)S(1)}) custom-call(f32[16,64,256]{2,1,0:T(8,128)S(1)} %get-tuple-element.52.s.refs_2_.refs_1_.refs_0_, f32[16,64,128]{2,1,0:T(8,128)S(1)} %get-tuple-element.64.refs_3_.refs_1_, f32[16,8,384]{2,1,0:T(8,128)S(1)} %get-tuple-element.72.refs_2_, ...), custom_call_target="tpu_custom_call" | custom-call | flops 1000 | bytes 5600000 | tf_op jit(solution)/shard_map/last_sweeps/pallas_call | solution.py:58
  34.5 2.0 %solve.1 = f32[16,64,256]{2,1,0:T(8,128)} custom-call(f32[16,5,8,128]{3,2,1,0:T(8,128)S(1)} %merge.3.gathered, f32[16,64,256]{2,1,0:T(8,128)S(1)} %get-tuple-element.93.fine, f32[8,64,256]{2,1,0:T(8,128)S(1)} %get-tuple-element.94.edges), custom_call_target="tpu_custom_call" | custom-call | flops 1000 | bytes 7700000 | tf_op jit(solution)/shard_map/solve/pallas_call | solution.py:58
  (20 shorter events, 0.2 us)
Async XLA Ops:
  2.2 7.2 %collective-permute-start = (f32[2,64,256]{2,1,0:T(8,128)S(1)}, f32[2,64,256]{2,1,0:T(8,128)S(1)}, u32[]{:S(2)}, u32[]{:S(2)}) collective-permute-start(f32[2,64,256]{2,1,0:T(8,128)S(1)} %get-tuple-element.54), channel_id=1, source_target_pairs={{0,16},{16,0},{1,17},{17,1},{2,18},{18,2},{3,19},{19,3},{4,20},{20... | collective-permute-start | bytes 393224 | tf_op jit(solution)/shard_map/ppermute | solution.py:1081
  4.3 5.1 %collective-permute-start.3 = (f32[2,64,128]{2,1,0:T(8,128)S(1)}, f32[2,64,128]{2,1,0:T(8,128)S(1)}, u32[]{:S(2)}, u32[]{:S(2)}) collective-permute-start(f32[2,64,128]{2,1,0:T(8,128)S(1)} %get-tuple-element.57.refs_10_), channel_id=1, source_target_pairs={{0,1},{1,0},{2,3},{3,2},{4,5},{5,4},{6,7},{7,6},{8,9},{9,8},{10,11... | collective-permute-start | bytes 196616 | tf_op jit(solution)/shard_map/ppermute | solution.py:1081
  5.2 4.1 %collective-permute-start.4 = (f32[2,64,128]{2,1,0:T(8,128)S(1)}, f32[2,64,128]{2,1,0:T(8,128)S(1)}, u32[]{:S(2)}, u32[]{:S(2)}) collective-permute-start(f32[2,64,128]{2,1,0:T(8,128)S(1)} %get-tuple-element.58.refs_11_), channel_id=1, source_target_pairs={{1,2},{2,1},{3,0},{0,3},{5,6},{6,5},{7,4},{4,7},{9,10},{10,9},{11,... | collective-permute-start | bytes 196616 | tf_op jit(solution)/shard_map/ppermute | solution.py:1084
  6.4 3.0 %collective-permute-start.1 = (f32[2,16,256]{2,1,0:T(8,128)S(1)}, f32[2,16,256]{2,1,0:T(8,128)S(1)}, u32[]{:S(2)}, u32[]{:S(2)}) collective-permute-start(f32[2,16,256]{2,1,0:T(8,128)S(1)} %get-tuple-element.55.refs_6_), channel_id=1, source_target_pairs={{0,4},{4,0},{8,12},{12,8},{1,5},{5,1},{9,13},{13,9},{2,6},{6,2},{1... | collective-permute-start | bytes 98312 | tf_op jit(solution)/shard_map/ppermute | solution.py:1081
  7.7 1.7 %collective-permute-start.2 = (f32[2,16,256]{2,1,0:T(8,128)S(1)}, f32[2,16,256]{2,1,0:T(8,128)S(1)}, u32[]{:S(2)}, u32[]{:S(2)}) collective-permute-start(f32[2,16,256]{2,1,0:T(8,128)S(1)} %get-tuple-element.56.refs_7_), channel_id=1, source_target_pairs={{0,1},{1,0},{2,3},{3,2},{4,8},{5,9},{6,10},{7,11},{8,4},{9,5},{10,... | collective-permute-start | bytes 98312 | tf_op jit(solution)/shard_map/ppermute | solution.py:1087
  9.5 19.2 %collective-permute-start.11 = (f32[9,64,256]{2,1,0:T(8,128)S(1)}, f32[9,64,256]{2,1,0:T(8,128)S(1)}, u32[]{:S(2)}, u32[]{:S(2)}) collective-permute-start(f32[9,64,256]{2,1,0:T(8,128)S(1)} %pack_deep.1), channel_id=1, source_target_pairs={{0,16},{16,0},{1,17},{17,1},{2,18},{18,2},{3,19},{19,3},{4,20},{20... | collective-permute-start | bytes 1769480 | tf_op jit(solution)/shard_map/ppermute | solution.py:1081
  10.7 7.4 %collective-permute-start.7 = (f32[25,8,256]{2,1,0:T(8,128)S(1)}, f32[25,8,256]{2,1,0:T(8,128)S(1)}, u32[]{:S(2)}, u32[]{:S(2)}) collective-permute-start(f32[25,8,256]{2,1,0:T(8,128)S(1)} %get-tuple-element.61.refs_3_), channel_id=1, source_target_pairs={{0,4},{4,0},{8,12},{12,8},{1,5},{5,1},{9,13},{13,9},{2,6},{6,2},{1... | collective-permute-start | bytes 614408 | tf_op jit(solution)/shard_map/ppermute | solution.py:1081
  13.0 5.1 %collective-permute-start.8 = (f32[25,8,256]{2,1,0:T(8,128)S(1)}, f32[25,8,256]{2,1,0:T(8,128)S(1)}, u32[]{:S(2)}, u32[]{:S(2)}) collective-permute-start(f32[25,8,256]{2,1,0:T(8,128)S(1)} %get-tuple-element.70), channel_id=1, source_target_pairs={{0,1},{1,0},{2,3},{3,2},{4,8},{5,9},{6,10},{7,11},{8,4},{9,5},{10,... | collective-permute-start | bytes 614408 | tf_op jit(solution)/shard_map/ppermute | solution.py:1087
  15.1 2.9 %collective-permute-start.5 = (f32[1,3,8,128]{3,2,1,0:T(8,128)S(1)}, f32[1,3,8,128]{3,2,1,0:T(8,128)S(1)}, u32[]{:S(2)}, u32[]{:S(2)}) collective-permute-start(f32[1,3,8,128]{3,2,1,0:T(8,128)S(1)} %get-tuple-element.59.cells), channel_id=1, source_target_pairs={{0,2},{1,3},{2,0},{3,1},{4,6},{5,7},{6,4},{7,5},{8,10},{9,11},{10,... | collective-permute-start | bytes 36872 | tf_op jit(solution)/shard_map/ppermute | solution.py:1176
  17.9 3.6 %collective-permute-start.6 = (f32[1,5,8,128]{3,2,1,0:T(8,128)S(1)}, f32[1,5,8,128]{3,2,1,0:T(8,128)S(1)}, u32[]{:S(2)}, u32[]{:S(2)}) collective-permute-start(f32[1,5,8,128]{3,2,1,0:T(8,128)S(1)} %pair.1.cells), channel_id=1, source_target_pairs={{0,8},{4,12},{8,0},{12,4},{1,9},{5,13},{9,1},{13,5},{2,10},{6,14},... | collective-permute-start | bytes 61448 | tf_op jit(solution)/shard_map/ppermute | solution.py:1176
  21.5 4.6 %collective-permute-start.9 = (f32[27,8,128]{2,1,0:T(8,128)S(1)}, f32[27,8,128]{2,1,0:T(8,128)S(1)}, u32[]{:S(2)}, u32[]{:S(2)}) collective-permute-start(f32[27,8,128]{2,1,0:T(8,128)S(1)} %join.1.joined), channel_id=1, source_target_pairs={{0,16},{16,0},{1,17},{17,1},{2,18},{18,2},{3,19},{19,3},{4,20},{20... | collective-permute-start | bytes 331784 | tf_op jit(solution)/shard_map/ppermute | solution.py:1081
  26.1 4.8 %collective-permute-start.10 = (f32[4,5,8,128]{3,2,1,0:T(8,128)S(1)}, f32[4,5,8,128]{3,2,1,0:T(8,128)S(1)}, u32[]{:S(2)}, u32[]{:S(2)}) collective-permute-start(f32[4,5,8,128]{3,2,1,0:T(8,128)S(1)} %split.1.cells), channel_id=1, source_target_pairs={{0,4},{4,0},{8,12},{12,8},{1,5},{5,1},{9,13},{13,9},{2,6},{6,2},{1... | collective-permute-start | bytes 245768 | tf_op jit(solution)/shard_map/ppermute | solution.py:1240
  30.9 3.6 %collective-permute-start.12 = (f32[8,5,8,128]{3,2,1,0:T(8,128)S(1)}, f32[8,5,8,128]{3,2,1,0:T(8,128)S(1)}, u32[]{:S(2)}, u32[]{:S(2)}) collective-permute-start(f32[8,5,8,128]{3,2,1,0:T(8,128)S(1)} %merge.2.cells), channel_id=1, source_target_pairs={{0,1},{1,0},{2,3},{3,2},{4,5},{5,4},{6,7},{7,6},{8,9},{9,8},{10,11... | collective-permute-start | bytes 491528 | tf_op jit(solution)/shard_map/ppermute | solution.py:1240

commit v8 on v7

--- a/solution.py
+++ b/solution.py
@@ -153,24 +153,16 @@
     y_out = refs[n : n + g.ysides]
     sems = refs[n + g.ysides]
     zi, yi, xi = g.where()
-    copies = []
-
-    def send(q, at, size, out, place):
-        source = src[q].at[pl.ds(at, size)]
-        target = out.at[pl.ds(place, size)]
-        copies.append(pltpu.make_async_copy(source, target, sems.at[3 + len(copies)]))
-
-    for side in range(g.zsides):
-        high = (zi % 2) == side
-        for q in range(2):
-            send(q, jnp.where(high, g.Z - 1, 0), 1, near[side], q)
     loads = [pltpu.make_async_copy(src[q], fields[q], sems.at[q]) for q in range(3)]
-    for copy in loads + copies:
+    for copy in loads:
         copy.start()
     lane = lane_of((g.Y, LANES))
     packs = [[jnp.zeros((g.Y, LANES), F32) for _ in range(g.blocks)] for _ in range(2)]
     for q in range(3):
         loads[q].wait()
+        if q < 2:
+            for side, out in enumerate(near):
+                out[q] = fields[q][jnp.where((zi % 2) == side, g.Z - 1, 0)]
         for z in range(g.Z):
             block, at = g.slot(q, z)
             pack = packs[(at // DEPTH) % 2]
@@ -193,8 +185,6 @@
         hi = roll(jnp.where(first_half, packs[1][block], packs[0][block]), DEPTH, 1)
         for side, out in enumerate(x_out):
             out[block] = jnp.where(even == (side == 0), hi, lo)
-    for copy in copies:
-        copy.wait()
 
 
 def pick(first, second, even, inside):
@@ -1105,7 +1095,7 @@
         + [x_shape] * g.xsides
         + [(2, Z, X)] * g.ysides,
         [pressure_start, permeability, source],
-        scratch=[pltpu.SemaphoreType.DMA((3 + 2 * g.zsides,))],
+        scratch=[pltpu.SemaphoreType.DMA((3,))],
         name="pack_faces",
         far=True,
     )

time: 36.8 us -> 36.8 us (level)
  no operation moved by 1% of the time
where the time goes in v8:
time: 36.8 us; the launch traced here: 36.7 us
  Pallas kernels  18.6 us (51%)
  starting transfers between devices  17.3 us (47%)
  waiting for transfers between devices  0.44 us (1%)
    pallas_call x18, Pallas kernels, run(): pl.pallas_call(kernel, out_shape=shapes, in_specs=[pl.BlockSpec(memory_sp...  18.6 us
    ppermute x6, starting transfers between devices, exchange(): got = [lax.ppermute(bufs[0], axis, pairs(count, 0))]  8.32 us
    ppermute x4, starting transfers between devices, shards(): got = lax.ppermute(cells, axis, flips(lax.axis_size(axis), bit))  4.94 us
    ppermute x2, starting transfers between devices, exchange(): got.append(lax.ppermute(bufs[1], (axis, beside), perm))  2.87 us
    ppermute x1, starting transfers between devices, exchange(): got.append(lax.ppermute(bufs[1], axis, pairs(count, 1)))  1.13 us
  transfers between devices with their start and end apart: 13, of which 1 were waited for; matrix products, arithmetic and copies ran while one was open for 0% of the time, Pallas kernels for 39%

profile of v8, /device:TPU:1, one launch (start us, length us, event | category | flops | bytes accessed | tf_op | source)
XLA Modules:
  0.0 36.7 jit_solution(7028234677342395754)
XLA Ops:
  0.0 2.1 %pack_faces.1 = (f32[16,64,256]{2,1,0:T(8,128)S(1)}, f32[16,64,256]{2,1,0:T(8,128)S(1)}, f32[16,64,256]{2,1,0:T(8,128)S(1)}, f32[2,64,256]{2,1,0:T(8,128)S(1)}, ...) custom-call(f32[16,64,256]{2,1,0:T(8,128)} %refs_0_.1, ...), custom_call_target="tpu_custom_call" | custom-call | flops 1000 | bytes 3500000 | tf_op jit(solution)/shard_map/pack_faces/pallas_call | solution.py:58
  2.2 2.1 %collective-permute-start = (f32[2,64,256]{2,1,0:T(8,128)S(1)}, f32[2,64,256]{2,1,0:T(8,128)S(1)}, u32[]{:S(2)}, u32[]{:S(2)}) collective-permute-start(f32[2,64,256]{2,1,0:T(8,128)S(1)} %get-tuple-element.54), channel_id=1, source_target_pairs={{0,16},{16,0},{1,17},{17,1},{2,18},{18,2},{3,19},{19,3},{4,20},{20... | collective-permute-start | bytes 393224 | tf_op jit(solution)/shard_map/ppermute | solution.py:1071
  4.3 1.0 %collective-permute-start.3 = (f32[2,64,128]{2,1,0:T(8,128)S(1)}, f32[2,64,128]{2,1,0:T(8,128)S(1)}, u32[]{:S(2)}, u32[]{:S(2)}) collective-permute-start(f32[2,64,128]{2,1,0:T(8,128)S(1)} %get-tuple-element.57.refs_10_), channel_id=1, source_target_pairs={{0,1},{1,0},{2,3},{3,2},{4,5},{5,4},{6,7},{7,6},{8,9},{9,8},{10,11... | collective-permute-start | bytes 196616 | tf_op jit(solution)/shard_map/ppermute | solution.py:1071
  5.2 1.1 %collective-permute-start.4 = (f32[2,64,128]{2,1,0:T(8,128)S(1)}, f32[2,64,128]{2,1,0:T(8,128)S(1)}, u32[]{:S(2)}, u32[]{:S(2)}) collective-permute-start(f32[2,64,128]{2,1,0:T(8,128)S(1)} %get-tuple-element.58.refs_11_), channel_id=1, source_target_pairs={{1,2},{2,1},{3,0},{0,3},{5,6},{6,5},{7,4},{4,7},{9,10},{10,9},{11,... | collective-permute-start | bytes 196616 | tf_op jit(solution)/shard_map/ppermute | solution.py:1074
  6.3 1.3 %collective-permute-start.1 = (f32[2,16,256]{2,1,0:T(8,128)S(1)}, f32[2,16,256]{2,1,0:T(8,128)S(1)}, u32[]{:S(2)}, u32[]{:S(2)}) collective-permute-start(f32[2,16,256]{2,1,0:T(8,128)S(1)} %get-tuple-element.55.refs_6_), channel_id=1, source_target_pairs={{0,4},{4,0},{8,12},{12,8},{1,5},{5,1},{9,13},{13,9},{2,6},{6,2},{1... | collective-permute-start | bytes 98312 | tf_op jit(solution)/shard_map/ppermute | solution.py:1071
  7.6 0.8 %collective-permute-start.2 = (f32[2,16,256]{2,1,0:T(8,128)S(1)}, f32[2,16,256]{2,1,0:T(8,128)S(1)}, u32[]{:S(2)}, u32[]{:S(2)}) collective-permute-start(f32[2,16,256]{2,1,0:T(8,128)S(1)} %get-tuple-element.56.refs_7_), channel_id=1, source_target_pairs={{0,1},{1,0},{2,3},{3,2},{4,8},{5,9},{6,10},{7,11},{8,4},{9,5},{10,... | collective-permute-start | bytes 98312 | tf_op jit(solution)/shard_map/ppermute | solution.py:1077
  8.4 0.9 %local_sums.1 = (f32[5,2,8,256]{3,2,1,0:T(8,128)S(1)}, f32[8,128]{1,0:T(8,128)S(1)}) custom-call(f32[16,64,256]{2,1,0:T(8,128)S(1)} %get-tuple-element.50.p.refs_0_.refs_11_, f32[16,64,256]{2,1,0:T(8,128)S(1)} %get-tuple-element.51.k.refs_1_.refs_0_.refs_5_.refs_15_, f32[16,64,256]{2,1,0:T(8,128)S(1)} %get-tuple-element.52.s.refs_2_.refs_1_.refs_0_), custom_call_target="tpu_custom_call" | custom-call | flops 1000 | bytes 4200000 | tf_op jit(solution)/shard_map/local_sums/pallas_call | solution.py:58
  9.4 0.4 %collective-permute-start.11 = (f32[9,64,256]{2,1,0:T(8,128)S(1)}, f32[9,64,256]{2,1,0:T(8,128)S(1)}, u32[]{:S(2)}, u32[]{:S(2)}) collective-permute-start(f32[9,64,256]{2,1,0:T(8,128)S(1)} %pack_deep.1), channel_id=1, source_target_pairs={{0,16},{16,0},{1,17},{17,1},{2,18},{18,2},{3,19},{19,3},{4,20},{20... | collective-permute-start | bytes 1769480 | tf_op jit(solution)/shard_map/ppermute | solution.py:1071
  9.8 0.7 %restrict.1 = (f32[1,3,8,128]{3,2,1,0:T(8,128)S(1)}, f32[8,128]{1,0:T(8,128)S(1)}) custom-call(f32[16,64,256]{2,1,0:T(8,128)S(1)} %get-tuple-element.50.p.refs_0_.refs_11_, f32[16,64,256]{2,1,0:T(8,128)S(1)} %get-tuple-element.51.k.refs_1_.refs_0_.refs_5_.refs_15_, f32[5,2,8,256]{3,2,1,0:T(8,128)S(1)} %get-tuple-element.53.refs_2_, ...), custom_call_target="tpu_custom_call" | custom-call | flops 1000 | bytes 2100000 | tf_op jit(solution)/shard_map/restrict/pallas_call | solution.py:58
  10.6 2.3 %collective-permute-start.7 = (f32[25,8,256]{2,1,0:T(8,128)S(1)}, f32[25,8,256]{2,1,0:T(8,128)S(1)}, u32[]{:S(2)}, u32[]{:S(2)}) collective-permute-start(f32[25,8,256]{2,1,0:T(8,128)S(1)} %get-tuple-element.61.refs_3_), channel_id=1, source_target_pairs={{0,4},{4,0},{8,12},{12,8},{1,5},{5,1},{9,13},{13,9},{2,6},{6,2},{1... | collective-permute-start | bytes 614408 | tf_op jit(solution)/shard_map/ppermute | solution.py:1071
  12.9 2.1 %collective-permute-start.8 = (f32[25,8,256]{2,1,0:T(8,128)S(1)}, f32[25,8,256]{2,1,0:T(8,128)S(1)}, u32[]{:S(2)}, u32[]{:S(2)}) collective-permute-start(f32[25,8,256]{2,1,0:T(8,128)S(1)} %get-tuple-element.70), channel_id=1, source_target_pairs={{0,1},{1,0},{2,3},{3,2},{4,8},{5,9},{6,10},{7,11},{8,4},{9,5},{10,... | collective-permute-start | bytes 614408 | tf_op jit(solution)/shard_map/ppermute | solution.py:1077
  15.0 0.2 collective-permute-start.5
  15.3 2.6 %weights.1 = (f32[16,64,128]{2,1,0:T(8,128)S(1)}, f32[16,64,128]{2,1,0:T(8,128)S(1)}, f32[16,64,128]{2,1,0:T(8,128)S(1)}, f32[16,64,384]{2,1,0:T(8,128)S(1)}, f3...) custom-call(f32[16,64,256]{2,1,0:T(8,128)S(1)} %get-tuple-element.51.k, ...), custom_call_target="tpu_custom_call" | custom-call | flops 1000 | bytes 14000000 | tf_op jit(solution)/shard_map/weights/pallas_call | solution.py:58
  17.9 0.1 collective-permute-start.6
  18.1 3.0 %extend.1 = (f32[16,8,384]{2,1,0:T(8,128)S(1)}, f32[16,8,384]{2,1,0:T(8,128)S(1)}, f32[16,8,384]{2,1,0:T(8,128)S(1)}, f32[16,8,384]{2,1,0:T(8,128)S(1)}, f32[16,...) custom-call(f32[16,64,256]{2,1,0:T(8,128)S(1)} %get-tuple-element.50, ...), custom_call_target="tpu_custom_call" | custom-call | flops 1000 | bytes 11200000 | tf_op jit(solution)/shard_map/extend/pallas_call | solution.py:58
  21.1 0.4 %collective-permute-done.6.got = f32[1,5,8,128]{3,2,1,0:T(8,128)S(1)} collective-permute-done((f32[1,5,8,128]{3,2,1,0:T(8,128)S(1)}, f32[1,5,8,128]{3,2,1,0:T(8,128)S(1)}, u32[]{:S(2)}, u32[]{:S(2)}) %collective-permute-start.6) | collective-permute-done | bytes 20512 | tf_op jit(solution)/shard_map/ppermute | solution.py:1166
  21.5 1.3 %collective-permute-start.9 = (f32[27,8,128]{2,1,0:T(8,128)S(1)}, f32[27,8,128]{2,1,0:T(8,128)S(1)}, u32[]{:S(2)}, u32[]{:S(2)}) collective-permute-start(f32[27,8,128]{2,1,0:T(8,128)S(1)} %join.1.joined), channel_id=1, source_target_pairs={{0,16},{16,0},{1,17},{17,1},{2,18},{18,2},{3,19},{19,3},{4,20},{20... | collective-permute-start | bytes 331784 | tf_op jit(solution)/shard_map/ppermute | solution.py:1071
  22.8 1.5 %inner_2.1 = (f32[16,72,384]{2,1,0:T(8,128)S(1)}, f32[8,128]{1,0:T(8,128)S(1)}) custom-call(f32[16,64,256]{2,1,0:T(8,128)S(1)} %get-tuple-element.52.s.refs_2_.refs_1_.refs_0_, f32[16,64,128]{2,1,0:T(8,128)S(1)} %get-tuple-element.64.refs_3_.refs_1_, f32[16,8,384]{2,1,0:T(8,128)S(1)} %get-tuple-element.72.refs_2_, ...), custom_call_target="tpu_custom_call" | custom-call | flops 1000 | bytes 7700000 | tf_op jit(solution)/shard_map/inner_2/pallas_call | solution.py:58
  24.3 1.8 %inner_3_4.1 = (f32[16,72,384]{2,1,0:T(8,128)S(1)}, f32[16,64,256]{2,1,0:T(8,128)S(1)}, f32[8,128]{1,0:T(8,128)S(1)}) custom-call(f32[16,64,256]{2,1,0:T(8,128)S(1)} %get-tuple-element.52.s.refs_2_.refs_1_.refs_0_, f32[16,64,128]{2,1,0:T(8,128)S(1)} %get-tuple-element.64.refs_3_.refs_1_, f32[16,8,384]{2,1,0:T(8,128)S(1)} %get-tuple-element.72.refs_2_, ...), custom_call_target="tpu_custom_call" | custom-call | flops 1000 | bytes 7700000 | tf_op jit(solution)/shard_map/inner_3_4/pallas_call | solution.py:58
  26.1 2.5 %collective-permute-start.10 = (f32[4,5,8,128]{3,2,1,0:T(8,128)S(1)}, f32[4,5,8,128]{3,2,1,0:T(8,128)S(1)}, u32[]{:S(2)}, u32[]{:S(2)}) collective-permute-start(f32[4,5,8,128]{3,2,1,0:T(8,128)S(1)} %split.1.cells), channel_id=1, source_target_pairs={{0,4},{4,0},{8,12},{12,8},{1,5},{5,1},{9,13},{13,9},{2,6},{6,2},{1... | collective-permute-start | bytes 245768 | tf_op jit(solution)/shard_map/ppermute | solution.py:1230
  28.6 2.2 %halo_sweeps.1 = (f32[16,72,384]{2,1,0:T(8,128)S(1)}, f32[8,72,384]{2,1,0:T(8,128)S(1)}, f32[16,72,384]{2,1,0:T(8,128)S(1)}, f32[16,72,384]{2,1,0:T(8,128)S(1)},...) custom-call(f32[16,64,256]{2,1,0:T(8,128)S(1)} %get-tuple-element.52.s.refs_2_.refs_1_.refs_0_, ...), custom_call_target="tpu_custom_call" | custom-call | flops 1000 | bytes 10500000 | tf_op jit(solution)/shard_map/halo_sweeps/pallas_call | solution.py:58
  30.9 2.1 %collective-permute-start.12 = (f32[8,5,8,128]{3,2,1,0:T(8,128)S(1)}, f32[8,5,8,128]{3,2,1,0:T(8,128)S(1)}, u32[]{:S(2)}, u32[]{:S(2)}) collective-permute-start(f32[8,5,8,128]{3,2,1,0:T(8,128)S(1)} %merge.2.cells), channel_id=1, source_target_pairs={{0,1},{1,0},{2,3},{3,2},{4,5},{5,4},{6,7},{7,6},{8,9},{9,8},{10,11... | collective-permute-start | bytes 491528 | tf_op jit(solution)/shard_map/ppermute | solution.py:1230
  33.0 1.5 %last_sweeps.1 = (f32[8,64,256]{2,1,0:T(8,128)S(1)}, f32[8,128]{1,0:T(8,128)S(1)}) custom-call(f32[16,64,256]{2,1,0:T(8,128)S(1)} %get-tuple-element.52.s.refs_2_.refs_1_.refs_0_, f32[16,64,128]{2,1,0:T(8,128)S(1)} %get-tuple-element.64.refs_3_.refs_1_, f32[16,8,384]{2,1,0:T(8,128)S(1)} %get-tuple-element.72.refs_2_, ...), custom_call_target="tpu_custom_call" | custom-call | flops 1000 | bytes 5600000 | tf_op jit(solution)/shard_map/last_sweeps/pallas_call | solution.py:58
  34.5 2.0 %solve.1 = f32[16,64,256]{2,1,0:T(8,128)} custom-call(f32[16,5,8,128]{3,2,1,0:T(8,128)S(1)} %merge.3.gathered, f32[16,64,256]{2,1,0:T(8,128)S(1)} %get-tuple-element.93.fine, f32[8,64,256]{2,1,0:T(8,128)S(1)} %get-tuple-element.94.edges), custom_call_target="tpu_custom_call" | custom-call | flops 1000 | bytes 7700000 | tf_op jit(solution)/shard_map/solve/pallas_call | solution.py:58
  (20 shorter events, 0.2 us)
Async XLA Ops:
  2.2 7.2 %collective-permute-start = (f32[2,64,256]{2,1,0:T(8,128)S(1)}, f32[2,64,256]{2,1,0:T(8,128)S(1)}, u32[]{:S(2)}, u32[]{:S(2)}) collective-permute-start(f32[2,64,256]{2,1,0:T(8,128)S(1)} %get-tuple-element.54), channel_id=1, source_target_pairs={{0,16},{16,0},{1,17},{17,1},{2,18},{18,2},{3,19},{19,3},{4,20},{20... | collective-permute-start | bytes 393224 | tf_op jit(solution)/shard_map/ppermute | solution.py:1071
  4.3 5.1 %collective-permute-start.3 = (f32[2,64,128]{2,1,0:T(8,128)S(1)}, f32[2,64,128]{2,1,0:T(8,128)S(1)}, u32[]{:S(2)}, u32[]{:S(2)}) collective-permute-start(f32[2,64,128]{2,1,0:T(8,128)S(1)} %get-tuple-element.57.refs_10_), channel_id=1, source_target_pairs={{0,1},{1,0},{2,3},{3,2},{4,5},{5,4},{6,7},{7,6},{8,9},{9,8},{10,11... | collective-permute-start | bytes 196616 | tf_op jit(solution)/shard_map/ppermute | solution.py:1071
  5.2 4.1 %collective-permute-start.4 = (f32[2,64,128]{2,1,0:T(8,128)S(1)}, f32[2,64,128]{2,1,0:T(8,128)S(1)}, u32[]{:S(2)}, u32[]{:S(2)}) collective-permute-start(f32[2,64,128]{2,1,0:T(8,128)S(1)} %get-tuple-element.58.refs_11_), channel_id=1, source_target_pairs={{1,2},{2,1},{3,0},{0,3},{5,6},{6,5},{7,4},{4,7},{9,10},{10,9},{11,... | collective-permute-start | bytes 196616 | tf_op jit(solution)/shard_map/ppermute | solution.py:1074
  6.3 3.0 %collective-permute-start.1 = (f32[2,16,256]{2,1,0:T(8,128)S(1)}, f32[2,16,256]{2,1,0:T(8,128)S(1)}, u32[]{:S(2)}, u32[]{:S(2)}) collective-permute-start(f32[2,16,256]{2,1,0:T(8,128)S(1)} %get-tuple-element.55.refs_6_), channel_id=1, source_target_pairs={{0,4},{4,0},{8,12},{12,8},{1,5},{5,1},{9,13},{13,9},{2,6},{6,2},{1... | collective-permute-start | bytes 98312 | tf_op jit(solution)/shard_map/ppermute | solution.py:1071
  7.6 1.7 %collective-permute-start.2 = (f32[2,16,256]{2,1,0:T(8,128)S(1)}, f32[2,16,256]{2,1,0:T(8,128)S(1)}, u32[]{:S(2)}, u32[]{:S(2)}) collective-permute-start(f32[2,16,256]{2,1,0:T(8,128)S(1)} %get-tuple-element.56.refs_7_), channel_id=1, source_target_pairs={{0,1},{1,0},{2,3},{3,2},{4,8},{5,9},{6,10},{7,11},{8,4},{9,5},{10,... | collective-permute-start | bytes 98312 | tf_op jit(solution)/shard_map/ppermute | solution.py:1077
  9.4 19.2 %collective-permute-start.11 = (f32[9,64,256]{2,1,0:T(8,128)S(1)}, f32[9,64,256]{2,1,0:T(8,128)S(1)}, u32[]{:S(2)}, u32[]{:S(2)}) collective-permute-start(f32[9,64,256]{2,1,0:T(8,128)S(1)} %pack_deep.1), channel_id=1, source_target_pairs={{0,16},{16,0},{1,17},{17,1},{2,18},{18,2},{3,19},{19,3},{4,20},{20... | collective-permute-start | bytes 1769480 | tf_op jit(solution)/shard_map/ppermute | solution.py:1071
  10.6 7.4 %collective-permute-start.7 = (f32[25,8,256]{2,1,0:T(8,128)S(1)}, f32[25,8,256]{2,1,0:T(8,128)S(1)}, u32[]{:S(2)}, u32[]{:S(2)}) collective-permute-start(f32[25,8,256]{2,1,0:T(8,128)S(1)} %get-tuple-element.61.refs_3_), channel_id=1, source_target_pairs={{0,4},{4,0},{8,12},{12,8},{1,5},{5,1},{9,13},{13,9},{2,6},{6,2},{1... | collective-permute-start | bytes 614408 | tf_op jit(solution)/shard_map/ppermute | solution.py:1071
  12.9 5.1 %collective-permute-start.8 = (f32[25,8,256]{2,1,0:T(8,128)S(1)}, f32[25,8,256]{2,1,0:T(8,128)S(1)}, u32[]{:S(2)}, u32[]{:S(2)}) collective-permute-start(f32[25,8,256]{2,1,0:T(8,128)S(1)} %get-tuple-element.70), channel_id=1, source_target_pairs={{0,1},{1,0},{2,3},{3,2},{4,8},{5,9},{6,10},{7,11},{8,4},{9,5},{10,... | collective-permute-start | bytes 614408 | tf_op jit(solution)/shard_map/ppermute | solution.py:1077
  15.0 2.9 %collective-permute-start.5 = (f32[1,3,8,128]{3,2,1,0:T(8,128)S(1)}, f32[1,3,8,128]{3,2,1,0:T(8,128)S(1)}, u32[]{:S(2)}, u32[]{:S(2)}) collective-permute-start(f32[1,3,8,128]{3,2,1,0:T(8,128)S(1)} %get-tuple-element.59.cells), channel_id=1, source_target_pairs={{0,2},{1,3},{2,0},{3,1},{4,6},{5,7},{6,4},{7,5},{8,10},{9,11},{10,... | collective-permute-start | bytes 36872 | tf_op jit(solution)/shard_map/ppermute | solution.py:1166
  17.9 3.6 %collective-permute-start.6 = (f32[1,5,8,128]{3,2,1,0:T(8,128)S(1)}, f32[1,5,8,128]{3,2,1,0:T(8,128)S(1)}, u32[]{:S(2)}, u32[]{:S(2)}) collective-permute-start(f32[1,5,8,128]{3,2,1,0:T(8,128)S(1)} %pair.1.cells), channel_id=1, source_target_pairs={{0,8},{4,12},{8,0},{12,4},{1,9},{5,13},{9,1},{13,5},{2,10},{6,14},... | collective-permute-start | bytes 61448 | tf_op jit(solution)/shard_map/ppermute | solution.py:1166
  21.5 4.6 %collective-permute-start.9 = (f32[27,8,128]{2,1,0:T(8,128)S(1)}, f32[27,8,128]{2,1,0:T(8,128)S(1)}, u32[]{:S(2)}, u32[]{:S(2)}) collective-permute-start(f32[27,8,128]{2,1,0:T(8,128)S(1)} %join.1.joined), channel_id=1, source_target_pairs={{0,16},{16,0},{1,17},{17,1},{2,18},{18,2},{3,19},{19,3},{4,20},{20... | collective-permute-start | bytes 331784 | tf_op jit(solution)/shard_map/ppermute | solution.py:1071
  26.1 4.8 %collective-permute-start.10 = (f32[4,5,8,128]{3,2,1,0:T(8,128)S(1)}, f32[4,5,8,128]{3,2,1,0:T(8,128)S(1)}, u32[]{:S(2)}, u32[]{:S(2)}) collective-permute-start(f32[4,5,8,128]{3,2,1,0:T(8,128)S(1)} %split.1.cells), channel_id=1, source_target_pairs={{0,4},{4,0},{8,12},{12,8},{1,5},{5,1},{9,13},{13,9},{2,6},{6,2},{1... | collective-permute-start | bytes 245768 | tf_op jit(solution)/shard_map/ppermute | solution.py:1230
  30.9 3.6 %collective-permute-start.12 = (f32[8,5,8,128]{3,2,1,0:T(8,128)S(1)}, f32[8,5,8,128]{3,2,1,0:T(8,128)S(1)}, u32[]{:S(2)}, u32[]{:S(2)}) collective-permute-start(f32[8,5,8,128]{3,2,1,0:T(8,128)S(1)} %merge.2.cells), channel_id=1, source_target_pairs={{0,1},{1,0},{2,3},{3,2},{4,5},{5,4},{6,7},{7,6},{8,9},{9,8},{10,11... | collective-permute-start | bytes 491528 | tf_op jit(solution)/shard_map/ppermute | solution.py:1230
